TPU v7x, 32 devices: a whole 2x2x4 slice. The times are simulated.
32 devices in a mesh: expert: 16 (over z, y, x), fsdp: 2 (over core).
Axes of the slice: x: 2, y: 2, z: 4, core: 2. Of those that a mesh axis runs over, the one named last changes fastest.
Arguments:
- hidden_in: bfloat16 [2, 2048, 2560], P('fsdp', 'expert'), may hold values from -6 to 6
- gain_attn: bfloat16 [2560], P('fsdp'), may hold values from 0.5 to 1.5
- query_weight: bfloat16 [2560, 2560], P('fsdp'), may hold values from -0.125 to 0.125
- key_matrix: bfloat16 [2560, 512], P('fsdp'), may hold values from -0.125 to 0.125
- value_matrix: bfloat16 [2560, 512], P('fsdp'), may hold values from -0.125 to 0.125
- out_weight: bfloat16 [2560, 2560], P('fsdp'), may hold values from -0.5 to 0.5
- gain_ffn: bfloat16 [2560], P('fsdp'), may hold values from 0.5 to 1.5
- router_weight: bfloat16 [2560, 16], P('fsdp'), may hold values from -0.0625 to 0.0625
- shared_gate: bfloat16 [2560, 3072], P('fsdp'), may hold values from -0.125 to 0.125
- shared_up: bfloat16 [2560, 3072], P('fsdp'), may hold values from -0.125 to 0.125
- shared_down: bfloat16 [3072, 2560], P('fsdp'), may hold values from -0.109375 to 0.109375
- expert_gate: bfloat16 [16, 2560, 1536], P('expert', 'fsdp'), may hold values from -0.125 to 0.125
- expert_up: bfloat16 [16, 2560, 1536], P('expert', 'fsdp'), may hold values from -0.125 to 0.125
- expert_down: bfloat16 [16, 1536, 2560], P('expert', 'fsdp'), may hold values from -0.15625 to 0.15625
- routes: int32 [2, 2048, 6], P('fsdp', 'expert'), may hold values from 0 to 15, all different within a row; in each aligned block of 128 rows (0 to 127, 128 to 255, ..., all dimensions but the last counted through in order) at most 64 rows name the same one
- segments: int32 [2, 2048], P('fsdp'), may hold values from 0 to 2, as said below
- positions: int32 [2, 2048], P('fsdp', 'expert'), may hold values from 0 to 4094, as said below
- grad_out: bfloat16 [2, 2048, 2560], P('fsdp', 'expert'), may hold values from -6 to 6
Outputs:
- output: bfloat16 [2, 2048, 2560], P('fsdp', 'expert')
- grad_in: bfloat16 [2, 2048, 2560], P('fsdp', 'expert')
- grad_gain_attn: float32 [2560], P('fsdp')
- grad_query: float32 [2560, 2560], P('fsdp')
- grad_key: float32 [2560, 512], P('fsdp')
- grad_value: float32 [2560, 512], P('fsdp')
- grad_out_weight: float32 [2560, 2560], P('fsdp')
- grad_gain_ffn: float32 [2560], P('fsdp')
- grad_router: float32 [2560, 16], P('fsdp')
- grad_shared_gate: float32 [2560, 3072], P('fsdp')
- grad_shared_up: float32 [2560, 3072], P('fsdp')
- grad_shared_down: float32 [3072, 2560], P('fsdp')
- grad_expert_gate: float32 [16, 2560, 1536], P('expert', 'fsdp')
- grad_expert_up: float32 [16, 2560, 1536], P('expert', 'fsdp')
- grad_expert_down: float32 [16, 1536, 2560], P('expert', 'fsdp')
Inputs may be any that keep to these rules, and one draw needn't show every extreme that they name: `routes`: the 6 experts of a token differ. Among the 128 tokens of one device (aligned blocks of rows in sequence order) no expert is named more than 64 times, a bound that some block reaches in each draw. `segments`: document numbers never fall along a sequence; every sequence holds documents 0, 1 and 2; documents 0 and 2 each hold between 204 and 2 * (204) tokens, document 1 the rest. Within a document positions rise by one from token to token; document 0 of each sequence starts at position 0; the last token of each sequence has the largest position.
All inputs are finite; a program needn't handle non-finite values.
Results may differ from a plain program's by a relative error of at most 0.023.
Values may be sent and summed in bfloat16 or wider, within the bound.
A program may use at most 640 MiB of HBM per device.

v0:
```python
import jax
import jax.numpy as jnp
from jax import lax
from jax.sharding import PartitionSpec as P

QUERY_HEADS = 20
KEY_HEADS = 4
HEAD_DIM = 128
FE = 1536


epsilon = 1e-05
rope_base = 500000.0
masked_score = -1e30
highest = lax.Precision.HIGHEST


def matrix_multiply(left, right):
    return jnp.dot(left, right, preferred_element_type=jnp.float32)


def matrix_multiply_transposed(left, right):
    return lax.dot_general(
        left, right, (((1,), (1,)), ((), ())), preferred_element_type=jnp.float32
    )


def matmul_tn(left, right):
    return lax.dot_general(
        left, right, (((0,), (0,)), ((), ())), preferred_element_type=jnp.float32
    )


def matmul_tn_exact(left, right):
    return lax.dot_general(
        left, right, (((0,), (0,)), ((), ())), preferred_element_type=jnp.float32, precision=highest
    )


def rms_scale(vector, gain):
    factor = lax.rsqrt(jnp.mean(vector * vector, axis=-1, keepdims=True) + epsilon)
    return vector * factor * gain


def apply_rotation(heads, cosine_table, sine_table):
    halfway = heads.shape[-1] // 2
    front_part = heads[..., :halfway]
    back_part = heads[..., halfway:]
    return jnp.concatenate(
        [
            front_part * cosine_table - back_part * sine_table,
            back_part * cosine_table + front_part * sine_table,
        ],
        axis=-1,
    )


def rope_tables(positions):
    frequency = 1.0 / rope_base ** (jnp.arange(0, HEAD_DIM, 2, dtype=jnp.float32) / HEAD_DIM)
    turned = positions.astype(jnp.float32)[:, None] * frequency[None, :]
    return (jnp.cos(turned)[:, None, :], jnp.sin(turned)[:, None, :])


def swiglu(gate_in, up_in):
    return jax.nn.silu(gate_in) * up_in


def gate_values(logits, chosen_ids):
    router_probs = jax.nn.softmax(logits, axis=-1)
    chosen = jnp.take_along_axis(router_probs, chosen_ids, axis=1)
    return chosen / jnp.sum(chosen, axis=1, keepdims=True)


def local(
    hidden_in,
    gain_attn,
    query_weight,
    key_matrix,
    value_matrix,
    out_weight,
    gain_ffn,
    router_weight,
    shared_gate,
    shared_up,
    shared_down,
    expert_gate,
    expert_up,
    expert_down,
    routes,
    segments,
    positions,
    grad_out,
):
    token_rows = hidden_in.shape[1]
    model_width = hidden_in.shape[2]
    experts = lax.axis_size("expert")
    topk_count = routes.shape[2]
    capacity = min(token_rows, 4 * token_rows * topk_count // (3 * experts))
    length_total = token_rows * experts
    group_width = QUERY_HEADS // KEY_HEADS
    score_scale = HEAD_DIM ** (-0.5)
    position = lax.axis_index("expert")
    x_rows = hidden_in[0].astype(jnp.float32)
    labels = segments[0]
    cosine_table, sine_table = rope_tables(positions[0])
    gain_one, w_query, key_projection_weight, w_value, output_weight, gain_two, w_router = (
        lax.all_gather(gain_attn, "fsdp", axis=0, tiled=True),
        lax.all_gather(query_weight, "fsdp", axis=0, tiled=True),
        lax.all_gather(key_matrix, "fsdp", axis=0, tiled=True),
        lax.all_gather(value_matrix, "fsdp", axis=0, tiled=True),
        lax.all_gather(out_weight, "fsdp", axis=0, tiled=True),
        lax.all_gather(gain_ffn, "fsdp", axis=0, tiled=True),
        lax.all_gather(router_weight, "fsdp", axis=0, tiled=True),
    )
    gain_first = gain_one.astype(jnp.float32)
    first_normed = rms_scale(x_rows, gain_first).astype(jnp.bfloat16)
    query_pre = matrix_multiply(first_normed, w_query).reshape(token_rows, QUERY_HEADS, HEAD_DIM)
    key_unrotated = matrix_multiply(first_normed, key_projection_weight).reshape(
        token_rows, KEY_HEADS, HEAD_DIM
    )
    query_reduced = apply_rotation(query_pre, cosine_table, sine_table).astype(jnp.bfloat16)
    key_reduced = (
        apply_rotation(key_unrotated, cosine_table, sine_table)
        .astype(jnp.bfloat16)
        .reshape(token_rows, KEY_HEADS * HEAD_DIM)
    )
    value_low = matrix_multiply(first_normed, w_value).astype(jnp.bfloat16)
    every_key, every_value = (
        lax.all_gather(key_reduced, "expert", axis=0, tiled=True),
        lax.all_gather(value_low, "expert", axis=0, tiled=True),
    )
    key_head_rows = every_key.reshape(length_total, KEY_HEADS, HEAD_DIM)
    value_head_rows = every_value.reshape(length_total, KEY_HEADS, HEAD_DIM)
    query_head_rows = query_reduced.reshape(token_rows, KEY_HEADS, group_width, HEAD_DIM)
    query_index = position * token_rows + jnp.arange(token_rows, dtype=jnp.int32)
    query_labels = lax.dynamic_slice_in_dim(labels, position * token_rows, token_rows)
    allowed = (query_labels[:, None] == labels[None, :]) & (
        jnp.arange(length_total, dtype=jnp.int32)[None, :] <= query_index[:, None]
    )

    def masked_scores():
        raw_scores = (
            jnp.einsum(
                "qgjd,kgd->gjqk", query_head_rows, key_head_rows, preferred_element_type=jnp.float32
            )
            * score_scale
        )
        return jnp.where(allowed[None, None], raw_scores, masked_score)

    scores = masked_scores()
    maxima = jnp.max(scores, axis=-1, keepdims=True)
    shifted = jnp.exp(scores - maxima)
    totals = jnp.sum(shifted, axis=-1, keepdims=True)
    log_total = maxima + jnp.log(totals)
    weights_low = (shifted / totals).astype(jnp.bfloat16)
    attended = jnp.einsum(
        "gjqk,kgd->qgjd", weights_low, value_head_rows, preferred_element_type=jnp.float32
    )
    attended_low = attended.reshape(token_rows, QUERY_HEADS * HEAD_DIM).astype(jnp.bfloat16)
    residual_one = x_rows + matrix_multiply(attended_low, output_weight)
    gain_second = gain_two.astype(jnp.float32)
    normed_two = rms_scale(residual_one, gain_second).astype(jnp.bfloat16)
    router_float = w_router.astype(jnp.float32)
    normed_float = normed_two.astype(jnp.float32)
    logits = jnp.dot(
        normed_float, router_float, precision=highest, preferred_element_type=jnp.float32
    )
    chosen_ids = routes[0]
    gate_weight, gate_pull = jax.vjp(lambda scores_in: gate_values(scores_in, chosen_ids), logits)
    gate_full, up_full, down_full = (
        lax.all_gather(shared_gate, "fsdp", axis=0, tiled=True),
        lax.all_gather(shared_up, "fsdp", axis=0, tiled=True),
        lax.all_gather(shared_down, "fsdp", axis=0, tiled=True),
    )
    shared_pre_gate = matrix_multiply(normed_two, gate_full)
    shared_pre_up = matrix_multiply(normed_two, up_full)
    shared_act, shared_pull = jax.vjp(swiglu, shared_pre_gate, shared_pre_up)
    shared_low = shared_act.astype(jnp.bfloat16)
    shared_out = matrix_multiply(shared_low, down_full)
    expert_gate_whole, expert_up_whole, expert_down_whole = (
        lax.all_gather(expert_gate, "fsdp", axis=1, tiled=True),
        lax.all_gather(expert_up, "fsdp", axis=1, tiled=True),
        lax.all_gather(expert_down, "fsdp", axis=1, tiled=True),
    )
    expert_w_gate = expert_gate_whole[0]
    expert_up_weight = expert_up_whole[0]
    expert_w_down = expert_down_whole[0]
    flat_ids = chosen_ids.reshape(token_rows * topk_count)
    onehot = (flat_ids[:, None] == jnp.arange(experts, dtype=jnp.int32)[None, :]).astype(jnp.int32)
    earlier = jnp.cumsum(onehot, axis=0) - onehot
    rank_in = jnp.sum(earlier * onehot, axis=1)
    slot_of = flat_ids * capacity + rank_in
    pair_token = jnp.arange(token_rows * topk_count, dtype=jnp.int32) // topk_count
    outgoing = (
        jnp.zeros((experts * capacity, model_width), jnp.bfloat16)
        .at[slot_of]
        .set(normed_two[pair_token])
        .reshape(experts, capacity, model_width)
    )
    received = lax.all_to_all(outgoing, "expert", split_axis=0, concat_axis=0, tiled=True)
    item_count = received.shape[1]
    flat_in = received.reshape(-1, model_width)
    pre_gate = matrix_multiply(flat_in, expert_w_gate)
    pre_up = matrix_multiply(flat_in, expert_up_weight)
    produced = matrix_multiply(swiglu(pre_gate, pre_up).astype(jnp.bfloat16), expert_w_down).astype(
        jnp.bfloat16
    )
    returned_rows = lax.all_to_all(
        produced.reshape(experts, item_count, model_width),
        "expert",
        split_axis=0,
        concat_axis=0,
        tiled=True,
    )
    kept_gate = pre_gate.reshape(experts, item_count, FE)
    kept_up = pre_up.reshape(experts, item_count, FE)
    pair_out = (
        returned_rows.reshape(experts * capacity, model_width)[slot_of]
        .astype(jnp.float32)
        .reshape(token_rows, topk_count, model_width)
    )
    expert_sum = jnp.sum(gate_weight[:, :, None] * pair_out, axis=1)
    output = residual_one + shared_out + expert_sum
    upstream = grad_out[0].astype(jnp.float32)
    upstream_low = grad_out[0]
    d_shared_act = matrix_multiply_transposed(upstream_low, down_full)
    d_shared_gate, d_shared_up = shared_pull(d_shared_act)
    d_shared_gate_low = d_shared_gate.astype(jnp.bfloat16)
    d_shared_up_low = d_shared_up.astype(jnp.bfloat16)
    d_normed_two = matrix_multiply_transposed(
        d_shared_gate_low, gate_full
    ) + matrix_multiply_transposed(d_shared_up_low, up_full)
    d_gate = jnp.sum(upstream[:, None, :] * pair_out, axis=-1)
    d_pair = (
        (gate_weight[:, :, None] * upstream[:, None, :])
        .astype(jnp.bfloat16)
        .reshape(token_rows * topk_count, model_width)
    )
    d_outgoing = (
        jnp.zeros((experts * capacity, model_width), jnp.bfloat16)
        .at[slot_of]
        .set(d_pair)
        .reshape(experts, capacity, model_width)
    )
    d_received = lax.all_to_all(d_outgoing, "expert", split_axis=0, concat_axis=0, tiled=True)
    d_block = d_received.reshape(-1, model_width)
    rows_in = received.reshape(-1, model_width)
    expert_act, expert_pull = jax.vjp(swiglu, kept_gate.reshape(-1, FE), kept_up.reshape(-1, FE))
    expert_act_low = expert_act.astype(jnp.bfloat16)
    d_expert_act = matrix_multiply_transposed(d_block, expert_w_down)
    d_expert_gate, d_expert_up = expert_pull(d_expert_act)
    d_expert_gate_low = d_expert_gate.astype(jnp.bfloat16)
    d_expert_up_low = d_expert_up.astype(jnp.bfloat16)
    term_expert_down = matmul_tn(expert_act_low, d_block)
    term_expert_gate = matmul_tn(rows_in, d_expert_gate_low)
    term_expert_up = matmul_tn(rows_in, d_expert_up_low)
    d_rows_out = (
        matrix_multiply_transposed(d_expert_gate_low, expert_w_gate)
        + matrix_multiply_transposed(d_expert_up_low, expert_up_weight)
    ).astype(jnp.bfloat16)
    d_returned = lax.all_to_all(
        d_rows_out.reshape(experts, -1, model_width),
        "expert",
        split_axis=0,
        concat_axis=0,
        tiled=True,
    )
    d_dispatch = (
        d_returned.reshape(experts * capacity, model_width)[slot_of]
        .astype(jnp.float32)
        .reshape(token_rows, topk_count, model_width)
    )
    d_normed_two = d_normed_two + jnp.sum(d_dispatch, axis=1)
    (d_logits,) = gate_pull(d_gate)
    d_normed_two = d_normed_two + lax.dot_general(
        d_logits,
        router_float,
        (((1,), (1,)), ((), ())),
        precision=highest,
        preferred_element_type=jnp.float32,
    )
    norm_two_out, norm_two_pull = jax.vjp(rms_scale, residual_one, gain_second)
    d_residual_norm, d_gain_two = norm_two_pull(d_normed_two)
    d_residual = upstream + d_residual_norm
    grad_attention_output = d_residual.astype(jnp.bfloat16)
    d_attended = (
        matrix_multiply_transposed(grad_attention_output, output_weight)
        .astype(jnp.bfloat16)
        .reshape(token_rows, KEY_HEADS, group_width, HEAD_DIM)
    )
    scores_again = masked_scores()
    probs_again = jnp.exp(scores_again - log_total)
    probs_low = probs_again.astype(jnp.bfloat16)
    d_probs = jnp.einsum(
        "qgjd,kgd->gjqk", d_attended, value_head_rows, preferred_element_type=jnp.float32
    )
    row_dot = jnp.sum(probs_again * d_probs, axis=-1, keepdims=True)
    d_scores = (probs_again * (d_probs - row_dot)).astype(jnp.bfloat16)
    d_query_turned = (
        jnp.einsum(
            "gjqk,kgd->qgjd", d_scores, key_head_rows, preferred_element_type=jnp.float32
        ).reshape(token_rows, QUERY_HEADS, HEAD_DIM)
        * score_scale
    )
    term_keys = (
        jnp.einsum(
            "gjqk,qgjd->kgd", d_scores, query_head_rows, preferred_element_type=jnp.float32
        ).reshape(length_total, KEY_HEADS * HEAD_DIM)
        * score_scale
    )
    term_values = jnp.einsum(
        "gjqk,qgjd->kgd", probs_low, d_attended, preferred_element_type=jnp.float32
    ).reshape(length_total, KEY_HEADS * HEAD_DIM)
    grad_key_rotated, d_value = (
        lax.psum_scatter(
            term_keys.astype(jnp.bfloat16), "expert", scatter_dimension=0, tiled=True
        ).astype(jnp.float32),
        lax.psum_scatter(
            term_values.astype(jnp.bfloat16), "expert", scatter_dimension=0, tiled=True
        ).astype(jnp.float32),
    )
    query_turn, query_back = jax.vjp(
        lambda heads: apply_rotation(heads, cosine_table, sine_table), query_pre
    )
    key_turn, key_restored = jax.vjp(
        lambda heads: apply_rotation(heads, cosine_table, sine_table), key_unrotated
    )
    d_query_low = (
        query_back(d_query_turned)[0]
        .reshape(token_rows, QUERY_HEADS * HEAD_DIM)
        .astype(jnp.bfloat16)
    )
    d_key_low = (
        key_restored(grad_key_rotated.reshape(token_rows, KEY_HEADS, HEAD_DIM))[0]
        .reshape(token_rows, KEY_HEADS * HEAD_DIM)
        .astype(jnp.bfloat16)
    )
    d_value_low = d_value.astype(jnp.bfloat16)
    d_normed_one = (
        matrix_multiply_transposed(d_query_low, w_query)
        + matrix_multiply_transposed(d_key_low, key_projection_weight)
        + matrix_multiply_transposed(d_value_low, w_value)
    )
    norm_one_out, norm_one_pull = jax.vjp(rms_scale, x_rows, gain_first)
    d_rows_norm, d_gain_one = norm_one_pull(d_normed_one)
    grad_in = (d_residual + d_rows_norm).astype(jnp.bfloat16)
    shares = (
        lax.psum_scatter(
            d_gain_one.astype(jnp.bfloat16), "fsdp", scatter_dimension=0, tiled=True
        ).astype(jnp.float32),
        lax.psum_scatter(
            matmul_tn(first_normed, d_query_low).astype(jnp.bfloat16),
            "fsdp",
            scatter_dimension=0,
            tiled=True,
        ).astype(jnp.float32),
        lax.psum_scatter(
            matmul_tn(first_normed, d_key_low).astype(jnp.bfloat16),
            "fsdp",
            scatter_dimension=0,
            tiled=True,
        ).astype(jnp.float32),
        lax.psum_scatter(
            matmul_tn(first_normed, d_value_low).astype(jnp.bfloat16),
            "fsdp",
            scatter_dimension=0,
            tiled=True,
        ).astype(jnp.float32),
        lax.psum_scatter(
            matmul_tn(attended_low, grad_attention_output).astype(jnp.bfloat16),
            "fsdp",
            scatter_dimension=0,
            tiled=True,
        ).astype(jnp.float32),
        lax.psum_scatter(
            d_gain_two.astype(jnp.bfloat16), "fsdp", scatter_dimension=0, tiled=True
        ).astype(jnp.float32),
        lax.psum_scatter(
            matmul_tn_exact(normed_float, d_logits).astype(jnp.bfloat16),
            "fsdp",
            scatter_dimension=0,
            tiled=True,
        ).astype(jnp.float32),
        lax.psum_scatter(
            matmul_tn(normed_two, d_shared_gate_low).astype(jnp.bfloat16),
            "fsdp",
            scatter_dimension=0,
            tiled=True,
        ).astype(jnp.float32),
        lax.psum_scatter(
            matmul_tn(normed_two, d_shared_up_low).astype(jnp.bfloat16),
            "fsdp",
            scatter_dimension=0,
            tiled=True,
        ).astype(jnp.float32),
        lax.psum_scatter(
            matmul_tn(shared_low, upstream_low).astype(jnp.bfloat16),
            "fsdp",
            scatter_dimension=0,
            tiled=True,
        ).astype(jnp.float32),
    )
    part_g1, part_q, part_k, part_v, part_o, part_g2, part_r, part_sg, part_su, part_sd = shares
    grad_g1, grad_q, grad_k, grad_v, grad_o, grad_g2, grad_r, grad_sg, grad_su, grad_sd = (
        lax.psum(part_g1.astype(jnp.bfloat16), "expert").astype(jnp.float32),
        lax.psum(part_q.astype(jnp.bfloat16), "expert").astype(jnp.float32),
        lax.psum(part_k.astype(jnp.bfloat16), "expert").astype(jnp.float32),
        lax.psum(part_v.astype(jnp.bfloat16), "expert").astype(jnp.float32),
        lax.psum(part_o.astype(jnp.bfloat16), "expert").astype(jnp.float32),
        lax.psum(part_g2.astype(jnp.bfloat16), "expert").astype(jnp.float32),
        lax.psum(part_r.astype(jnp.bfloat16), "expert").astype(jnp.float32),
        lax.psum(part_sg.astype(jnp.bfloat16), "expert").astype(jnp.float32),
        lax.psum(part_su.astype(jnp.bfloat16), "expert").astype(jnp.float32),
        lax.psum(part_sd.astype(jnp.bfloat16), "expert").astype(jnp.float32),
    )
    grad_eg, grad_eu, grad_ed = (
        lax.psum_scatter(
            term_expert_gate.astype(jnp.bfloat16), "fsdp", scatter_dimension=0, tiled=True
        ).astype(jnp.float32),
        lax.psum_scatter(
            term_expert_up.astype(jnp.bfloat16), "fsdp", scatter_dimension=0, tiled=True
        ).astype(jnp.float32),
        lax.psum_scatter(
            term_expert_down.astype(jnp.bfloat16), "fsdp", scatter_dimension=0, tiled=True
        ).astype(jnp.float32),
    )
    return (
        output.astype(jnp.bfloat16)[None],
        grad_in[None],
        grad_g1,
        grad_q,
        grad_k,
        grad_v,
        grad_o,
        grad_g2,
        grad_r,
        grad_sg,
        grad_su,
        grad_sd,
        grad_eg[None],
        grad_eu[None],
        grad_ed[None],
    )


def solution(mesh):
    placed = (
        P("fsdp", "expert", None),
        P("fsdp"),
        P("fsdp", None),
        P("fsdp", None),
        P("fsdp", None),
        P("fsdp", None),
        P("fsdp"),
        P("fsdp", None),
        P("fsdp", None),
        P("fsdp", None),
        P("fsdp", None),
        P("expert", "fsdp", None),
        P("expert", "fsdp", None),
        P("expert", "fsdp", None),
        P("fsdp", "expert", None),
        P("fsdp", None),
        P("fsdp", "expert"),
        P("fsdp", "expert", None),
    )
    return jax.shard_map(
        local,
        mesh=mesh,
        in_specs=placed,
        out_specs=(
            P("fsdp", "expert", None),
            P("fsdp", "expert", None),
            P("fsdp"),
            P("fsdp", None),
            P("fsdp", None),
            P("fsdp", None),
            P("fsdp", None),
            P("fsdp"),
            P("fsdp", None),
            P("fsdp", None),
            P("fsdp", None),
            P("fsdp", None),
            P("expert", "fsdp", None),
            P("expert", "fsdp", None),
            P("expert", "fsdp", None),
        ),
        check_vma=False,
    )
```

profile of v0, /device:TPU:0, one launch (start us, length us, event | category | flops | bytes accessed | tf_op | source)
XLA Modules:
  0.0 2357.6 jit_solution(2343145038775698932)
XLA Ops:
  73.8 29.2 %all-gather.17.cloned.1.call-done = bf16[2048,512]{1,0:T(8,128)(2,1)} async-done(((bf16[128,512]{1,0:T(8,128)(2,1)}), bf16[2048,512]{1,0:T(8,128)(2,1)}) %all-gather.17.cloned.1.call-update) | async-done | bytes 2097168 | tf_op jit(solution)/shard_map/all_gather | solution.py:130
  107.0 21.6 all-gather.23.cloned.1.call-done
  128.5 17.6 copy.70
  154.6 41.6 %all-gather.21.cloned.1.call-done = bf16[2048,512]{0,1:T(8,128)(2,1)} async-done(((bf16[128,512]{0,1:T(8,128)(2,1)}), bf16[2048,512]{0,1:T(8,128)(2,1)}) %all-gather.21.cloned.1.call-update) | async-done | bytes 2097168 | tf_op jit(solution)/shard_map/all_gather | solution.py:129
  237.0 17.2 scatter_custom_fusion.1
  259.3 28.0 %scatter_custom_fusion = bf16[1024,2560]{1,0:T(8,128)(2,1)} fusion(s32[768]{0:T(1024)S(1)} %copy-done.56, bf16[128,2560]{1,0:T(8,128)(2,1)S(1)} %multiply_convert_fusion.6, s32[1024]{0:T(1024)S(1)} %pad_clamp_fusion.1, bf16[]{:T(256)} %constant.82.clone.1), kind=kCustom, calls=%fused_computation.64 | custom fusion | bytes 5242882 | tf_op jit(solution)/shard_map/scatter | solution.py:197
  287.3 71.8 %all-to-all-done.2 = bf16[16,64,2560]{2,1,0:T(8,128)(2,1)} async-done(((bf16[16,64,2560]{2,1,0:T(8,128)(2,1)}), bf16[16,64,2560]{2,1,0:T(8,128)(2,1)}, u32[]{:S(2)}, u32[]{:S(2)}) %all-to-all-start.2) | async-done | bytes 5242912 | tf_op jit(solution)/shard_map/all_to_all | solution.py:245
  359.1 24.9 %all-to-all-start = ((bf16[16,64,2560]{2,1,0:T(8,128)(2,1)}), bf16[16,64,2560]{2,1,0:T(8,128)(2,1)}, u32[]{:S(2)}, u32[]{:S(2)}) async-start(bf16[16,64,2560]{2,1,0:T(8,128)(2,1)} %bitcast.272), calls=%async_computation | async-start | bytes 10485760 | tf_op jit(solution)/shard_map/all_to_all | solution.py:200
  399.2 81.8 %all-to-all-done = bf16[16,64,2560]{2,1,0:T(8,128)(2,1)} async-done(((bf16[16,64,2560]{2,1,0:T(8,128)(2,1)}), bf16[16,64,2560]{2,1,0:T(8,128)(2,1)}, u32[]{:S(2)}, u32[]{:S(2)}) %all-to-all-start) | async-done | bytes 5242912 | tf_op jit(solution)/shard_map/all_to_all | solution.py:200
  494.8 18.5 fusion.24
  527.6 24.0 %all-to-all-start.1 = ((bf16[16,64,2560]{2,1,0:T(8,128)(2,1)}), bf16[16,64,2560]{2,1,0:T(8,128)(2,1)}, u32[]{:S(2)}, u32[]{:S(2)}) async-start(bf16[16,64,2560]{2,1,0:T(8,128)(2,1)} %bitcast.286), calls=%async_computation.1 | async-start | bytes 10485760 | tf_op jit(solution)/shard_map/all_to_all | solution.py:208
  564.0 15.3 add_convert_fusion
  579.4 69.2 %all-to-all-done.1 = bf16[16,64,2560]{2,1,0:T(8,128)(2,1)} async-done(((bf16[16,64,2560]{2,1,0:T(8,128)(2,1)}), bf16[16,64,2560]{2,1,0:T(8,128)(2,1)}, u32[]{:S(2)}, u32[]{:S(2)}) %all-to-all-start.1) | async-done | bytes 5242912 | tf_op jit(solution)/shard_map/all_to_all | solution.py:208
  648.5 24.1 %all-to-all-start.3 = ((bf16[16,64,2560]{2,1,0:T(8,128)(2,1)}), bf16[16,64,2560]{2,1,0:T(8,128)(2,1)}, u32[]{:S(2)}, u32[]{:S(2)}) async-start(bf16[16,64,2560]{2,1,0:T(8,128)(2,1)} %bitcast.285), calls=%async_computation.3 | async-start | bytes 10485760 | tf_op jit(solution)/shard_map/all_to_all | solution.py:261
  744.3 36.6 %scatter_fusion = f32[128,16]{0,1:T(8,128)S(1)} fusion(f32[128,16]{0,1:T(8,128)S(1)} %broadcast_in_dim.100, s32[768]{0:T(1024)S(1)} %reshape.594, f32[768]{0:T(1024)S(1)} %reshape.596), kind=kCustom, calls=%fused_computation.6 | custom fusion | flops 768 | bytes 15360 | tf_op jit(solution)/shard_map/transpose(jvp(jit(take_along_axis)))/scatter-add | solution.py:70
  865.0 14.6 fusion.2
  889.9 48.3 %reduce-scatter.42.cloned.1.call-done = bf16[128,512]{1,0:T(8,128)(2,1)} async-done(((bf16[2048,512]{1,0:T(8,128)(2,1)}), bf16[128,512]{1,0:T(8,128)(2,1)}) %reduce-scatter.42.cloned.1.call-update) | async-done | bytes 131088
  941.9 76.9 %reduce-scatter.40.cloned.1.call-done = bf16[128,512]{1,0:T(8,128)(2,1)} async-done(((bf16[2048,512]{1,0:T(8,128)(2,1)}), bf16[128,512]{1,0:T(8,128)(2,1)}) %reduce-scatter.40.cloned.1.call-update) | async-done | bytes 131088
  1081.9 14.7 convolution_convert_fusion.5
  1110.9 15.0 convolution_convert_fusion.7
  1130.6 26.0 %reduce-scatter.24.cloned.1.call-done = bf16[1280,2560]{1,0:T(8,128)(2,1)} async-done(((bf16[2560,2560]{1,0:T(8,128)(2,1)}), bf16[1280,2560]{1,0:T(8,128)(2,1)}) %reduce-scatter.24.cloned.1.call-update) | async-done | bytes 6553616 | tf_op jit(solution)/shard_map/reduce_scatter | solution.py:369
  1156.6 26.2 %reduce-scatter.18.cloned.1.call-done = bf16[1280,2560]{1,0:T(8,128)(2,1)} async-done(((bf16[2560,2560]{1,0:T(8,128)(2,1)}), bf16[1280,2560]{1,0:T(8,128)(2,1)}) %reduce-scatter.18.cloned.1.call-update) | async-done | bytes 6553616 | tf_op jit(solution)/shard_map/reduce_scatter | solution.py:351
  1210.4 78.8 %all-reduce.6 = (bf16[1280]{0:T(1024)(128)(2,1)S(1)}, bf16[1280]{0:T(1024)(128)(2,1)S(1)}, bf16[1280,16]{0,1:T(8,128)(2,1)S(1)}) all-reduce(bf16[1280]{0:T(1024)(128)(2,1)S(1)} %dynamic-slice.2, bf16[1280]{0:T(1024)(128)(2,1)S(1)} %dynamic-slice.4, ...), channel_id=1, replica_groups=mesh['expert'=16,'fsdp'=2] {'expert'}, use_global_device_ids=true, to_apply=%region_25.26 | all-reduce | flops 23040 | bytes 92160 | tf_op jit(solution)/shard_map/psum | solution.py:405
  1313.4 983.5 %all-reduce.11.cloned.1.call-done = (bf16[1280,2560]{1,0:T(8,128)(2,1)}, bf16[1280,512]{1,0:T(8,128)(2,1)}, bf16[1280,512]{1,0:T(8,128)(2,1)}, bf16[1280,2560]{1...) async-done(((bf16[1280,2560]{1,0:T(8,128)(2,1)}, bf16[1280,512]{1,0:T(8,128)(2,1)}, ...) | async-done | bytes 39321616 | tf_op jit(solution)/shard_map/psum | solution.py:406
  (363 shorter events, 536.0 us)
Async XLA Ops:
  26.8 101.7 %all-gather.23.cloned.1.call-start = ((), (), s32[]{:S(2)}) async-start(), calls=%async_computation.21 | async-start | bytes 19660800 | tf_op jit(solution)/shard_map/all_gather | solution.py:108
  27.4 168.7 %all-gather.21.cloned.1.call-start = ((), (), s32[]{:S(2)}) async-start(), calls=%async_computation.20 | async-start | bytes 2228224 | tf_op jit(solution)/shard_map/all_gather | solution.py:129
  45.5 177.7 %all-gather.25.cloned.1.call-start = ((), (), s32[]{:S(2)}) async-start(), calls=%async_computation.22 | async-start | bytes 19660800 | tf_op jit(solution)/shard_map/all_gather | solution.py:111
  46.1 338.7 %all-gather.37.cloned.1.call-start = ((), (), s32[]{:S(2)}) async-start(), calls=%async_computation.28 | async-start | bytes 11796480 | tf_op jit(solution)/shard_map/all_gather | solution.py:183
  46.8 352.3 %all-gather.35.cloned.1.call-start = ((), (), s32[]{:S(2)}) async-start(), calls=%async_computation.27 | async-start | bytes 11796480 | tf_op jit(solution)/shard_map/all_gather | solution.py:182
  47.6 447.2 %all-gather.33.cloned.1.call-start = ((), (), s32[]{:S(2)}) async-start(), calls=%async_computation.26 | async-start | bytes 11796480 | tf_op jit(solution)/shard_map/all_gather | solution.py:181
  48.4 624.8 %all-gather.27.cloned.1.call-start = ((), (), s32[]{:S(2)}) async-start(), calls=%async_computation.23 | async-start | bytes 23592960 | tf_op jit(solution)/shard_map/all_gather | solution.py:171
  254.2 104.8 %all-to-all-start.2 = ((bf16[16,64,2560]{2,1,0:T(8,128)(2,1)}), bf16[16,64,2560]{2,1,0:T(8,128)(2,1)}, u32[]{:S(2)}, u32[]{:S(2)}) async-start(bf16[16,64,2560]{2,1,0:T(8,128)(2,1)} %bitcast.273), calls=%async_computation.2 | async-start | bytes 10485760 | tf_op jit(solution)/shard_map/all_to_all | solution.py:245
  359.1 121.9 %all-to-all-start = ((bf16[16,64,2560]{2,1,0:T(8,128)(2,1)}), bf16[16,64,2560]{2,1,0:T(8,128)(2,1)}, u32[]{:S(2)}, u32[]{:S(2)}) async-start(bf16[16,64,2560]{2,1,0:T(8,128)(2,1)} %bitcast.272), calls=%async_computation | async-start | bytes 10485760 | tf_op jit(solution)/shard_map/all_to_all | solution.py:200
  384.0 298.0 %all-gather.29.cloned.1.call-start = ((), (), s32[]{:S(2)}) async-start(), calls=%async_computation.24 | async-start | bytes 23592960 | tf_op jit(solution)/shard_map/all_gather | solution.py:172
  527.6 120.9 %all-to-all-start.1 = ((bf16[16,64,2560]{2,1,0:T(8,128)(2,1)}), bf16[16,64,2560]{2,1,0:T(8,128)(2,1)}, u32[]{:S(2)}, u32[]{:S(2)}) async-start(bf16[16,64,2560]{2,1,0:T(8,128)(2,1)} %bitcast.286), calls=%async_computation.1 | async-start | bytes 10485760 | tf_op jit(solution)/shard_map/all_to_all | solution.py:208
  551.6 139.2 %all-gather.31.cloned.1.call-start = ((), (), s32[]{:S(2)}) async-start(), calls=%async_computation.25 | async-start | bytes 23592960 | tf_op jit(solution)/shard_map/all_gather | solution.py:173
  648.5 132.5 %all-to-all-start.3 = ((bf16[16,64,2560]{2,1,0:T(8,128)(2,1)}), bf16[16,64,2560]{2,1,0:T(8,128)(2,1)}, u32[]{:S(2)}, u32[]{:S(2)}) async-start(bf16[16,64,2560]{2,1,0:T(8,128)(2,1)} %bitcast.285), calls=%async_computation.3 | async-start | bytes 10485760 | tf_op jit(solution)/shard_map/all_to_all | solution.py:261
  672.6 265.6 %reduce-scatter.42.cloned.1.call-start = ((), (), s32[]{:S(2)}) async-start(), calls=%async_computation.41 | async-start | bytes 2228224
  850.4 168.4 %reduce-scatter.40.cloned.1.call-start = ((), (), s32[]{:S(2)}) async-start(), calls=%async_computation.40 | async-start | bytes 2228224
  889.9 236.3 %reduce-scatter.22.cloned.1.call-start = ((), (), s32[]{:S(2)}) async-start(), calls=%async_computation.31 | async-start | bytes 3932160 | tf_op jit(solution)/shard_map/reduce_scatter | solution.py:363
  941.6 184.6 %reduce-scatter.20.cloned.1.call-start = ((), (), s32[]{:S(2)}) async-start(), calls=%async_computation.30 | async-start | bytes 3932160 | tf_op jit(solution)/shard_map/reduce_scatter | solution.py:357
  1052.7 103.9 %reduce-scatter.24.cloned.1.call-start = ((), (), s32[]{:S(2)}) async-start(), calls=%async_computation.32 | async-start | bytes 19660800 | tf_op jit(solution)/shard_map/reduce_scatter | solution.py:369
  1063.4 119.4 %reduce-scatter.18.cloned.1.call-start = ((), (), s32[]{:S(2)}) async-start(), calls=%async_computation.29 | async-start | bytes 19660800 | tf_op jit(solution)/shard_map/reduce_scatter | solution.py:351
  1080.1 130.2 %reduce-scatter.26.cloned.1.call-start = ((), (), s32[]{:S(2)}) async-start(), calls=%async_computation.33 | async-start | bytes 122880 | tf_op jit(solution)/shard_map/reduce_scatter | solution.py:378
  1081.8 212.0 %reduce-scatter.38.cloned.1.call-start = ((), (), s32[]{:S(2)}) async-start(), calls=%async_computation.39 | async-start | bytes 11796480 | tf_op jit(solution)/shard_map/reduce_scatter | solution.py:423
  1096.6 203.8 %reduce-scatter.36.cloned.1.call-start = ((), (), s32[]{:S(2)}) async-start(), calls=%async_computation.38 | async-start | bytes 11796480 | tf_op jit(solution)/shard_map/reduce_scatter | solution.py:420
  1110.8 196.1 %reduce-scatter.34.cloned.1.call-start = ((), (), s32[]{:S(2)}) async-start(), calls=%async_computation.37 | async-start | bytes 11796480 | tf_op jit(solution)/shard_map/reduce_scatter | solution.py:417
  1125.9 1171.1 %all-reduce.11.cloned.1.call-start = ((), (), s32[]{:S(2)}) async-start(), calls=%async_computation.42 | async-start | bytes 78643200 | tf_op jit(solution)/shard_map/psum | solution.py:406
  (81 other events, 3013.0 us)
Sparse Core Ops, SparseCore 0:
  9.6 14.0 all-gather.14
  25.2 12.5 all-gather.18
  41.1 61.8 all-gather.16
  104.4 24.0 all-gather.22
  131.6 64.4 all-gather.20
  197.6 23.5 all-gather.24
  222.7 20.2 all-gather.36
  244.6 20.2 all-gather.34
  266.4 20.2 all-gather.32
  288.1 29.6 all-gather.26
  386.4 29.7 all-gather.28
  553.7 29.7 all-gather.30
  850.5 87.6 reduce-scatter.41
  940.9 77.8 reduce-scatter.39
  1031.5 11.4 reduce-scatter.19
  1045.7 26.4 reduce-scatter.27
  1075.0 26.3 reduce-scatter.29
  1104.2 26.3 reduce-scatter.31
  1133.4 23.2 reduce-scatter.23
  1159.5 23.2 reduce-scatter.17
  1197.1 17.6 reduce-scatter.37
  1217.6 17.6 reduce-scatter.35
  1238.2 17.6 reduce-scatter.33
  1263.3 1033.6 all-reduce.10
  (2 shorter events, 15.8 us)
where the time goes:
time: 2360 us
  waiting for transfers between devices  1510 us (64%)
  matrix products  345 us (15%)
  other arithmetic  176 us (7%)
  local copies, waits for them, and re-layouts  144 us (6%)
  blocking collectives  88 us (4%)
  starting transfers between devices  80 us (3%)
    psum x1, waiting for transfers between devices, local(): lax.psum(part_q.astype(jnp.bfloat16), 'expert').astype(jnp.float32)  984 us
    unnamed x28, waiting for transfers between devices  132 us
    dot_general x10, matrix products, matrix_multiply_transposed(): lax.dot_general(left, right, (((1,), (1,)), ((), ())), preferred_element_...  100 us
    dot_general x10, matrix products, matrix_multiply(): return jnp.dot(left, right, preferred_element_type=jnp.float32)  92.6 us
    dot_general x10, matrix products, matmul_tn(): lax.dot_general(left, right, (((0,), (0,)), ((), ())), preferred_element_...  92.2 us
    all_to_all x1, waiting for transfers between devices, local(): lax.all_to_all(outgoing, 'expert', split_axis=0, concat_axis=0, tiled=True)  81.8 us
    psum x1, blocking collectives, local(): lax.psum(part_g1.astype(jnp.bfloat16), 'expert').astype(jnp.float32)  78.8 us
    all_to_all x1, waiting for transfers between devices, local(): lax.all_to_all(d_outgoing, 'expert', split_axis=0, concat_axis=0, tiled=T...  71.8 us
  transfers between devices with their start and end apart: 30, of which 14 were waited for; matrix products, arithmetic and copies ran while one was open for 22% of the time, Pallas kernels for 0%

commit v1 on v0

v1 whole, which is shorter than its diff:
```python
import jax
import jax.numpy as jnp
from jax import lax
from jax.experimental import pallas as pl
from jax.experimental.pallas import tpu as pltpu
from jax.sharding import PartitionSpec as P

QUERY_HEADS = 20
KEY_HEADS = 4
HEAD_DIM = 128

epsilon = 1e-05
rope_base = 500000.0
masked_score = -1e30
highest = lax.Precision.HIGHEST
LOW = jnp.bfloat16
MESH = pl.DeviceIdType.MESH


def dot_nn(left, right):
    return jnp.dot(left, right, preferred_element_type=jnp.float32)


def dot_nt(left, right):
    return lax.dot_general(
        left, right, (((1,), (1,)), ((), ())), preferred_element_type=jnp.float32
    )


def dot_tn(left, right):
    return lax.dot_general(
        left, right, (((0,), (0,)), ((), ())), preferred_element_type=jnp.float32
    )


def rms_scale(vector, gain):
    factor = lax.rsqrt(jnp.mean(vector * vector, axis=-1, keepdims=True) + epsilon)
    return vector * factor * gain


def rms_back(vector, gain, grad):
    factor = lax.rsqrt(jnp.mean(vector * vector, axis=-1, keepdims=True) + epsilon)
    scaled = grad * gain
    inner = jnp.mean(scaled * vector, axis=-1, keepdims=True)
    d_vector = factor * scaled - vector * (factor * factor * factor * inner)
    return d_vector, jnp.sum(grad * vector * factor, axis=0)


def rotate(heads, cosine, sine):
    half = heads.shape[-1] // 2
    front, back = heads[..., :half], heads[..., half:]
    return jnp.concatenate([front * cosine - back * sine, back * cosine + front * sine], axis=-1)


def rope_tables(positions):
    frequency = 1.0 / rope_base ** (jnp.arange(0, HEAD_DIM, 2, dtype=jnp.float32) / HEAD_DIM)
    turned = positions.astype(jnp.float32)[:, None] * frequency[None, :]
    return jnp.cos(turned)[:, None, :], jnp.sin(turned)[:, None, :]


def swiglu(gate, up):
    return gate * jax.nn.sigmoid(gate) * up


def swiglu_back(gate, up, grad):
    sigma = jax.nn.sigmoid(gate)
    return grad * up * (sigma * (1.0 + gate * (1.0 - sigma))), grad * gate * sigma


def coordinates():
    me = lax.axis_index("expert")
    quarter = lax.rem(me, 4)
    depth = me // 4
    across = quarter + 1 - 2 * lax.rem(quarter, 2)
    beside = quarter + 2 - 4 * (quarter // 2)
    return me, quarter, depth, across, beside


def when(condition):
    return pl.when(condition)


def send(source, target, send_sem, recv_sem, **device):
    return pltpu.make_async_remote_copy(
        src_ref=source,
        dst_ref=target,
        send_sem=send_sem,
        recv_sem=recv_sem,
        device_id=device,
        device_id_type=MESH,
    )


def enter(peers, everyone):
    me, quarter, depth, across, beside = coordinates()
    barrier = pltpu.get_barrier_semaphore()

    def greet(**device):
        pl.semaphore_signal(barrier, inc=1, device_id=device, device_id_type=MESH)

    if everyone:
        for step in range(1, 16):
            greet(expert=lax.rem(me + step, 16))
        near = 15
    else:
        greet(expert=depth * 4 + across)
        greet(expert=depth * 4 + beside)

        @when(depth < 3)
        def _():
            greet(expert=me + 4)

        @when(depth > 0)
        def _():
            greet(expert=me - 4)

        near = 2 + jnp.minimum(depth, 1) + jnp.minimum(3 - depth, 1)

    side = lax.axis_index("fsdp")
    for step in range(1, peers):
        greet(fsdp=lax.rem(side - step + peers, peers))
    pl.semaphore_wait(barrier, near + (peers - 1))


class Gather:
    def __init__(self, rows, width, peers):
        self.rows, self.width = rows, width
        self.peers = peers
        self.half = self.width // 2 // 128 * 128

    def scratch(self):
        shapes = [pltpu.SemaphoreType.DMA((11, 4)), pltpu.SemaphoreType.DMA((2,))]
        if self.peers > 1:
            shapes += [pltpu.SemaphoreType.DMA((2, self.peers - 1, 16))]
        return shapes

    def stages(self, source, out, sems, own_sem, mate_sems=None):
        rows, half = self.rows, self.half
        names = ("zr", "xr", "yr", "ar", "br", "us", "ds", "xs", "ys", "as", "bs")
        row_of = {name: index for index, name in enumerate(names)}
        spans = {"a": pl.ds(0, half), "b": pl.ds(half, self.width - half)}

        def sem(name, plane):
            return sems.at[row_of[name], plane]

        columns = pl.ds(0, self.width)

        def block(index):
            return out.at[0, index, :, columns]

        def part(index, name):
            return out.at[0, index, :, spans[name]]

        def hop(name, plane):
            me, quarter, depth, across, beside = coordinates()
            own = plane * 4 + quarter
            if name in ("u", "d"):
                shift = 4 if name == "u" else -4
                return send(
                    block(own), block(own), sem(name + "s", plane), sem("zr", plane),
                    expert=me + shift,
                )
            if name == "x":
                return send(
                    block(own), block(own), sem("xs", plane), sem("xr", plane),
                    expert=depth * 4 + across,
                )
            if name == "y":
                return send(
                    block(own), block(own), sem("ys", plane), sem("yr", plane),
                    expert=depth * 4 + beside,
                )
            if name == "a":
                index = plane * 4 + across
                return send(
                    part(index, "a"), part(index, "a"), sem("as", plane), sem("ar", plane),
                    expert=depth * 4 + beside,
                )
            index = plane * 4 + beside
            return send(
                part(index, "b"), part(index, "b"), sem("bs", plane), sem("br", plane),
                expert=depth * 4 + across,
            )

        def landed(name, plane):
            me, quarter, depth, across, beside = coordinates()
            index = {
                "z": plane * 4 + quarter,
                "x": plane * 4 + across,
                "y": plane * 4 + beside,
                "a": plane * 4 + (3 - quarter),
                "b": plane * 4 + (3 - quarter),
            }[name]
            ref = part(index, name) if name in ("a", "b") else block(index)
            return send(ref, ref, sem("us", plane), sem(name + "r", plane), expert=me)

        def mates(index, start):
            side = lax.axis_index("fsdp")
            for step in range(1, self.peers):
                copy = send(
                    out.at[0, index, :, columns],
                    out.at[step, index, :, columns],
                    mate_sems.at[0, step - 1, index],
                    mate_sems.at[1, step - 1, index],
                    fsdp=lax.rem(side - step + self.peers, self.peers),
                )
                if start:
                    copy.start()
                else:
                    copy.wait()

        def own_copy():
            me = lax.axis_index("expert")
            return pltpu.make_async_copy(source.at[:, columns], block(me), own_sem.at[0])

        def spread(plane):
            hop("x", plane).start()
            hop("y", plane).start()
            mates(plane * 4 + coordinates()[1], True)

        def first():
            depth = coordinates()[2]
            own_copy().start()
            own_copy().wait()

            @when(depth < 3)
            def _():
                hop("u", depth).start()

            @when(depth > 0)
            def _():
                hop("d", depth).start()

            spread(depth)

        def arrive(distance):
            depth = coordinates()[2]

            @when(depth >= distance)
            def _():
                plane = depth - distance
                landed("z", plane).wait_recv()

                @when(depth < 3)
                def _():
                    hop("u", plane).start()

                spread(plane)

            @when(depth + distance <= 3)
            def _():
                plane = depth + distance
                landed("z", plane).wait_recv()

                @when(depth > 0)
                def _():
                    hop("d", plane).start()

                spread(plane)

        def both(distance, action):
            depth = coordinates()[2]
            if distance == 0:
                action(depth)
                return

            @when(depth >= distance)
            def _():
                action(depth - distance)

            @when(depth + distance <= 3)
            def _():
                action(depth + distance)

        def cross(plane):
            me, quarter, depth, across, beside = coordinates()
            landed("x", plane).wait_recv()
            hop("a", plane).start()
            mates(plane * 4 + across, True)
            landed("y", plane).wait_recv()
            hop("b", plane).start()
            mates(plane * 4 + beside, True)

        def corner(plane):
            quarter = coordinates()[1]
            landed("a", plane).wait_recv()
            landed("b", plane).wait_recv()
            mates(plane * 4 + 3 - quarter, True)

        def finish():
            me, quarter, depth, across, beside = coordinates()
            for plane in range(4):
                for name in ("x", "y", "a", "b"):
                    hop(name, plane).wait_send()

                @when((plane <= depth) & (depth < 3))
                def _():
                    hop("u", plane).wait_send()

                @when((plane >= depth) & (depth > 0))
                def _():
                    hop("d", plane).wait_send()

            if self.peers > 1:
                def settle(index, carry):
                    mates(index, False)
                    return carry

                lax.fori_loop(0, 16, settle, 0)

        stages = [first]
        stages.append(lambda: arrive(1))
        stages.append(lambda: both(0, cross))
        stages.append(lambda: arrive(2))
        stages.append(lambda: both(1, cross))
        stages.append(lambda: (both(0, corner), arrive(3)))
        stages.append(lambda: both(2, cross))
        stages.append(lambda: both(1, corner))
        stages.append(lambda: both(3, cross))
        stages.append(lambda: both(2, corner))
        stages.append(lambda: (both(3, corner), finish()))
        return stages


class GatherLast:
    def __init__(self, rows, start, width, peers):
        self.rows, self.start, self.width, self.peers = rows, start, width, peers
        self.half = (rows // 2 + 15) // 16 * 16

    def scratch(self):
        shapes = [pltpu.SemaphoreType.DMA((8,)), pltpu.SemaphoreType.DMA((3, 16))]
        shapes += [pltpu.SemaphoreType.DMA((1,))]
        if self.peers > 1:
            shapes += [pltpu.SemaphoreType.DMA((2, self.peers - 1, 16))]
        return shapes

    def stages(self, source, out, sems, line_sems, own_sem, mate_sems=None):
        columns = pl.ds(self.start, self.width)
        spans = {"a": pl.ds(0, self.half), "b": pl.ds(self.half, self.rows - self.half)}

        def block(index, slot=0):
            return out.at[slot, index, :, columns]

        def part(index, name):
            return out.at[0, index, spans[name], columns]

        def hop(name):
            me, quarter, depth, across, beside = coordinates()
            at_x, at_y = depth * 4 + across, depth * 4 + beside
            if name == "x":
                return send(block(me), block(me), sems.at[0], sems.at[1], expert=at_x)
            if name == "y":
                return send(block(me), block(me), sems.at[2], sems.at[3], expert=at_y)
            if name == "a":
                ref = part(at_x, "a")
                return send(ref, ref, sems.at[4], sems.at[5], expert=at_y)
            ref = part(at_y, "b")
            return send(ref, ref, sems.at[6], sems.at[7], expert=at_x)

        def landed(name):
            me, quarter, depth, across, beside = coordinates()
            corner = depth * 4 + 3 - quarter
            ref = {
                "x": lambda: block(depth * 4 + across),
                "y": lambda: block(depth * 4 + beside),
                "a": lambda: part(corner, "a"),
                "b": lambda: part(corner, "b"),
            }[name]()
            number = {"x": 1, "y": 3, "a": 5, "b": 7}[name]
            return send(ref, ref, sems.at[number - 1], sems.at[number], expert=me)

        def along(index, up):
            me = lax.axis_index("expert")
            return send(
                block(index), block(index),
                line_sems.at[0 if up else 1, index], line_sems.at[2, index],
                expert=me + 4 if up else me - 4,
            )

        def mates(index, start):
            side = lax.axis_index("fsdp")
            for step in range(1, self.peers):
                copy = send(
                    block(index), block(index, step),
                    mate_sems.at[0, step - 1, index], mate_sems.at[1, step - 1, index],
                    fsdp=lax.rem(side - step + self.peers, self.peers),
                )
                if start:
                    copy.start()
                else:
                    copy.wait()

        def both_ways(index):
            depth = coordinates()[2]

            @when(depth < 3)
            def _():
                along(index, True).start()

            @when(depth > 0)
            def _():
                along(index, False).start()

            mates(index, True)

        def first():
            me = lax.axis_index("expert")
            own = pltpu.make_async_copy(source.at[:, columns], block(me), own_sem.at[0])
            own.start()
            own.wait()
            hop("x").start()
            hop("y").start()
            both_ways(me)

        def cross():
            me, quarter, depth, across, beside = coordinates()
            landed("x").wait_recv()
            hop("a").start()
            both_ways(depth * 4 + across)
            landed("y").wait_recv()
            hop("b").start()
            both_ways(depth * 4 + beside)

        def corner():
            me, quarter, depth, across, beside = coordinates()
            landed("a").wait_recv()
            landed("b").wait_recv()
            both_ways(depth * 4 + 3 - quarter)

        def arrive(distance, which):
            depth = coordinates()[2]

            @when(depth >= distance)
            def _():
                for quarter in which:
                    index = (depth - distance) * 4 + quarter
                    along(index, True).wait_recv()

                    @when(depth < 3)
                    def _(index=index):
                        along(index, True).start()

                    mates(index, True)

            @when(depth + distance <= 3)
            def _():
                for quarter in which:
                    index = (depth + distance) * 4 + quarter
                    along(index, False).wait_recv()

                    @when(depth > 0)
                    def _(index=index):
                        along(index, False).start()

                    mates(index, True)

        def finish():
            depth = coordinates()[2]
            for name in ("x", "y", "a", "b"):
                hop(name).wait_send()

            def settle(index, carry):
                plane = index // 4

                @when((plane <= depth) & (depth < 3))
                def _():
                    along(index, True).wait_send()

                @when((plane >= depth) & (depth > 0))
                def _():
                    along(index, False).wait_send()

                if self.peers > 1:
                    mates(index, False)
                return carry

            lax.fori_loop(0, 16, settle, 0)

        stages = [first, cross, corner]
        for distance in (1, 2, 3):
            for which in ((0, 1), (2, 3)):
                stages.append(lambda d=distance, w=which: arrive(d, w))
        return stages + [finish]


def plane_at(order):
    depth = coordinates()[2]
    inner = lax.rem(lax.rem(depth, 2) + depth // 2, 2)
    upper = depth // 2
    plane = (3 - order) + inner * (0, -2, 1, 1)[order]
    return plane + upper * (3 - 2 * plane)


def wide(value):
    return value.astype(jnp.float32)


def by_rows(start, rows, action):
    def step(index, carry):
        action(pl.ds(pl.multiple_of(start + index * 16, 16), 16))
        return carry

    lax.fori_loop(0, rows // 16, step, 0)


class Scatter:
    def __init__(self, rows, start, width):
        self.rows, self.start, self.width = rows, start, width
        self.half = self.width // 2 // 128 * 128

    def scratch(self):
        rows, half = self.rows, self.half
        rest = self.width - half
        return [
            pltpu.VMEM((2, 2, rows, half), LOW),
            pltpu.VMEM((2, 2, rows, rest), LOW),
            pltpu.VMEM((4, 2, rows, half), LOW),
            pltpu.VMEM((4, 2, rows, rest), LOW),
            pltpu.VMEM((4, rows, half), LOW),
            pltpu.VMEM((4, rows, rest), LOW),
            pltpu.VMEM((4, rows, self.width), LOW),
            pltpu.VMEM((5, rows, self.width), LOW),
            pltpu.SemaphoreType.DMA((14, 4)),
        ]

    def stages(
        self, terms, out, own_a, own_b, got_a, got_b, more_a, more_b, plane_sum, line, sems
    ):
        rows, half, width = self.rows, self.half, self.width
        left, right = pl.ds(0, half), pl.ds(half, width - half)
        mine = pl.ds(0, width)
        from_left = pl.ds(self.start, half)
        from_right = pl.ds(self.start + half, width - half)

        def over_rows(action):
            by_rows(0, rows, action)

        def bits():
            quarter = coordinates()[1]
            return lax.rem(quarter, 2), quarter // 2

        def load(order):
            plane, slot = plane_at(order), order % 2
            x, y = bits()
            return (
                pltpu.make_async_copy(
                    terms.at[plane, y, :, :, from_left], own_a.at[slot], sems.at[0, plane]
                ),
                pltpu.make_async_copy(
                    terms.at[plane, :, x, :, from_right], own_b.at[slot], sems.at[1, plane]
                ),
            )

        def first_hop(plane):
            me, quarter, depth, across, beside = coordinates()
            x, y = bits()
            return (
                send(
                    terms.at[plane, 1 - y, :, :, from_left], got_a.at[plane],
                    sems.at[2, plane], sems.at[3, plane], expert=depth * 4 + beside,
                ),
                send(
                    terms.at[plane, :, 1 - x, :, from_right], got_b.at[plane],
                    sems.at[4, plane], sems.at[5, plane], expert=depth * 4 + across,
                ),
            )

        def second_hop(order):
            me, quarter, depth, across, beside = coordinates()
            plane, slot = plane_at(order), order % 2
            x, y = bits()
            return (
                send(
                    own_a.at[slot, 1 - x], more_a.at[plane],
                    sems.at[6, plane], sems.at[7, plane], expert=depth * 4 + across,
                ),
                send(
                    own_b.at[slot, 1 - y], more_b.at[plane],
                    sems.at[8, plane], sems.at[9, plane], expert=depth * 4 + beside,
                ),
            )

        def upward(plane):
            me = lax.axis_index("expert")
            return send(
                plane_sum.at[plane], line.at[plane], sems.at[10, plane], sems.at[11, plane],
                expert=me + 4,
            )

        def downward(plane, receiver):
            me = lax.axis_index("expert")
            slot = plane + (4 - plane) * (1 - jnp.minimum(jnp.abs(plane - receiver), 1))
            return send(
                plane_sum.at[plane], line.at[slot], sems.at[12, plane], sems.at[13, plane],
                expert=me - 4,
            )

        def begin(copies):
            for copy in copies:
                copy.start()

        def pair_sums(order):
            plane, slot = plane_at(order), order % 2
            for copy in load(order):
                copy.wait()
            for copy in first_hop(plane):
                copy.wait_recv()
            for mine, got in ((own_a, got_a), (own_b, got_b)):
                for index in range(2):
                    def add(span, mine=mine, got=got, index=index):
                        mine[slot, index, span, :] = (
                            wide(mine[slot, index, span, :]) + wide(got[plane, index, span, :])
                        ).astype(LOW)

                    over_rows(add)
            begin(second_hop(order))
            if order + 2 < 4:
                begin(first_hop(plane_at(order + 2)))

        def plane_sums(order):
            plane, slot = plane_at(order), order % 2
            x, y = bits()
            for copy in second_hop(order):
                copy.wait_recv()

            def add(span):
                plane_sum[plane, span, left] = (
                    wide(own_a[slot, x, span, :]) + wide(more_a[plane, span, :])
                ).astype(LOW)
                plane_sum[plane, span, right] = (
                    wide(own_b[slot, y, span, :]) + wide(more_b[plane, span, :])
                ).astype(LOW)

            over_rows(add)
            for copy in second_hop(order):
                copy.wait_send()
            if order + 2 < 4:
                begin(load(order + 2))

        def pass_on(order):
            plane = plane_at(order)
            depth = coordinates()[2]

            def join(slot):
                def add(span):
                    plane_sum[plane, span, :] = (
                        wide(plane_sum[plane, span, :]) + wide(line[slot, span, :])
                    ).astype(LOW)

                over_rows(add)

            @when(plane > depth)
            def _():
                @when(depth > 0)
                def _():
                    upward(plane).wait_recv()
                    join(plane)

                upward(plane).start()

            @when(plane < depth)
            def _():
                @when(depth < 3)
                def _():
                    downward(plane, depth).wait_recv()
                    join(plane)

                downward(plane, depth - 1).start()

        def start():
            for order in range(2):
                begin(first_hop(plane_at(order)) + load(order))

        def finish():
            depth = coordinates()[2]

            def plain(span):
                out[span, mine] = wide(plane_sum[depth, span, :])

            over_rows(plain)

            @when(depth > 0)
            def _():
                upward(depth).wait_recv()

                def add(span):
                    out[span, mine] = out[span, mine] + wide(line[depth, span, :])

                over_rows(add)

            @when(depth < 3)
            def _():
                downward(depth, depth).wait_recv()

                def add(span):
                    out[span, mine] = out[span, mine] + wide(line[4, span, :])

                over_rows(add)

            for plane in range(4):
                for copy in first_hop(plane):
                    copy.wait_send()

                @when(plane > depth)
                def _():
                    upward(plane).wait_send()

                @when(plane < depth)
                def _():
                    downward(plane, depth - 1).wait_send()

        return [
            start,
            lambda: pair_sums(0),
            lambda: plane_sums(0),
            lambda: pair_sums(1),
            lambda: pass_on(0),
            lambda: plane_sums(1),
            lambda: pair_sums(2),
            lambda: pass_on(1),
            lambda: plane_sums(2),
            lambda: pair_sums(3),
            lambda: pass_on(2),
            lambda: plane_sums(3),
            finish,
        ]


class ScatterLast:
    def __init__(self, rows, start, width, place):
        self.rows, self.start, self.width, self.place = rows, start, width, place
        self.half = (rows // 2 + 15) // 16 * 16

    def scratch(self):
        rows, width, half = self.rows, self.width, self.half
        return [
            pltpu.VMEM((4, 2, 2, rows, width), LOW),
            pltpu.VMEM((5, 2, 2, rows, width), LOW),
            pltpu.VMEM((2, half, width), LOW),
            pltpu.VMEM((2, rows - half, width), LOW),
            pltpu.VMEM((half, width), LOW),
            pltpu.VMEM((rows - half, width), LOW),
            pltpu.SemaphoreType.DMA((5, 4)),
            pltpu.SemaphoreType.DMA((8,)),
        ]

    def stages(self, terms, out, own, line, got_a, got_b, more_a, more_b, sems, plane_sems):
        rows, half = self.rows, self.half
        columns = pl.ds(self.start, self.width)
        mine = pl.ds(self.place, self.width)
        upper, lower = pl.ds(0, half), pl.ds(half, rows - half)

        def bits():
            quarter = coordinates()[1]
            return lax.rem(quarter, 2), quarter // 2

        def load(plane):
            return pltpu.make_async_copy(
                terms.at[plane, :, :, :, columns], own.at[plane], sems.at[0, plane]
            )

        def upward(plane):
            me = lax.axis_index("expert")
            return send(
                own.at[plane], line.at[plane], sems.at[1, plane], sems.at[2, plane], expert=me + 4
            )

        def downward(plane, receiver):
            me = lax.axis_index("expert")
            slot = plane + (4 - plane) * (1 - jnp.minimum(jnp.abs(plane - receiver), 1))
            return send(
                own.at[plane], line.at[slot], sems.at[3, plane], sems.at[4, plane], expert=me - 4
            )

        def first_hop():
            me, quarter, depth, across, beside = coordinates()
            x, y = bits()
            return (
                send(
                    own.at[depth, 1 - y, :, upper], got_a, plane_sems.at[0], plane_sems.at[1],
                    expert=depth * 4 + beside,
                ),
                send(
                    own.at[depth, :, 1 - x, lower], got_b, plane_sems.at[2], plane_sems.at[3],
                    expert=depth * 4 + across,
                ),
            )

        def second_hop():
            me, quarter, depth, across, beside = coordinates()
            x, y = bits()
            return (
                send(
                    got_a.at[1 - x], more_a, plane_sems.at[4], plane_sems.at[5],
                    expert=depth * 4 + across,
                ),
                send(
                    got_b.at[1 - y], more_b, plane_sems.at[6], plane_sems.at[7],
                    expert=depth * 4 + beside,
                ),
            )

        def join(plane, slot):
            for index in range(4):
                y, x = index // 2, index % 2

                def add(span):
                    own[plane, y, x, span, :] = (
                        wide(own[plane, y, x, span, :]) + wide(line[slot, y, x, span, :])
                    ).astype(LOW)

                by_rows(0, rows, add)

        def start():
            for order in range(4):
                load(plane_at(order)).start()

        def pass_on(order):
            plane = plane_at(order)
            depth = coordinates()[2]
            load(plane).wait()

            @when(plane > depth)
            def _():
                @when(depth > 0)
                def _():
                    upward(plane).wait_recv()
                    join(plane, plane)

                upward(plane).start()

            @when(plane < depth)
            def _():
                @when(depth < 3)
                def _():
                    downward(plane, depth).wait_recv()
                    join(plane, plane)

                downward(plane, depth - 1).start()

        def gather_own():
            depth = coordinates()[2]
            load(depth).wait()

            @when(depth > 0)
            def _():
                upward(depth).wait_recv()
                join(depth, depth)

            @when(depth < 3)
            def _():
                downward(depth, depth).wait_recv()
                join(depth, 4)

            for copy in first_hop():
                copy.start()

        def pair():
            depth = coordinates()[2]
            x, y = bits()
            for copy in first_hop():
                copy.wait_recv()
            for index in range(2):

                def add_a(span):
                    got_a[index, span, :] = (
                        wide(got_a[index, span, :]) + wide(own[depth, y, index, span, :])
                    ).astype(LOW)

                by_rows(0, half, add_a)

                def add_b(span, index=index):
                    there = pl.ds(pl.multiple_of(span.start + half, 16), 16)
                    got_b[index, span, :] = (
                        wide(got_b[index, span, :]) + wide(own[depth, index, x, there, :])
                    ).astype(LOW)

                by_rows(0, rows - half, add_b)
            for copy in second_hop():
                copy.start()

        def finish():
            depth = coordinates()[2]
            x, y = bits()
            for copy in second_hop():
                copy.wait_recv()

            def total_a(span):
                out[span, mine] = wide(got_a[x, span, :]) + wide(more_a[span, :])

            by_rows(0, half, total_a)

            def total_b(span):
                there = pl.ds(pl.multiple_of(span.start + half, 16), 16)
                out[there, mine] = wide(got_b[y, span, :]) + wide(more_b[span, :])

            by_rows(0, rows - half, total_b)
            for copy in first_hop() + second_hop():
                copy.wait_send()
            for plane in range(4):

                @when(plane > depth)
                def _(plane=plane):
                    upward(plane).wait_send()

                @when(plane < depth)
                def _(plane=plane):
                    downward(plane, depth - 1).wait_send()

        return [start] + [lambda k=k: pass_on(k) for k in range(3)] + [gather_own, pair, finish]


class Direct:
    def scratch(self):
        return [pltpu.SemaphoreType.DMA((2, 16)), pltpu.SemaphoreType.DMA((1,))]

    def stages(self, source, out, sems, own_sem):
        def copy(step):
            me = lax.axis_index("expert")
            peer = lax.rem(me + step, 16)
            return send(source.at[peer], out.at[me], sems.at[0, peer], sems.at[1, me], expert=peer)

        def own():
            me = lax.axis_index("expert")
            return pltpu.make_async_copy(source.at[me], out.at[me], own_sem.at[0])

        def begin():
            own().start()
            for step in range(1, 16):
                copy(step).start()

        def finish():
            own().wait()
            me = lax.axis_index("expert")
            for step in range(1, 16):
                copy(step).wait_send()
                peer = lax.rem(me + step, 16)
                landed = send(
                    source.at[peer], out.at[peer], sems.at[0, peer], sems.at[1, peer], expert=peer
                )
                landed.wait_recv()

        return [begin, finish]


class Exchange:
    def __init__(self, peers, split):
        self.peers, self.split = peers, split

    def scratch(self):
        return [pltpu.SemaphoreType.DMA((2, self.peers - 1))]

    def stages(self, source, out, sems):
        def copies():
            side = lax.axis_index("fsdp")
            for step in range(1, self.peers):
                peer = lax.rem(side - step + self.peers, self.peers)
                part = source
                if self.split:
                    width = source.shape[1] // self.peers
                    part = source.at[:, pl.ds(pl.multiple_of(peer * width, 128), width)]
                yield send(
                    part, out.at[step - 1], sems.at[0, step - 1], sems.at[1, step - 1], fsdp=peer
                )

        def begin():
            for copy in copies():
                copy.start()

        def finish():
            for copy in copies():
                copy.wait()

        return [begin, finish]


class Work:
    def __init__(self, steps, inputs, outputs, body, scratch=(), held=()):
        self.steps, self.inputs, self.outputs, self.body = steps, inputs, outputs, body
        self.scratch, self.held = list(scratch), list(held)


def in_turn(lists):
    placed = []
    for number, one in enumerate(lists):
        for index, stage in enumerate(one[:-1]):
            placed.append((index / (len(one) - 1), number, index, stage))
    placed.sort(key=lambda item: item[:3])
    return [item[3] for item in placed] + [lambda: [one[-1]() for one in lists]]


def last_columns(width):
    return width // 4 // 128 * 128


def carry(
    name,
    collective_id,
    peers,
    gathers=(),
    scatters=(),
    directs=(),
    exchanges=(),
    works=(),
    lead=0,
    vmem=60,
):
    steps = max(1, sum(work.steps for work in works))
    any_spec = pl.BlockSpec(memory_space=pl.ANY)
    vmem_spec = pl.BlockSpec(memory_space=pltpu.VMEM)
    operands, in_specs, out_shapes, out_specs, scratch = [], [], [], [], []
    programs, places = [], []

    def add(array, out_shape, out_spec, *mine):
        for program in mine:
            programs.append(program)
            places.append((len(operands), len(out_shapes)))
        operands.append(array)
        in_specs.append(any_spec)
        out_shapes.append(out_shape)
        out_specs.append(out_spec)

    for block, own in gathers:
        rows, width = own.shape
        last = last_columns(width)
        mine = [Gather(rows, width - last, block)]
        if last:
            mine.append(GatherLast(rows, width - last, last, block))
        add(own, jax.ShapeDtypeStruct((block, 16, rows, width), own.dtype), any_spec, *mine)
    for terms, start, width in scatters:
        rows, columns = terms.shape[1:]
        last = last_columns(width)
        mine = [Scatter(rows, start, width - last)]
        if last:
            mine.append(ScatterLast(rows, start + width - last, last, width - last))
        add(
            terms.reshape(4, 2, 2, rows, columns),
            jax.ShapeDtypeStruct((rows, width), jnp.float32),
            vmem_spec,
            *mine,
        )
    for blocks in directs:
        add(blocks, jax.ShapeDtypeStruct(blocks.shape, blocks.dtype), any_spec, Direct())
    for array, split in exchanges:
        rows, width = array.shape
        width = width // peers if split else width
        shape = jax.ShapeDtypeStruct((peers - 1, rows, width), array.dtype)
        add(array, shape, any_spec, Exchange(peers, split))
    transfers = len(operands)
    scratch_counts = []
    for program in programs:
        shapes = program.scratch()
        scratch_counts.append(len(shapes))
        scratch += shapes
    begun = 0
    spans = []
    for work in works:
        def local(index, begun=begun, steps=work.steps):
            return jnp.clip(index - begun, 0, steps - 1)

        for array, shape, index_of in work.inputs:
            operands.append(array)
            in_specs.append(pl.BlockSpec(shape, lambda i, f=index_of, at=local: f(at(i))))
        for array, shape, _ in work.held:
            if isinstance(array, int):
                scratch.append(pltpu.VMEM(shape, out_shapes[array].dtype))
                continue
            operands.append(array)
            in_specs.append(any_spec)
            scratch.append(pltpu.VMEM(shape, array.dtype))
        if work.held:
            scratch.append(pltpu.SemaphoreType.DMA((len(work.held),)))
        for shape, dtype, block_shape, index_of in work.outputs:
            out_shapes.append(jax.ShapeDtypeStruct(shape, dtype))
            out_specs.append(pl.BlockSpec(block_shape, lambda i, f=index_of, at=local: f(at(i))))
        scratch += work.scratch
        spans.append((begun, begun + work.steps))
        begun += work.steps
    counts = (len(operands), len(out_shapes))

    def kernel(*refs):
        ins = refs[: counts[0]]
        outs = refs[counts[0] : counts[0] + counts[1]]
        rest = list(refs[counts[0] + counts[1] :])
        step = pl.program_id(0)
        lists = []
        for index, program in enumerate(programs):
            mine, rest = rest[: scratch_counts[index]], rest[scratch_counts[index] :]
            in_place, out_place = places[index]
            lists.append(program.stages(ins[in_place], outs[out_place], *mine))
        at = {0: [one[0] for one in lists[:lead]]}
        if lead:
            at[0] += [one[0] for one in lists[lead:]]
            at[0] += in_turn([one[1:] for one in lists[:lead]])
            lists = [one[1:] for one in lists[lead:]]
        stages = in_turn(lists)
        for index, stage in enumerate(stages):
            place = index * steps // len(stages) if index + 1 < len(stages) else steps - 1
            if lead:
                place = max(place, min(1, steps - 1))
            at.setdefault(place, []).append(stage)
        in_at, out_at = transfers, transfers
        holds, tasks = [], []
        for work, (low, high) in zip(works, spans):
            work_ins = list(ins[in_at : in_at + len(work.inputs)])
            in_at += len(work.inputs)
            sources = []
            for array, _, _ in work.held:
                sources.append(None if isinstance(array, int) else ins[in_at])
                in_at += not isinstance(array, int)
            work_outs = outs[out_at : out_at + len(work.outputs)]
            out_at += len(work.outputs)
            if work.held:
                held, sems, rest = rest[: len(sources)], rest[len(sources)], rest[len(sources) + 1 :]
                for index, (array, _, view) in enumerate(work.held):
                    source = outs[array] if isinstance(array, int) else sources[index]
                    holds.append((view(source), held[index], sems.at[index]))
                work_ins += held
            own, rest = rest[: len(work.scratch)], rest[len(work.scratch) :]
            tasks.append((work, low, high, work_ins, work_outs, own))
        for place in sorted(at):
            def act(place=place):
                if place == 0:
                    enter(peers, len(directs) > 0)
                for stage in at[place]:
                    stage()
                if place == 0:
                    for action in ("start", "wait"):
                        for hold in holds:
                            getattr(pltpu.make_async_copy(*hold), action)()

            if steps == 1:
                act()
            else:
                pl.when(step == place)(act)
        for work, low, high, work_ins, work_outs, own in tasks:
            def do(work=work, low=low, work_ins=work_ins, work_outs=work_outs, own=own):
                work.body(step - low, work_ins, work_outs, *own)

            if len(works) == 1:
                do()
            else:
                pl.when((step >= low) & (step < high))(do)

    return pl.pallas_call(
        kernel,
        name=name,
        grid=(steps,),
        out_shape=out_shapes,
        in_specs=in_specs,
        out_specs=out_specs,
        scratch_shapes=scratch,
        compiler_params=pltpu.CompilerParams(
            collective_id=collective_id,
            has_side_effects=True,
            vmem_limit_bytes=vmem * 1024 * 1024,
            dimension_semantics=("arbitrary",),
        ),
    )(*operands)


def tile_of(size):
    return 512 if size % 512 == 0 else size


def weight_parts(own, others):
    count, share, hidden = others.shape
    if share % 128:
        side = lax.axis_index("fsdp")
        mine = lax.dynamic_slice_in_dim(own, side * hidden, hidden, 1)
        twice = jnp.concatenate([mine] + [others[i] for i in range(count)], axis=0)
        twice = jnp.concatenate([twice, twice], axis=0)
        start = lax.rem(count + 1 - side, count + 1) * share
        whole = lax.dynamic_slice_in_dim(twice, start, (count + 1) * share, 0)
        return [(whole, whole.shape, lambda ref: ref)]

    def own_view(ref):
        start = pl.multiple_of(lax.axis_index("fsdp") * hidden, 128)
        return ref.at[:, pl.ds(start, hidden)]

    return [(own, (share, hidden), own_view)] + [
        (others, (share, hidden), lambda ref, w=w: ref.at[w]) for w in range(count)
    ]


def down_back(upstream, down):
    total, model = upstream.shape
    hidden = down.shape[0]
    tile = tile_of(hidden)
    across = hidden // tile

    def body(step, ins, outs):
        part = pl.ds(pl.multiple_of(lax.rem(step, across) * tile, tile), tile)
        outs[0][...] = dot_nt(ins[0][...], ins[1][part, :]).astype(LOW)

    return Work(
        total // 512 * across,
        [(upstream, (512, model), lambda s: (s // across, 0))],
        [((total, hidden), LOW, (512, tile), lambda s: (s // across, lax.rem(s, across)))],
        body,
        held=[(down, down.shape, lambda ref: ref)],
    )


def hidden_units(rows_all, d_act, gates, ups, tokens, groups):
    total, model = rows_all.shape
    count = len(gates)
    share, hidden = gates[0][1]
    tile = tile_of(hidden)
    across, height = hidden // tile, 256
    each, holds = total // groups // height, height // tokens

    def body(step, ins, outs, own_gate, own_up):
        part = pl.ds(pl.multiple_of(lax.rem(step, across) * tile, tile), tile)
        side = lax.axis_index("fsdp")
        me = lax.axis_index("expert")
        weights = ins[2:]
        pre_gate = pre_up = None
        for which in range(count):
            start = 0
            if count > 1:
                start = pl.multiple_of(lax.rem(side + which, count) * share, 128)
            rows = ins[0][:, pl.ds(start, share)]
            more_gate = dot_nn(rows, weights[which][:, part])
            more_up = dot_nn(rows, weights[count + which][:, part])
            pre_gate = more_gate if pre_gate is None else pre_gate + more_gate
            pre_up = more_up if pre_up is None else pre_up + more_up
        grad = ins[1][...].astype(jnp.float32)
        sigma = 1.0 / (1.0 + jnp.exp(-pre_gate))
        silu = pre_gate * sigma
        outs[0][...] = (silu * pre_up).astype(LOW)
        outs[1][...] = (grad * pre_up * (sigma * (1.0 + pre_gate * (1.0 - sigma)))).astype(LOW)
        outs[2][...] = (grad * silu).astype(LOW)
        row_tile = step // across

        @pl.when(lax.rem(row_tile, each) == 0)
        def _():
            here = pl.ds(pl.multiple_of(lax.rem(me, holds) * tokens, tokens), tokens)
            there = pl.ds(pl.multiple_of(row_tile // each * tokens, tokens), tokens)
            own_gate[there, part] = outs[1][here, :]
            own_up[there, part] = outs[2][here, :]

        for which in range(count):

            @pl.when(step == (groups - 1) * each * across + across + which)
            def _(which=which):
                start = 0
                if count > 1:
                    start = pl.multiple_of(lax.rem(side + which, count) * share, 128)
                outs[3][:, pl.ds(start, share)] = (
                    dot_nt(own_gate[...], weights[which][...])
                    + dot_nt(own_up[...], weights[count + which][...])
                ).astype(LOW)

    def row_tile(s):
        number = s // across
        turned = lax.rem(lax.rem(number, each) + lax.axis_index("expert") // holds, each)
        return number // each * each + turned

    def spot(s):
        return row_tile(s), lax.rem(s, across)

    return Work(
        total // height * across,
        [(rows_all, (height, model), lambda s: (row_tile(s), 0)), (d_act, (height, tile), spot)],
        [((total, hidden), LOW, (height, tile), spot)] * 3
        + [((groups * tokens, model), LOW, (groups * tokens, model), lambda s: (0, 0))],
        body,
        [pltpu.VMEM((groups * tokens, hidden), LOW)] * 2,
        held=list(gates) + list(ups),
    )


def turned_products(left, rights, dtype, depth):
    total, height = left.shape
    width = rights[0].shape[1]
    tall, tile = tile_of(height), tile_of(width)
    across, deep = width // tile, total // depth

    def body(step, ins, outs, turned, *sums):
        now = lax.rem(step, deep)
        span = pl.ds(pl.multiple_of(now * depth, depth), depth)

        @pl.when(lax.rem(step // deep, across) == 0)
        def _():
            turned[:, span] = ins[0][...].T

        for which in range(len(rights)):
            product = dot_nn(turned[:, span], ins[1 + which][...])
            if deep == 1:
                outs[which][...] = product.astype(dtype)
            else:
                sums[which][...] = jnp.where(now == 0, 0.0, sums[which][...]) + product

        if deep > 1:

            @pl.when(now == deep - 1)
            def _():
                for which in range(len(rights)):
                    outs[which][...] = sums[which][...].astype(dtype)

    def left_spot(s):
        first = lax.rem(s // deep, across) == 0
        return jnp.where(first, lax.rem(s, deep), deep - 1), s // (deep * across)

    def right_spot(s):
        return lax.rem(s, deep), lax.rem(s // deep, across)

    work = Work(
        height // tall * across * deep,
        [(left, (depth, tall), left_spot)]
        + [(right, (depth, tile), right_spot) for right in rights],
        [
            (
                (height, width),
                dtype,
                (tall, tile),
                lambda s: (s // (deep * across), lax.rem(s // deep, across)),
            )
        ]
        * len(rights),
        body,
        [pltpu.VMEM((tall, total), left.dtype)]
        + [pltpu.VMEM((tall, tile), jnp.float32)] * (len(rights) if deep > 1 else 0),
    )
    work.flops = 2 * total * height * width * len(rights)
    work.traffic = 2 * total * (height + len(rights) * width * (height // tall))
    return work


def alone(name, work, vmem=60):
    count = len(work.inputs)

    def kernel(*refs):
        outs = refs[count : count + len(work.outputs)]
        work.body(pl.program_id(0), refs[:count], outs, *refs[count + len(work.outputs) :])

    return pl.pallas_call(
        kernel,
        name=name,
        grid=(work.steps,),
        in_specs=[
            pl.BlockSpec(shape, index_of) for _, shape, index_of in work.inputs
        ],
        out_specs=[pl.BlockSpec(shape, index_of) for _, _, shape, index_of in work.outputs],
        out_shape=[jax.ShapeDtypeStruct(shape, dtype) for shape, dtype, _, _ in work.outputs],
        scratch_shapes=work.scratch,
        compiler_params=pltpu.CompilerParams(vmem_limit_bytes=vmem * 1024 * 1024),
        cost_estimate=pl.CostEstimate(
            flops=work.flops, bytes_accessed=work.traffic, transcendentals=0
        ),
    )(*[array for array, _, _ in work.inputs])


CHUNK = 256


def tile_columns(value, count):
    return jnp.concatenate([value] * count, axis=1)


def stacked(ref, count):
    return jnp.concatenate(
        [ref[:, index * HEAD_DIM : (index + 1) * HEAD_DIM] for index in range(count)], axis=0
    )


def unstacked(turned, count, tokens):
    return jnp.concatenate(
        [turned[:, index * tokens : (index + 1) * tokens].T for index in range(count)], axis=1
    )


def chunks_of(ref, columns=None):
    def chunk(index):
        if columns is None:
            return ref[pl.ds(pl.multiple_of(index * CHUNK, CHUNK), CHUNK), :]
        blocks = CHUNK // ref.shape[1]
        return ref[pl.ds(index * blocks, blocks), :, columns].reshape(CHUNK, HEAD_DIM)

    return chunk


def chunk_scores(keys, queries, key_labels, query_labels, chunk, place, count):
    tokens = queries.shape[0] // count
    span = pl.ds(pl.multiple_of(chunk * CHUNK, CHUNK), CHUNK)
    raw = dot_nt(keys(chunk), queries) * HEAD_DIM ** (-0.5)
    row = chunk * CHUNK + lax.broadcasted_iota(jnp.int32, (CHUNK, tokens), 0)
    column = place * tokens + lax.broadcasted_iota(jnp.int32, (CHUNK, tokens), 1)
    allowed = (key_labels[span, :] == query_labels[...]) & (row <= column)
    bias = jnp.where(allowed, 0.0, masked_score)
    return span, raw + tile_columns(bias, count)


def attend_kernel(place, q_ref, keys, values, kl_ref, ql_ref, out_ref, log_ref, score_ref):
    tokens = q_ref.shape[0]
    count = q_ref.shape[1] // HEAD_DIM
    queries = stacked(q_ref, count)
    chunks = kl_ref.shape[0] // CHUNK

    def scores(chunk, top):
        span, value = chunk_scores(keys, queries, kl_ref, ql_ref, chunk, place[0], count)
        score_ref[span, :] = value
        return jnp.maximum(top, jnp.max(value, axis=0, keepdims=True))

    top = lax.fori_loop(
        0, chunks, scores, jnp.full((1, count * tokens), masked_score, jnp.float32)
    )

    def mix(chunk, carried):
        total, mixed = carried
        span = pl.ds(pl.multiple_of(chunk * CHUNK, CHUNK), CHUNK)
        prob = jnp.exp(score_ref[span, :] - top)
        return (
            total + jnp.sum(prob, axis=0, keepdims=True),
            mixed + dot_tn(values(chunk), prob.astype(LOW)),
        )

    total, mixed = lax.fori_loop(
        0,
        chunks,
        mix,
        (
            jnp.zeros((1, count * tokens), jnp.float32),
            jnp.zeros((HEAD_DIM, count * tokens), jnp.float32),
        ),
    )
    out_ref[...] = unstacked(mixed / total, count, tokens).astype(LOW)
    log_ref[0] = jnp.broadcast_to(top + jnp.log(total), log_ref.shape[1:])


def attend_back_kernel(
    place, q_ref, k_ref, v_ref, kl_ref, ql_ref, grad_ref, log_ref, dq_ref, pair_ref, p_ref, dp_ref
):
    tokens = q_ref.shape[0]
    count = q_ref.shape[1] // HEAD_DIM
    queries = stacked(q_ref, count)
    grads = stacked(grad_ref, count)
    chunks = k_ref.shape[0] // CHUNK
    keys, values = chunks_of(k_ref), chunks_of(v_ref)
    log_total = log_ref[0, 0:1, :]
    scale = HEAD_DIM ** (-0.5)

    def probs(chunk, row_dot):
        span, value = chunk_scores(keys, queries, kl_ref, ql_ref, chunk, place[0], count)
        prob = jnp.exp(value - log_total)
        d_prob = dot_nt(values(chunk), grads)
        p_ref[span, :] = prob
        dp_ref[span, :] = d_prob
        return row_dot + jnp.sum(prob * d_prob, axis=0, keepdims=True)

    row_dot = lax.fori_loop(
        0, chunks, probs, jnp.zeros((1, count * tokens), jnp.float32)
    )

    def back(chunk, d_query):
        span = pl.ds(pl.multiple_of(chunk * CHUNK, CHUNK), CHUNK)
        prob = p_ref[span, :]
        d_score = (prob * (dp_ref[span, :] - row_dot)).astype(LOW)
        pair_ref[span, :HEAD_DIM] = (dot_nn(d_score, queries) * scale).astype(LOW)
        pair_ref[span, HEAD_DIM:] = dot_nn(prob.astype(LOW), grads).astype(LOW)
        return d_query + dot_tn(keys(chunk), d_score)

    d_query = lax.fori_loop(
        0, chunks, back, jnp.zeros((HEAD_DIM, count * tokens), jnp.float32)
    )
    dq_ref[...] = unstacked(d_query * scale, count, tokens)


def attention_specs(tokens, length, group):
    return [
        pl.BlockSpec(memory_space=pltpu.SMEM),
        pl.BlockSpec((tokens, group), lambda g: (0, g)),
        pl.BlockSpec((length, HEAD_DIM), lambda g: (0, g)),
        pl.BlockSpec((length, HEAD_DIM), lambda g: (0, KEY_HEADS + g)),
        pl.BlockSpec((length, 1), lambda g: (0, 0)),
        pl.BlockSpec((1, tokens), lambda g: (0, 0)),
    ]


def attend_work(queries, pairs_at, key_labels, query_labels):
    tokens, width = queries.shape
    length, group = key_labels.shape[0], width // KEY_HEADS
    stack = group // HEAD_DIM * tokens
    pair_width = 2 * KEY_HEADS * HEAD_DIM

    def body(step, ins, outs, scores):
        q_ref, kl_ref, ql_ref, pairs = ins
        start = pl.multiple_of(step * HEAD_DIM, HEAD_DIM)
        keys = chunks_of(pairs, pl.ds(start, HEAD_DIM))
        values = chunks_of(pairs, pl.ds(KEY_HEADS * HEAD_DIM + start, HEAD_DIM))
        place = [lax.axis_index("expert")]
        attend_kernel(place, q_ref, keys, values, kl_ref, ql_ref, *outs, scores)

    return Work(
        KEY_HEADS,
        [
            (queries, (tokens, group), lambda s: (0, s)),
            (key_labels, (length, 1), lambda s: (0, 0)),
            (query_labels, (1, tokens), lambda s: (0, 0)),
        ],
        [
            ((tokens, width), LOW, (tokens, group), lambda s: (0, s)),
            ((KEY_HEADS, 8, stack), jnp.float32, (1, 8, stack), lambda s: (s, 0, 0)),
        ],
        body,
        [pltpu.VMEM((length, stack), jnp.float32)],
        held=[
            (
                pairs_at,
                (length // tokens, tokens, pair_width),
                lambda ref: ref.at[0, :, :, pl.ds(0, pair_width)],
            )
        ],
    )


def attend_back(place, queries, pairs, key_labels, query_labels, grads, log_total):
    tokens, width = queries.shape
    length, group = pairs.shape[0], width // KEY_HEADS
    stack = group // HEAD_DIM * tokens
    return pl.pallas_call(
        attend_back_kernel,
        name="attend_back",
        grid=(KEY_HEADS,),
        in_specs=attention_specs(tokens, length, group)
        + [
            pl.BlockSpec((tokens, group), lambda g: (0, g)),
            pl.BlockSpec((1, 8, stack), lambda g: (g, 0, 0)),
        ],
        out_specs=[
            pl.BlockSpec((tokens, group), lambda g: (0, g)),
            pl.BlockSpec((length, 2 * HEAD_DIM), lambda g: (0, g)),
        ],
        out_shape=[
            jax.ShapeDtypeStruct((tokens, width), jnp.float32),
            jax.ShapeDtypeStruct((length, 2 * KEY_HEADS * HEAD_DIM), LOW),
        ],
        scratch_shapes=[pltpu.VMEM((length, stack), jnp.float32)] * 2,
        compiler_params=pltpu.CompilerParams(vmem_limit_bytes=50 * 1024 * 1024),
    )(place, queries, pairs, pairs, key_labels, query_labels, grads, log_total)


def dispatch_kernel(place, n_ref, u_ref, p_ref, m_ref, w_ref, rows_ref, up_ref, pair_ref, g_ref):
    rows = n_ref[0]
    pick = p_ref[0]
    logits = dot_nt(w_ref[...], rows)
    chosen = m_ref[...] > 0.5
    top = jnp.max(jnp.where(chosen, logits, masked_score), axis=0, keepdims=True)
    power = jnp.where(chosen, jnp.exp(jnp.where(chosen, logits - top, 0.0)), 0.0)
    mine = lax.broadcasted_iota(jnp.int32, logits.shape, 0) == place[0]
    gate = jnp.sum(jnp.where(mine, power, 0.0), axis=0, keepdims=True) / jnp.sum(
        power, axis=0, keepdims=True
    )
    slot_gate = jnp.sum(pick.astype(jnp.float32) * gate, axis=1, keepdims=True)
    rows_ref[...] = dot_nn(pick, rows).astype(LOW)
    ups = dot_nn(pick, u_ref[...])
    up_ref[...] = ups.astype(LOW)
    pair_ref[...] = (slot_gate * ups).astype(LOW)
    g_ref[...] = slot_gate


def dispatch(place, normed, upstream, pick, chosen, w_router):
    blocks, capacity, tokens = pick.shape
    model = upstream.shape[1]
    experts = w_router.shape[0]
    wide = pl.BlockSpec((capacity, model), lambda b: (b, 0))
    return pl.pallas_call(
        dispatch_kernel,
        name="dispatch",
        grid=(blocks,),
        in_specs=[
            pl.BlockSpec(memory_space=pltpu.SMEM),
            pl.BlockSpec((1, tokens, model), lambda b: (b, 0, 0)),
            pl.BlockSpec((tokens, model), lambda b: (b, 0)),
            pl.BlockSpec((1, capacity, tokens), lambda b: (b, 0, 0)),
            pl.BlockSpec((experts, tokens), lambda b: (0, b)),
            pl.BlockSpec((experts, model), lambda b: (0, 0)),
        ],
        out_specs=[wide, wide, wide, pl.BlockSpec((capacity, 1), lambda b: (b, 0))],
        out_shape=[jax.ShapeDtypeStruct((blocks * capacity, model), LOW)] * 3
        + [jax.ShapeDtypeStruct((blocks * capacity, 1), jnp.float32)],
    )(place, normed, upstream, pick, chosen, w_router)


def join_columns(side, groups, own, others):
    rows, columns = others[0].shape
    tile = rows // 10

    def kernel(side_ref, *refs):
        for step, ref in enumerate(refs[:-1]):
            start = lax.rem(side_ref[0] + step, groups) * columns
            refs[-1][:, pl.ds(pl.multiple_of(start, 128), columns)] = ref[...].astype(jnp.float32)

    return pl.pallas_call(
        kernel,
        name="join_columns",
        grid_spec=pltpu.PrefetchScalarGridSpec(
            num_scalar_prefetch=1,
            grid=(10,),
            in_specs=[pl.BlockSpec((tile, columns), lambda i, side: (side[0] * 10 + i, 0))]
            + [pl.BlockSpec((tile, columns), lambda i, side: (i, 0))] * len(others),
            out_specs=pl.BlockSpec((tile, groups * columns), lambda i, side: (i, 0)),
        ),
        out_shape=jax.ShapeDtypeStruct((rows, groups * columns), jnp.float32),
    )(side, own, *others)


def widen(arrays, cuts):
    rows = arrays[0].shape[0]
    steps = 10 if rows % 10 == 0 else 12
    tile = rows // steps
    widths = [
        [high - low for low, high in zip([0] + cut, cut + [array.shape[1]])]
        for array, cut in zip(arrays, cuts)
    ]

    def kernel(*refs):
        outs = iter(refs[len(arrays) :])
        for ref, parts in zip(refs, widths):
            start = 0
            for part in parts:
                next(outs)[...] = ref[:, start : start + part].astype(jnp.float32)
                start += part

    flat = [part for parts in widths for part in parts]
    return pl.pallas_call(
        kernel,
        name="widen",
        grid=(steps,),
        in_specs=[pl.BlockSpec((tile, array.shape[1]), lambda i: (i, 0)) for array in arrays],
        out_specs=[pl.BlockSpec((tile, part), lambda i: (i, 0)) for part in flat],
        out_shape=[jax.ShapeDtypeStruct((rows, part), jnp.float32) for part in flat],
    )(*arrays)


def expert_kernel(
    count, side, rows_ref, up_ref, pair_ref, gate_ref, back_ref, *refs
):
    w_gate, w_up, w_down = refs[:count], refs[count : 2 * count], refs[2 * count : 3 * count]
    act_ref, dg_ref, du_ref, d_gate_ref, out_ref, term_ref = refs[3 * count :]
    share = w_gate[0].shape[0]
    units = w_down[0].shape[0]
    model = rows_ref.shape[1]
    blocks, tokens, capacity = back_ref.shape

    def place(which, size):
        if count == 1:
            return pl.ds(0, size)
        return pl.ds(pl.multiple_of(lax.rem(side[0] + which, count) * size, 128), size)

    for which in range(count):
        span = place(which, units)
        pre_gate = pre_up = None
        for part in range(count):
            rows = rows_ref[:, place(part, share)]
            more_gate = dot_nn(rows, w_gate[part][:, span])
            more_up = dot_nn(rows, w_up[part][:, span])
            pre_gate = more_gate if pre_gate is None else pre_gate + more_gate
            pre_up = more_up if pre_up is None else pre_up + more_up
        d_act = dot_nt(pair_ref[...], w_down[which][...])
        sigma = 1.0 / (1.0 + jnp.exp(-pre_gate))
        silu = pre_gate * sigma
        act_ref[:, span] = (silu * pre_up).astype(LOW)
        dg_ref[:, span] = (
            d_act * pre_up * (sigma * (1.0 + pre_gate * (1.0 - sigma)))
        ).astype(LOW)
        du_ref[:, span] = (d_act * silu).astype(LOW)

    def returned(target, values, span):
        for block in range(blocks):
            mine = values[block * capacity : (block + 1) * capacity]
            target[block, :, span] = dot_nn(back_ref[block], mine).astype(LOW)

    d_gate = jnp.zeros(d_gate_ref.shape, jnp.float32)
    tile = tile_of(model)
    for index in range(model // tile):
        span = pl.ds(index * tile, tile)
        produced = None
        for part in range(count):
            more = dot_nn(act_ref[:, place(part, units)], w_down[part][:, span])
            produced = more if produced is None else produced + more
        produced = produced.astype(LOW).astype(jnp.float32)
        d_gate += jnp.sum(produced * up_ref[:, span].astype(jnp.float32), axis=1, keepdims=True)
        returned(out_ref, (gate_ref[...] * produced).astype(LOW), span)
    d_gate_ref[...] = d_gate
    for part in range(count):
        pieces = 2 if share % 256 == 0 else 1
        for piece in range(pieces):
            width = share // pieces
            rows = pl.ds(piece * width, width)
            d_rows = dot_nt(dg_ref[...], w_gate[part][rows, :]) + dot_nt(
                du_ref[...], w_up[part][rows, :]
            )
            start = piece * width
            if count > 1:
                start = pl.multiple_of(lax.rem(side[0] + part, count) * share + start, 128)
            returned(term_ref, d_rows.astype(LOW), pl.ds(start, width))


def run_expert(side, rows_in, rows_up, d_pair, slot_gate, pick, gates, ups, downs):
    slots, model = rows_in.shape
    blocks, capacity, tokens = pick.shape
    hidden = gates[0].shape[1]
    count = len(gates)
    group = 4
    tile = group * capacity
    wide = pl.BlockSpec((tile, model), lambda i, side: (i, 0))
    narrow = pl.BlockSpec((tile, hidden), lambda i, side: (i, 0))
    single = pl.BlockSpec((tile, 1), lambda i, side: (i, 0))
    terms = pl.BlockSpec((group, tokens, model), lambda i, side: (i, 0, 0))
    weights = list(gates) + list(ups) + list(downs)

    def kernel(*refs):
        expert_kernel(count, *refs)

    return pl.pallas_call(
        kernel,
        name="expert",
        grid_spec=pltpu.PrefetchScalarGridSpec(
            num_scalar_prefetch=1,
            grid=(blocks // group,),
            in_specs=[
                wide,
                wide,
                wide,
                single,
                pl.BlockSpec((group, tokens, capacity), lambda i, side: (i, 0, 0)),
            ]
            + [
                pl.BlockSpec(w.shape, lambda i, side: (0, 0), pipeline_mode=pl.Buffered(1))
                for w in weights
            ],
            out_specs=[narrow, narrow, narrow, single, terms, terms],
        ),
        out_shape=[jax.ShapeDtypeStruct((slots, hidden), LOW)] * 3
        + [jax.ShapeDtypeStruct((slots, 1), jnp.float32)]
        + [jax.ShapeDtypeStruct((blocks, tokens, model), LOW)] * 2,
        compiler_params=pltpu.CompilerParams(vmem_limit_bytes=60 * 1024 * 1024),
    )(side, rows_in, rows_up, d_pair, slot_gate, pick.transpose(0, 2, 1), *weights)


def local(
    hidden_in,
    gain_attn,
    query_weight,
    key_matrix,
    value_matrix,
    out_weight,
    gain_ffn,
    router_weight,
    shared_gate,
    shared_up,
    shared_down,
    expert_gate,
    expert_up,
    expert_down,
    routes,
    segments,
    positions,
    grad_out,
):
    tokens = hidden_in.shape[1]
    model = hidden_in.shape[2]
    experts = lax.axis_size("expert")
    groups = lax.axis_size("fsdp")
    topk = routes.shape[2]
    capacity = min(tokens, 4 * tokens * topk // (3 * experts))
    length = tokens * experts
    group_width = QUERY_HEADS // KEY_HEADS
    score_scale = HEAD_DIM ** (-0.5)
    place = lax.axis_index("expert")
    side = lax.axis_index("fsdp")
    share = model // groups

    def peer(values, step):
        if step == 0:
            return values
        return lax.ppermute(
            values, "fsdp", [((i + step) % groups, i) for i in range(groups)]
        )

    def ring(values):
        return [peer(values, step) for step in range(groups)]

    def scattered(values, axis):
        size = values.shape[axis] // groups
        return [
            peer(
                lax.dynamic_slice_in_dim(
                    values, ((side - step + groups) % groups) * size, size, axis
                ),
                step,
            )
            for step in range(groups)
        ]

    def in_order(parts, axis):
        if groups == 2:
            first = side == 0
            return jnp.concatenate(
                [jnp.where(first, parts[0], parts[1]), jnp.where(first, parts[1], parts[0])], axis
            )
        size = parts[0].shape[axis]
        twice = jnp.concatenate(parts + parts, axis)
        start = ((groups - side) % groups) * size
        return lax.dynamic_slice_in_dim(twice, start, groups * size, axis)

    def own_columns(values, step):
        size = values.shape[-1] // groups
        return lax.dynamic_slice_in_dim(values, ((side + step) % groups) * size, size, 1)

    def rows_product(values, parts):
        if len(parts) == 1:
            return dot_nn(values, parts[0])
        total = dot_nn(own_columns(values, 0), parts[0])
        for step in range(1, groups):
            total = total + dot_nn(own_columns(values, step), parts[step])
        return total

    small = jnp.concatenate([gain_attn[None], gain_ffn[None], router_weight.T], axis=0)
    small_full = in_order(ring(small), 1)
    gain_first = small_full[0].astype(jnp.float32)
    gain_second = small_full[1].astype(jnp.float32)
    w_router = small_full[2:]
    w_query, w_key, w_value, w_out = (
        ring(query_weight),
        ring(key_matrix),
        ring(value_matrix),
        ring(out_weight),
    )
    expert_ids = jnp.arange(experts, dtype=jnp.int32)
    chosen = jnp.any(routes[0][:, :, None] == expert_ids[None, None, :], axis=1)
    upstream_low = grad_out[0]
    upstream = upstream_low.astype(jnp.float32)

    x_rows = hidden_in[0].astype(jnp.float32)
    labels = segments[0]
    cosine, sine = rope_tables(positions[0])
    normed_one = rms_scale(x_rows, gain_first).astype(LOW)
    key_rows = rotate(
        rows_product(normed_one, w_key).reshape(tokens, KEY_HEADS, HEAD_DIM), cosine, sine
    ).astype(LOW)
    value_rows = rows_product(normed_one, w_value).astype(LOW)
    wide = KEY_HEADS * HEAD_DIM
    pair_rows = jnp.concatenate(
        [
            key_rows.reshape(tokens, wide),
            value_rows,
            jnp.pad(chosen.astype(LOW), ((0, 0), (0, 128 - experts))),
        ],
        axis=1,
    )
    here = place.reshape(1)
    queries = (
        rotate(
            rows_product(normed_one, w_query).reshape(tokens, QUERY_HEADS, HEAD_DIM), cosine, sine
        )
        .astype(LOW)
        .reshape(tokens, QUERY_HEADS * HEAD_DIM)
    )
    key_labels = labels[:, None]
    query_labels = lax.dynamic_slice_in_dim(labels, place * tokens, tokens)[None]
    (
        every_pair,
        upstream_each,
        gate_others,
        up_others,
        eg_others,
        eu_others,
        ed_others,
        attended,
        log_total,
    ) = carry(
        "attend",
        7,
        groups,
        gathers=[(1, pair_rows), (groups, upstream_low)],
        exchanges=[
            (shared_gate, True),
            (shared_up, True),
            (expert_gate[0], False),
            (expert_up[0], False),
            (expert_down[0], False),
        ],
        works=[attend_work(queries, 0, key_labels, query_labels)],
        lead=2,
    )
    every_pair = every_pair.reshape(length, 2 * wide + 128)
    chosen_all = every_pair[:, 2 * wide : 2 * wide + experts].T.astype(jnp.float32)
    upstream_each = upstream_each.reshape(groups * length, model)
    residual_one = x_rows + rows_product(attended, w_out)
    normed_two = rms_scale(residual_one, gain_second).astype(LOW)

    gate_parts = weight_parts(shared_gate, gate_others)
    up_parts = weight_parts(shared_up, up_others)
    normed_each, shared_d_act = carry(
        "rows",
        2,
        groups,
        gathers=[(groups, normed_two)],
        works=[down_back(upstream_each, shared_down)],
    )
    normed_blocks = normed_each.reshape(groups * experts, tokens, model)
    normed_each = normed_each.reshape(groups * length, model)

    logits = dot_nt(normed_two, w_router)
    router_probs = jax.nn.softmax(logits, axis=-1)
    chosen_probs = jnp.where(chosen, router_probs, 0.0)
    chosen_sum = jnp.sum(chosen_probs, axis=1, keepdims=True)
    gate_own = chosen_probs / chosen_sum

    def shares(own, others):
        parts = [own[0]] + [others[index] for index in range(groups - 1)]
        aligned = share % 128 == 0 and expert_down.shape[1] % 128 == 0
        return parts if aligned else [in_order(parts, 0)]

    member = (
        lax.dynamic_index_in_dim(chosen_all, place, 0, keepdims=False).reshape(experts, tokens)
        > 0.5
    )
    below = jnp.tril(jnp.ones((tokens, tokens), LOW), -1)
    rank = dot_nt(member.astype(LOW), below)
    slots = (
        member[:, None, :]
        & (rank.astype(jnp.int32)[:, None, :] == jnp.arange(capacity, dtype=jnp.int32)[None, :, None])
    )
    pick = slots.astype(LOW)

    rows_in, rows_up, d_pair, slot_weight = dispatch(
        here, normed_blocks, upstream_each, pick, chosen_all, w_router
    )
    here_side = side.reshape(1)
    expert_act, d_gate_pre, d_up_pre, d_gate_slots, out_terms, row_terms = run_expert(
        here_side,
        rows_in,
        rows_up,
        d_pair,
        slot_weight,
        pick,
        shares(expert_gate, eg_others),
        shares(expert_up, eu_others),
        shares(expert_down, ed_others),
    )
    d_gate_slots = d_gate_slots.reshape(experts, capacity, 1)
    d_gate_rows = jnp.sum(jnp.where(slots, d_gate_slots, 0.0), axis=1)
    d_gate_rows = jnp.broadcast_to(d_gate_rows[:, None, :], (experts, 8, tokens))
    half_model = model // 2
    (
        expert_back,
        out_left,
        d_gate_own,
        shared_act,
        shared_d_gate,
        shared_d_up,
        back_parts,
    ) = carry(
        "row_grads",
        3,
        1,
        scatters=[(row_terms, 0, model), (out_terms, 0, half_model)],
        directs=[d_gate_rows],
        works=[
            hidden_units(normed_each, shared_d_act, gate_parts, up_parts, tokens, groups)
        ],
    )
    d_gate_own = d_gate_own[:, 0, :].T
    def returned(terms):
        total = terms[0].astype(jnp.float32)
        for step in range(1, groups):
            back = lax.ppermute(
                terms[step], "fsdp", [(i, (i + step) % groups) for i in range(groups)]
            )
            total = total + back.astype(jnp.float32)
        return total

    shared_back = returned(back_parts.reshape(groups, tokens, model))

    d_chosen = jnp.where(
        chosen,
        (d_gate_own - jnp.sum(gate_own * d_gate_own, axis=1, keepdims=True)) / chosen_sum,
        0.0,
    )
    d_logits = router_probs * (
        d_chosen - jnp.sum(router_probs * d_chosen, axis=1, keepdims=True)
    )
    d_normed_two = (
        shared_back
        + expert_back
        + lax.dot_general(
            d_logits,
            w_router.astype(jnp.float32),
            (((1,), (0,)), ((), ())),
            precision=highest,
            preferred_element_type=jnp.float32,
        )
    )
    d_residual_norm, d_gain_two = rms_back(residual_one, gain_second, d_normed_two)
    d_residual = upstream + d_residual_norm
    d_attn_out = d_residual.astype(LOW)
    grad_router = lax.dot_general(
        d_logits,
        normed_two.astype(jnp.float32),
        (((0,), (0,)), ((), ())),
        precision=highest,
        preferred_element_type=jnp.float32,
    )

    def chip_term(left, right):
        return dot_tn(
            jnp.concatenate(scattered(left, 1), axis=0), jnp.concatenate(ring(right), axis=0)
        ).astype(LOW)

    def blocks(term):
        rows, width = term.shape
        rows = rows // experts
        term = term.reshape(experts, rows, width)
        return jnp.pad(term, ((0, 0), (0, -rows % 16), (0, 0)))

    term_o = chip_term(attended, d_attn_out)

    d_attended = in_order([dot_nt(d_attn_out, part) for part in w_out], 1).astype(LOW)
    d_query, term_pairs = attend_back(
        here, queries, every_pair, key_labels, query_labels, d_attended, log_total
    )
    d_pairs, out_right, mine_o, grad_sg, grad_su = carry(
        "pair_grads",
        4,
        1,
        scatters=[
            (term_pairs.reshape(experts, tokens, -1), 0, 2 * wide),
            (out_terms, half_model, half_model),
            (blocks(term_o), 0, model),
        ],
        works=[turned_products(normed_each, [shared_d_gate, shared_d_up], LOW, length)],
    )
    d_pairs = d_pairs.reshape(tokens, KEY_HEADS, 2, HEAD_DIM)
    d_query_low = rotate(
        d_query.reshape(tokens, QUERY_HEADS, HEAD_DIM), cosine, -sine
    ).reshape(tokens, -1).astype(LOW)
    d_key_low = rotate(d_pairs[:, :, 0], cosine, -sine).reshape(tokens, -1).astype(LOW)
    d_value_low = d_pairs[:, :, 1].reshape(tokens, -1).astype(LOW)
    d_normed_one = in_order(
        [
            dot_nt(d_query_low, w_query[step])
            + dot_nt(d_key_low, w_key[step])
            + dot_nt(d_value_low, w_value[step])
            for step in range(groups)
        ],
        1,
    )
    d_rows_norm, d_gain_one = rms_back(x_rows, gain_first, d_normed_one)
    grad_in = (d_residual + d_rows_norm).astype(LOW)
    small_grads = jnp.concatenate([d_gain_one[None], d_gain_two[None], grad_router], axis=0)
    small_grads = jnp.pad(small_grads, ((0, 256 - small_grads.shape[0]), (0, 0))).astype(LOW)
    small_parts = [part.astype(jnp.float32) for part in scattered(small_grads, 1)]
    small_term = sum(small_parts).astype(LOW).T
    term_pre = chip_term(
        normed_one, jnp.concatenate([d_query_low, d_key_low, d_value_low], axis=1)
    )
    all_o, mine_pre, mine_small, term_eg, term_eu, term_ed = carry(
        "sums",
        5,
        1,
        gathers=[(1, mine_o.astype(LOW))],
        scatters=[(blocks(term_pre), 0, term_pre.shape[1]), (blocks(small_term), 0, 256)],
        works=[
            turned_products(rows_in, [d_gate_pre, d_up_pre], LOW, rows_in.shape[0]),
            turned_products(expert_act, [d_pair], LOW, rows_in.shape[0]),
        ],
    )
    all_o = all_o.reshape(experts, -1, model)[:, : share // experts].reshape(share, model)
    mine_pre = jnp.concatenate([mine_pre, mine_small], axis=1)[: share // experts].astype(LOW)
    all_pre = lax.all_gather(mine_pre, "expert", axis=0, tiled=True)

    mine_pre, shared_act, term_eg, term_eu, term_ed, grad_sg, grad_su = lax.optimization_barrier(
        (mine_pre, shared_act, term_eg, term_eu, term_ed, grad_sg, grad_su)
    )

    own_act = lax.dynamic_slice_in_dim(
        shared_act.reshape(groups, length, -1), place * tokens, tokens, 1
    ).reshape(groups * tokens, -1)
    out_parts = dot_nn(own_act, shared_down).astype(LOW).reshape(groups, tokens, model)
    expert_sum = jnp.concatenate([out_left, out_right], axis=1)
    output = residual_one + returned(out_parts) + expert_sum

    def summed(term):
        parts = scattered(term, 0)
        size = term.shape[0] // groups
        total = lax.dynamic_slice_in_dim(term, side * size, size, 0).astype(jnp.float32)
        for part in parts[1:]:
            total = total + part.astype(jnp.float32)
        return total

    grad_eg, grad_eu, grad_ed = summed(term_eg), summed(term_eu), summed(term_ed)
    (grad_sd,) = alone(
        "down_grads", turned_products(shared_act, [upstream_each], jnp.float32, length)
    )
    grad_sg, grad_su = [
        join_columns(here_side, groups, term, scattered(term, 0)[1:])
        for term in (grad_sg, grad_su)
    ]
    grad_o, grad_q, grad_k, grad_v, small_grads = widen(
        [all_o, all_pre], [[], [model, model + wide, model + 2 * wide]]
    )
    small_grads = small_grads[:, : 2 + experts].T
    return (
        output.astype(LOW)[None],
        grad_in[None],
        small_grads[0],
        grad_q,
        grad_k,
        grad_v,
        grad_o,
        small_grads[1],
        small_grads[2:].T,
        grad_sg,
        grad_su,
        grad_sd,
        grad_eg[None],
        grad_eu[None],
        grad_ed[None],
    )


def solution(mesh):
    rows, split = P("fsdp", None), P("fsdp")
    tokens, expert = P("fsdp", "expert", None), P("expert", "fsdp", None)
    return jax.shard_map(
        local,
        mesh=mesh,
        in_specs=(
            (tokens, split, rows, rows, rows, rows, split)
            + (rows,) * 4
            + (expert,) * 3
            + (tokens, rows, P("fsdp", "expert"), tokens)
        ),
        out_specs=(
            (tokens, tokens, split)
            + (rows,) * 4
            + (split,)
            + (rows,) * 4
            + (expert,) * 3
        ),
        check_vma=False,
    )
```

time: 2360 us -> 1200 us (0.51)
  waiting for transfers between devices: 1510 us -> 6.21 us
  Pallas kernels: 0 us -> 995 us
  matrix products: 345 us -> 66.8 us
  other arithmetic: 176 us -> 47.7 us
  local copies, waits for them, and re-layouts: 144 us -> 50.5 us
  blocking collectives: 88 us -> 0 us
  starting transfers between devices: 80 us -> 4.01 us
    pallas_call x0 -> x12, Pallas kernels: none -> 995 us  [the longest x5 767 us: carry(): pl.pallas_call(kernel, name=name, grid=(steps,), out_shape=out_shapes, in...]
    psum x1 -> x0, waiting for transfers between devices: 984 us -> none  [local(): lax.psum(part_q.astype(jnp.bfloat16), 'expert').astype(jnp.float32)]
    dot_general x39 -> x23, matrix products: 345 us -> 66.8 us  [the longest x10 27.6 us: dot_nt(): lax.dot_general(left, right, (((1,), (1,)), ((), ())), preferred_element_...]
    all_to_all x4 -> x0, waiting for transfers between devices: 223 us -> none  [the longest x1 81.8 us: local(): lax.all_to_all(outgoing, 'expert', split_axis=0, concat_axis=0, tiled=True)]
    unnamed x28 -> x1, waiting for transfers between devices: 132 us -> 0.02 us
    all_gather x12 -> x1, waiting for transfers between devices: 113 us -> 3.64 us  [local(): all_pre = lax.all_gather(mine_pre, 'expert', axis=0, tiled=True)]
    psum x1 -> x0, blocking collectives: 78.8 us -> none  [local(): lax.psum(part_g1.astype(jnp.bfloat16), 'expert').astype(jnp.float32)]
    all_to_all x4 -> x0, starting transfers between devices: 78 us -> none  [the longest x1 24.9 us: local(): lax.all_to_all(outgoing, 'expert', split_axis=0, concat_axis=0, tiled=True)]
  transfers between devices with their start and end apart: 30 -> 18, of which waited for: 14 -> 3; matrix products, arithmetic and copies ran while one was open for 22% -> 10% of each run, Pallas kernels for 0% -> 55%
where the time goes in v1:
time: 1200 us; the launch traced here: 1190 us
  Pallas kernels  995 us (83%)
  matrix products  66.8 us (6%)
  local copies, waits for them, and re-layouts  50.5 us (4%)
  other arithmetic  47.7 us (4%)
  between operations  15.4 us (1%)
    pallas_call x5, Pallas kernels, carry(): pl.pallas_call(kernel, name=name, grid=(steps,), out_shape=out_shapes, in...  767 us
    pallas_call x1, Pallas kernels, run_expert(): pl.pallas_call(kernel, name='expert', grid_spec=pltpu.PrefetchScalarGridS...  83.6 us
    pallas_call x1, Pallas kernels, alone(): pl.pallas_call(kernel, name=name, grid=(work.steps,), in_specs=[pl.BlockS...  57 us
    dot_general x10, matrix products, dot_nt(): lax.dot_general(left, right, (((1,), (1,)), ((), ())), preferred_element_...  27.6 us
    pallas_call x1, Pallas kernels, attend_back(): pl.pallas_call(attend_back_kernel, name='attend_back', grid=(KEY_HEADS,),...  27.1 us
  transfers between devices with their start and end apart: 18, of which 3 were waited for; matrix products, arithmetic and copies ran while one was open for 10% of the time, Pallas kernels for 55%

profile of v1, /device:TPU:0, one launch (start us, length us, event | category | flops | bytes accessed | tf_op | source)
XLA Modules:
  0.0 1185.3 jit_solution(10825742777274941373)
XLA Ops:
  36.8 167.8 %attend.1 = (bf16[1,16,128,1152]{3,2,1,0:T(8,128)(2,1)}, bf16[2,16,128,2560]{3,2,1,0:T(8,128)(2,1)}, bf16[1,1280,1536]{2,1,0:T(8,128)(2,1)}, bf16[1,1280,1536]{2...) custom-call(bf16[128,1152]{1,0:T(8,128)(2,1)} %pad_maximum_fusion.6., ...), custom_call_target="tpu_custom_call" | custom-call | tf_op jit(solution)/shard_map/attend/pallas_call | solution.py:1145
  221.4 113.7 %rows.1 = (bf16[2,16,128,2560]{3,2,1,0:T(8,128)(2,1)}, bf16[4096,1536]{1,0:T(8,128)(2,1)}) custom-call(bf16[128,2560]{1,0:T(8,128)(2,1)} %copy-done.8, bf16[4096,2560]{1,0:T(8,128)(2,1)} %bitcast.114, bf16[1536,2560]{1,0:T(8,128)(2,1)} %refs_2_.3), custom_call_target="tpu_custom_call" | custom-call | tf_op jit(solution)/shard_map/rows/pallas_call | solution.py:1145
  335.1 20.6 %dispatch.1 = (bf16[1024,2560]{1,0:T(8,128)(2,1)}, bf16[1024,2560]{1,0:T(8,128)(2,1)}, bf16[1024,2560]{1,0:T(8,128)(2,1)}, f32[1024,1]{1,0:T(8,128)}) custom-call(s32[1]{0:T(128)} %bitcast.11.place, bf16[32,128,2560]{2,1,0:T(8,128)(2,1)} %bitcast.111, bf16[4096,2560]{1,0:T(8,128)(2,1)} %bitcast.115, bf16[16,64,128]{2,1,0:T(8,128)(2,1)} %fusion.41.p_ref, ...), custom_call_target="tpu_custom_call" | custom-call | tf_op jit(solution)/shard_map/dispatch/pallas_call | solution.py:1568
  355.7 83.6 %expert.1 = (bf16[1024,1536]{1,0:T(8,128)(2,1)}, bf16[1024,1536]{1,0:T(8,128)(2,1)}, bf16[1024,1536]{1,0:T(8,128)(2,1)}, f32[1024,1]{1,0:T(8,128)}, bf16[16,128,...) custom-call(s32[1]{0:T(128)} %bitcast.13.refs_0_.side_ref, bf16[1024,2560]{1,0:T(8,128)(2,1)} %get-tuple-element.71.refs_1_.refs_3_, ...), custom_call_target="tpu_custom_call" | custom-call | tf_op jit(solution)/shard_map/expert/pallas_call | solution.py:1717
  441.5 164.5 %row_grads.1 = (f32[128,2560]{1,0:T(8,128)}, f32[128,1280]{1,0:T(8,128)}, f32[16,8,128]{2,1,0:T(8,128)}, bf16[4096,1536]{1,0:T(8,128)(2,1)}, bf16[4096,1536]{1,0...) custom-call(bf16[4,2,2,128,2560]{4,3,2,1,0:T(8,128)(2,1)} %bitcast.137, ...), custom_call_target="tpu_custom_call" | custom-call | tf_op jit(solution)/shard_map/row_grads/pallas_call | solution.py:1145
  614.4 5.3 fusion.79
  619.6 5.3 select_convert_fusion.1
  626.2 27.1 %attend_back.1 = (f32[128,2560]{1,0:T(8,128)S(1)}, bf16[2048,1024]{1,0:T(8,128)(2,1)}) custom-call(s32[1]{0:T(128)} %bitcast.11.place, bf16[128,2560]{1,0:T(8,128)(2,1)S(1)} %copy-done.1, bf16[2048,1152]{1,0:T(8,128)(2,1)} %bitcast.121, bf16[2048,1152]{1,0:T(8,128)(2,1)} %bitcast.122, s32[2048,1]{1,0:T(8,128)S(1)} %copy-done, s32[1,128]{1,0:T(1,128)S(1)} %copy-done.3, ...), custom_call_target="tpu_custom_call" | custom-call | tf_op jit(solution)/shard_map/attend_back/pallas_call | solution.py:1522
  656.9 5.1 fusion.80
  662.1 6.1 convolution_convert_fusion.1
  668.2 184.0 %pair_grads.1 = (f32[128,1024]{1,0:T(8,128)}, f32[128,1280]{1,0:T(8,128)}, f32[80,2560]{1,0:T(8,128)}, bf16[2560,1536]{1,0:T(8,128)(2,1)}, bf16[2560,1536]{1,0:T(8,128)(2,1)}) custom-call(bf16[4,2,2,128,1024]{4,3,2,1,0:T(8,128)(2,1)} %bitcast.149, bf16[4,2,2,128,2560]{4,3,2,1,0:T(8,128)(2,1)} %bitcast.118, bf16[4,2,2,80,2560]{4,3,2,1,0:T(8,128)(2,1)} %bitcast.119, ...), custom_call_target="tpu_custom_call" | custom-call | tf_op jit(solution)/shard_map/pair_grads/pallas_call | solution.py:1145
  864.6 5.1 broadcast_select_fusion.1
  876.6 7.6 convolution_convert_fusion
  884.1 137.4 %sums.1 = (bf16[1,16,80,2560]{3,2,1,0:T(8,128)(2,1)}, f32[80,3584]{1,0:T(8,128)}, f32[80,256]{1,0:T(8,128)}, bf16[2560,1536]{1,0:T(8,128)(2,1)}, bf16[2560,1536]{1,0:T(8,128)(2,1)}, /*index=5*/bf16[1536,2560]{1,0:T(8,128)(2,1)}) custom-call(bf16[80,2560]{1,0:T(8,128)(2,1)} %convert_element_type.157.refs_0_, bf16[4,2,2,80,3584]{4,3,2,1,0:T(8,128)(2,1)} %bitcast.138, ...), custom_call_target="tpu_custom_call" | custom-call | tf_op jit(solution)/shard_map/sums/pallas_call | solution.py:1145
  1023.9 4.5 constant_dynamic-slice_fusion
  1028.4 4.9 constant_dynamic-slice_fusion.1
  1048.6 57.0 %down_grads.1 = f32[1536,2560]{1,0:T(8,128)} custom-call(bf16[4096,1536]{1,0:T(8,128)(2,1)} %get-tuple-element.105.refs_0_, bf16[4096,2560]{1,0:T(8,128)(2,1)} %bitcast.116), custom_call_target="tpu_custom_call" | custom-call | flops 32212254720 | bytes 75497472 | tf_op jit(solution)/shard_map/down_grads/pallas_call | solution.py:1338
  1105.6 4.3 fusion.33
  1109.9 10.6 join_columns.3
  1120.5 10.8 join_columns.2
  1131.2 7.8 add_bitcast_fusion
  1139.1 7.8 add_bitcast_fusion.1
  1146.9 6.5 add_bitcast_fusion.2
  1157.0 17.7 %widen.1 = (f32[1280,2560]{1,0:T(8,128)}, f32[1280,2560]{1,0:T(8,128)}, f32[1280,512]{1,0:T(8,128)}, f32[1280,512]{1,0:T(8,128)}, f32[1280,256]{1,0:T(8,128)}) custom-call(bf16[1280,2560]{1,0:T(8,128)(2,1)} %bitcast.145, bf16[1280,3840]{1,0:T(8,128)(2,1)} %all-gather.2.cloned.1.call-done.refs_1_), custom_call_target="tpu_custom_call" | custom-call | tf_op jit(solution)/shard_map/widen/pallas_call | solution.py:1627
  (247 shorter events, 104.9 us)
Async XLA Ops:
  7.2 1149.8 %all-gather.2.cloned.1.call-start = ((), (), s32[]{:S(2)}) async-start(), calls=%async_computation | async-start | bytes 10444800 | tf_op jit(solution)/shard_map/all_gather | solution.py:2074
  7.2 21.6 %collective-permute-start.3 = (bf16[1280,2560]{1,0:T(8,128)(2,1)}, bf16[1280,2560]{1,0:T(8,128)(2,1)}, u32[]{:S(2)}, u32[]{:S(2)}) collective-permute-start(bf16[1280,2560]{1,0:T(8,128)(2,1)} %param.20), channel_id=1, source_target_pairs={{1,0},{0,1},{3,2},{2,3},{5,4},{4,5},{7,6},{6,7},{9,8},{8,9},{11,10... | collective-permute-start | bytes 19660808 | tf_op jit(solution)/shard_map/ppermute | solution.py:1779
  10.0 8.5 collective-permute-start
  10.1 14.0 %collective-permute-start.1 = (bf16[1280,512]{1,0:T(8,128)(2,1)}, bf16[1280,512]{1,0:T(8,128)(2,1)}, u32[]{:S(2)}, u32[]{:S(2)}) collective-permute-start(bf16[1280,512]{1,0:T(8,128)(2,1)} %param.21), channel_id=1, source_target_pairs={{1,0},{0,1},{3,2},{2,3},{5,4},{4,5},{7,6},{6,7},{9,8},{8,9},{11,10... | collective-permute-start | bytes 3932168 | tf_op jit(solution)/shard_map/ppermute | solution.py:1779
  10.5 15.8 %collective-permute-start.2 = (bf16[1280,512]{1,0:T(8,128)(2,1)}, bf16[1280,512]{1,0:T(8,128)(2,1)}, u32[]{:S(2)}, u32[]{:S(2)}) collective-permute-start(bf16[1280,512]{1,0:T(8,128)(2,1)} %param.22), channel_id=1, source_target_pairs={{1,0},{0,1},{3,2},{2,3},{5,4},{4,5},{7,6},{6,7},{9,8},{8,9},{11,10... | collective-permute-start | bytes 3932168 | tf_op jit(solution)/shard_map/ppermute | solution.py:1779
  10.6 204.6 %collective-permute-start.4 = (bf16[1280,2560]{1,0:T(8,128)(2,1)}, bf16[1280,2560]{1,0:T(8,128)(2,1)}, u32[]{:S(2)}, u32[]{:S(2)}) collective-permute-start(bf16[1280,2560]{1,0:T(8,128)(2,1)} %param.23), channel_id=1, source_target_pairs={{1,0},{0,1},{3,2},{2,3},{5,4},{4,5},{7,6},{6,7},{9,8},{8,9},{11,10... | collective-permute-start | bytes 19660808 | tf_op jit(solution)/shard_map/ppermute | solution.py:1779
  21.2 199.4 %copy-start.19 = (bf16[16,2560]{1,0:T(8,128)(2,1)}, bf16[16,2560]{1,0:T(8,128)(2,1)S(1)}, u32[]{:S(2)}) copy-start(bf16[16,2560]{1,0:T(8,128)(2,1)S(1)} %pad_maximum_fusion.9.w_ref) | copy-start | bytes 245764
  206.7 455.4 %collective-permute-start.6 = (bf16[128,1280]{1,0:T(8,128)(2,1)}, bf16[128,1280]{1,0:T(8,128)(2,1)}, u32[]{:S(2)}, u32[]{:S(2)}) collective-permute-start(bf16[128,1280]{1,0:T(8,128)(2,1)} %get-tuple-element.185), channel_id=1, source_target_pairs={{1,0},{0,1},{3,2},{2,3},{5,4},{4,5},{7,6},{6,7},{9,8},{8,9},{11,10... | collective-permute-start | bytes 983048 | tf_op jit(solution)/shard_map/ppermute | solution.py:1779
  608.1 2.2 collective-permute-start.5
  614.2 47.9 %collective-permute-start.7 = (bf16[128,2560]{1,0:T(8,128)(2,1)}, bf16[128,2560]{1,0:T(8,128)(2,1)}, u32[]{:S(2)}, u32[]{:S(2)}) collective-permute-start(bf16[128,2560]{1,0:T(8,128)(2,1)} %fusion.77), channel_id=1, source_target_pairs={{1,0},{0,1},{3,2},{2,3},{5,4},{4,5},{7,6},{6,7},{9,8},{8,9},{11,10... | collective-permute-start | bytes 1966088 | tf_op jit(solution)/shard_map/ppermute | solution.py:1779
  871.0 2.4 collective-permute-start.10
  872.1 4.5 collective-permute-start.9
  872.6 4.0 collective-permute-start.8
  1023.8 16.9 %slice-start.4 = ((s8[7864320]{0:T(1024)(128)(4,1)}), s8[4194304]{0:T(1024)(128)(4,1)S(1)}, s32[]{:S(2)}) async-start(s8[7864320]{0:T(1024)(128)(4,1)} %bitcast.139), calls=%async_computation.5 | async-start | bytes 8388608
  1028.4 102.8 %collective-permute-start.16 = (bf16[768,2560]{1,0:T(8,128)(2,1)}, bf16[768,2560]{1,0:T(8,128)(2,1)}, u32[]{:S(2)}, u32[]{:S(2)}) collective-permute-start(bf16[768,2560]{1,0:T(8,128)(2,1)} %constant_dynamic-slice_fusion), channel_id=1, source_target_pairs={{1,0},{0,1},{3,2},{2,3},{5,4},{4,5},{7,6},{6,7},{9,8},{8,9},{11,10... | collective-permute-start | bytes 11796488 | tf_op jit(solution)/shard_map/ppermute | solution.py:1779
  1033.3 105.8 %collective-permute-start.15 = (bf16[1280,1536]{1,0:T(8,128)(2,1)}, bf16[1280,1536]{1,0:T(8,128)(2,1)}, u32[]{:S(2)}, u32[]{:S(2)}) collective-permute-start(bf16[1280,1536]{1,0:T(8,128)(2,1)} %constant_dynamic-slice_fusion.1), channel_id=1, source_target_pairs={{1,0},{0,1},{3,2},{2,3},{5,4},{4,5},{7,6},{6,7},{9,8},{8,9},{11,10... | collective-permute-start | bytes 11796488 | tf_op jit(solution)/shard_map/ppermute | solution.py:1779
  1035.6 74.3 %collective-permute-start.13 = (bf16[1280,1536]{1,0:T(8,128)(2,1)}, bf16[1280,1536]{1,0:T(8,128)(2,1)}, u32[]{:S(2)}, u32[]{:S(2)}) collective-permute-start(bf16[1280,1536]{1,0:T(8,128)(2,1)} %constant_dynamic-slice_fusion.3), channel_id=1, source_target_pairs={{1,0},{0,1},{3,2},{2,3},{5,4},{4,5},{7,6},{6,7},{9,8},{8,9},{11,10... | collective-permute-start | bytes 11796488 | tf_op jit(solution)/shard_map/ppermute | solution.py:1779
  1039.5 81.0 %collective-permute-start.12 = (bf16[1280,1536]{1,0:T(8,128)(2,1)}, bf16[1280,1536]{1,0:T(8,128)(2,1)}, u32[]{:S(2)}, u32[]{:S(2)}) collective-permute-start(bf16[1280,1536]{1,0:T(8,128)(2,1)} %constant_dynamic-slice_fusion.4), channel_id=1, source_target_pairs={{1,0},{0,1},{3,2},{2,3},{5,4},{4,5},{7,6},{6,7},{9,8},{8,9},{11,10... | collective-permute-start | bytes 11796488 | tf_op jit(solution)/shard_map/ppermute | solution.py:1779
  1044.1 4.3 collective-permute-start.11
  1046.9 58.7 %copy-start.7 = (f32[128,2560]{1,0:T(8,128)S(1)}, f32[128,2560]{1,0:T(8,128)}, u32[]{:S(2)}) copy-start(f32[128,2560]{1,0:T(8,128)} %copy-done.6) | copy-start | bytes 3932164
  1046.9 58.7 %copy-start.29 = (f32[2560]{0:T(1024)S(1)}, f32[2560]{0:T(1024)}, u32[]{:S(2)}) copy-start(f32[2560]{0:T(1024)} %copy-done.27) | copy-start | bytes 30724
  1046.9 58.7 %copy-start.35 = (f32[128]{0:T(128)S(1)}, f32[128]{0:T(128)}, u32[]{:S(2)}) copy-start(f32[128]{0:T(128)} %copy-done.33) | copy-start | bytes 1540
  1046.9 58.7 %copy-start.37 = (f32[128]{0:T(128)S(1)}, f32[128]{0:T(128)}, u32[]{:S(2)}) copy-start(f32[128]{0:T(128)} %copy-done.36) | copy-start | bytes 1540
  1048.4 98.5 %collective-permute-start.14 = (bf16[1280,1536]{1,0:T(8,128)(2,1)}, bf16[1280,1536]{1,0:T(8,128)(2,1)}, u32[]{:S(2)}, u32[]{:S(2)}) collective-permute-start(bf16[1280,1536]{1,0:T(8,128)(2,1)} %constant_dynamic-slice_fusion.2), channel_id=1, source_target_pairs={{1,0},{0,1},{3,2},{2,3},{5,4},{4,5},{7,6},{6,7},{9,8},{8,9},{11,10... | collective-permute-start | bytes 11796488 | tf_op jit(solution)/shard_map/ppermute | solution.py:1779
  (46 other events, 168.5 us)
Sparse Core Ops, SparseCore 0:
  1023.9 133.0 all-gather.1

commit v2 on v1

--- a/solution.py
+++ b/solution.py
@@ -518,17 +518,17 @@
             pltpu.VMEM((4, 2, rows, rest), LOW),
             pltpu.VMEM((4, rows, half), LOW),
             pltpu.VMEM((4, rows, rest), LOW),
-            pltpu.VMEM((4, rows, self.width), LOW),
             pltpu.VMEM((5, rows, self.width), LOW),
-            pltpu.SemaphoreType.DMA((14, 4)),
+            pltpu.SemaphoreType.DMA((18, 4)),
         ]
 
     def stages(
-        self, terms, out, own_a, own_b, got_a, got_b, more_a, more_b, plane_sum, line, sems
+        self, terms, out, own_a, own_b, got_a, got_b, more_a, more_b, line, sems
     ):
         rows, half, width = self.rows, self.half, self.width
         left, right = pl.ds(0, half), pl.ds(half, width - half)
         mine = pl.ds(0, width)
+        mine_left, mine_right = pl.ds(0, half), pl.ds(half, width - half)
         from_left = pl.ds(self.start, half)
         from_right = pl.ds(self.start + half, width - half)
 
@@ -582,18 +582,34 @@
 
         def upward(plane):
             me = lax.axis_index("expert")
-            return send(
-                plane_sum.at[plane], line.at[plane], sems.at[10, plane], sems.at[11, plane],
-                expert=me + 4,
+            return (
+                send(
+                    more_a.at[plane], line.at[plane, :, left],
+                    sems.at[10, plane], sems.at[11, plane], expert=me + 4,
+                ),
+                send(
+                    more_b.at[plane], line.at[plane, :, right],
+                    sems.at[12, plane], sems.at[13, plane], expert=me + 4,
+                ),
             )
 
         def downward(plane, receiver):
             me = lax.axis_index("expert")
             slot = plane + (4 - plane) * (1 - jnp.minimum(jnp.abs(plane - receiver), 1))
-            return send(
-                plane_sum.at[plane], line.at[slot], sems.at[12, plane], sems.at[13, plane],
-                expert=me - 4,
+            return (
+                send(
+                    more_a.at[plane], line.at[slot, :, left],
+                    sems.at[14, plane], sems.at[15, plane], expert=me - 4,
+                ),
+                send(
+                    more_b.at[plane], line.at[slot, :, right],
+                    sems.at[16, plane], sems.at[17, plane], expert=me - 4,
+                ),
             )
+
+        def arrived(copies):
+            for copy in copies:
+                copy.wait_recv()
 
         def begin(copies):
             for copy in copies:
@@ -624,10 +640,10 @@
                 copy.wait_recv()
 
             def add(span):
-                plane_sum[plane, span, left] = (
+                more_a[plane, span, :] = (
                     wide(own_a[slot, x, span, :]) + wide(more_a[plane, span, :])
                 ).astype(LOW)
-                plane_sum[plane, span, right] = (
+                more_b[plane, span, :] = (
                     wide(own_b[slot, y, span, :]) + wide(more_b[plane, span, :])
                 ).astype(LOW)
 
@@ -643,8 +659,11 @@
 
             def join(slot):
                 def add(span):
-                    plane_sum[plane, span, :] = (
-                        wide(plane_sum[plane, span, :]) + wide(line[slot, span, :])
+                    more_a[plane, span, :] = (
+                        wide(more_a[plane, span, :]) + wide(line[slot, span, left])
+                    ).astype(LOW)
+                    more_b[plane, span, :] = (
+                        wide(more_b[plane, span, :]) + wide(line[slot, span, right])
                     ).astype(LOW)
 
                 over_rows(add)
@@ -653,19 +672,19 @@
             def _():
                 @when(depth > 0)
                 def _():
-                    upward(plane).wait_recv()
+                    arrived(upward(plane))
                     join(plane)
 
-                upward(plane).start()
+                begin(upward(plane))
 
             @when(plane < depth)
             def _():
                 @when(depth < 3)
                 def _():
-                    downward(plane, depth).wait_recv()
+                    arrived(downward(plane, depth))
                     join(plane)
 
-                downward(plane, depth - 1).start()
+                begin(downward(plane, depth - 1))
 
         def start():
             for order in range(2):
@@ -675,13 +694,14 @@
             depth = coordinates()[2]
 
             def plain(span):
-                out[span, mine] = wide(plane_sum[depth, span, :])
+                out[span, mine_left] = wide(more_a[depth, span, :])
+                out[span, mine_right] = wide(more_b[depth, span, :])
 
             over_rows(plain)
 
             @when(depth > 0)
             def _():
-                upward(depth).wait_recv()
+                arrived(upward(depth))
 
                 def add(span):
                     out[span, mine] = out[span, mine] + wide(line[depth, span, :])
@@ -690,7 +710,7 @@
 
             @when(depth < 3)
             def _():
-                downward(depth, depth).wait_recv()
+                arrived(downward(depth, depth))
 
                 def add(span):
                     out[span, mine] = out[span, mine] + wide(line[4, span, :])
@@ -702,12 +722,14 @@
                     copy.wait_send()
 
                 @when(plane > depth)
-                def _():
-                    upward(plane).wait_send()
+                def _(plane=plane):
+                    for copy in upward(plane):
+                        copy.wait_send()
 
                 @when(plane < depth)
-                def _():
-                    downward(plane, depth - 1).wait_send()
+                def _(plane=plane):
+                    for copy in downward(plane, depth - 1):
+                        copy.wait_send()
 
         return [
             start,
@@ -1003,7 +1025,7 @@
     exchanges=(),
     works=(),
     lead=0,
-    vmem=60,
+    vmem=62,
 ):
     steps = max(1, sum(work.steps for work in works))
     any_spec = pl.BlockSpec(memory_space=pl.ANY)
@@ -1163,6 +1185,16 @@
     return 512 if size % 512 == 0 else size
 
 
+def over_columns(width, action):
+    size = 256 if width % 256 == 0 else 128
+
+    def step(index, carry):
+        action(pl.multiple_of(index * size, size), size)
+        return carry
+
+    lax.fori_loop(0, width // size, step, 0)
+
+
 def weight_parts(own, others):
     count, share, hidden = others.shape
     if share % 128:
@@ -1190,8 +1222,13 @@
     across = hidden // tile
 
     def body(step, ins, outs):
-        part = pl.ds(pl.multiple_of(lax.rem(step, across) * tile, tile), tile)
-        outs[0][...] = dot_nt(ins[0][...], ins[1][part, :]).astype(LOW)
+        base = lax.rem(step, across) * tile
+
+        def columns(start, size):
+            part = pl.ds(pl.multiple_of(base + start, size), size)
+            outs[0][:, pl.ds(start, size)] = dot_nt(ins[0][...], ins[1][part, :]).astype(LOW)
+
+        over_columns(tile, columns)
 
     return Work(
         total // 512 * across,
@@ -1207,30 +1244,38 @@
     count = len(gates)
     share, hidden = gates[0][1]
     tile = tile_of(hidden)
-    across, height = hidden // tile, 256
+    across, height = hidden // tile, 512
     each, holds = total // groups // height, height // tokens
 
     def body(step, ins, outs, own_gate, own_up):
-        part = pl.ds(pl.multiple_of(lax.rem(step, across) * tile, tile), tile)
+        base = pl.multiple_of(lax.rem(step, across) * tile, tile)
+        part = pl.ds(base, tile)
         side = lax.axis_index("fsdp")
         me = lax.axis_index("expert")
         weights = ins[2:]
-        pre_gate = pre_up = None
-        for which in range(count):
-            start = 0
-            if count > 1:
-                start = pl.multiple_of(lax.rem(side + which, count) * share, 128)
-            rows = ins[0][:, pl.ds(start, share)]
-            more_gate = dot_nn(rows, weights[which][:, part])
-            more_up = dot_nn(rows, weights[count + which][:, part])
-            pre_gate = more_gate if pre_gate is None else pre_gate + more_gate
-            pre_up = more_up if pre_up is None else pre_up + more_up
-        grad = ins[1][...].astype(jnp.float32)
-        sigma = 1.0 / (1.0 + jnp.exp(-pre_gate))
-        silu = pre_gate * sigma
-        outs[0][...] = (silu * pre_up).astype(LOW)
-        outs[1][...] = (grad * pre_up * (sigma * (1.0 + pre_gate * (1.0 - sigma)))).astype(LOW)
-        outs[2][...] = (grad * silu).astype(LOW)
+
+        def columns(start, size):
+            there, here = pl.ds(pl.multiple_of(base + start, size), size), pl.ds(start, size)
+            pre_gate = pre_up = None
+            for which in range(count):
+                first = 0
+                if count > 1:
+                    first = pl.multiple_of(lax.rem(side + which, count) * share, 128)
+                rows = ins[0][:, pl.ds(first, share)]
+                more_gate = dot_nn(rows, weights[which][:, there])
+                more_up = dot_nn(rows, weights[count + which][:, there])
+                pre_gate = more_gate if pre_gate is None else pre_gate + more_gate
+                pre_up = more_up if pre_up is None else pre_up + more_up
+            grad = ins[1][:, here].astype(jnp.float32)
+            sigma = 0.5 + 0.5 * jnp.tanh(0.5 * pre_gate)
+            silu = pre_gate * sigma
+            outs[0][:, here] = (silu * pre_up).astype(LOW)
+            outs[1][:, here] = (
+                grad * pre_up * (sigma * (1.0 + pre_gate * (1.0 - sigma)))
+            ).astype(LOW)
+            outs[2][:, here] = (grad * silu).astype(LOW)
+
+        over_columns(tile, columns)
         row_tile = step // across
 
         @pl.when(lax.rem(row_tile, each) == 0)
@@ -1271,33 +1316,44 @@
     )
 
 
-def turned_products(left, rights, dtype, depth):
+def turned_products(left, rights, depth):
     total, height = left.shape
     width = rights[0].shape[1]
     tall, tile = tile_of(height), tile_of(width)
     across, deep = width // tile, total // depth
+    chunk = 512 if depth % 512 == 0 else depth
 
     def body(step, ins, outs, turned, *sums):
         now = lax.rem(step, deep)
-        span = pl.ds(pl.multiple_of(now * depth, depth), depth)
 
         @pl.when(lax.rem(step // deep, across) == 0)
         def _():
-            turned[:, span] = ins[0][...].T
-
-        for which in range(len(rights)):
-            product = dot_nn(turned[:, span], ins[1 + which][...])
-            if deep == 1:
-                outs[which][...] = product.astype(dtype)
-            else:
-                sums[which][...] = jnp.where(now == 0, 0.0, sums[which][...]) + product
-
-        if deep > 1:
-
-            @pl.when(now == deep - 1)
-            def _():
-                for which in range(len(rights)):
-                    outs[which][...] = sums[which][...].astype(dtype)
+            def turn(index, carry):
+                start = pl.multiple_of(index * chunk, chunk)
+                there = pl.ds(pl.multiple_of(now * depth + start, chunk), chunk)
+                turned[:, there] = ins[0][pl.ds(start, chunk), :].T
+                return carry
+
+            lax.fori_loop(0, depth // chunk, turn, 0)
+
+        @pl.when(now == 0)
+        def _():
+            for ref in sums:
+                ref[...] = jnp.zeros(ref.shape, jnp.float32)
+
+        def add(index, carry):
+            start = pl.multiple_of(index * chunk, chunk)
+            there = pl.ds(pl.multiple_of(now * depth + start, chunk), chunk)
+            for ref, right in zip(sums, ins[1:]):
+                ref[...] += dot_nn(turned[:, there], right[pl.ds(start, chunk), :])
+            return carry
+
+        lax.fori_loop(0, depth // chunk, add, 0)
+
+        @pl.when(now == deep - 1)
+        def _():
+            for ref, out in zip(sums, outs):
+                out[...] = ref[...].astype(LOW)
 
     def left_spot(s):
         first = lax.rem(s // deep, across) == 0
@@ -1306,50 +1362,22 @@
     def right_spot(s):
         return lax.rem(s, deep), lax.rem(s // deep, across)
 
-    work = Work(
+    return Work(
         height // tall * across * deep,
         [(left, (depth, tall), left_spot)]
         + [(right, (depth, tile), right_spot) for right in rights],
         [
             (
                 (height, width),
-                dtype,
+                LOW,
                 (tall, tile),
                 lambda s: (s // (deep * across), lax.rem(s // deep, across)),
             )
         ]
         * len(rights),
         body,
-        [pltpu.VMEM((tall, total), left.dtype)]
-        + [pltpu.VMEM((tall, tile), jnp.float32)] * (len(rights) if deep > 1 else 0),
-    )
-    work.flops = 2 * total * height * width * len(rights)
-    work.traffic = 2 * total * (height + len(rights) * width * (height // tall))
-    return work
-
-
-def alone(name, work, vmem=60):
-    count = len(work.inputs)
-
-    def kernel(*refs):
-        outs = refs[count : count + len(work.outputs)]
-        work.body(pl.program_id(0), refs[:count], outs, *refs[count + len(work.outputs) :])
-
-    return pl.pallas_call(
-        kernel,
-        name=name,
-        grid=(work.steps,),
-        in_specs=[
-            pl.BlockSpec(shape, index_of) for _, shape, index_of in work.inputs
-        ],
-        out_specs=[pl.BlockSpec(shape, index_of) for _, _, shape, index_of in work.outputs],
-        out_shape=[jax.ShapeDtypeStruct(shape, dtype) for shape, dtype, _, _ in work.outputs],
-        scratch_shapes=work.scratch,
-        compiler_params=pltpu.CompilerParams(vmem_limit_bytes=vmem * 1024 * 1024),
-        cost_estimate=pl.CostEstimate(
-            flops=work.flops, bytes_accessed=work.traffic, transcendentals=0
-        ),
-    )(*[array for array, _, _ in work.inputs])
+        [pltpu.VMEM((tall, total), LOW)] + [pltpu.VMEM((tall, tile), jnp.float32)] * len(rights),
+    )
 
 
 CHUNK = 256
@@ -1541,10 +1569,22 @@
     )(place, queries, pairs, pairs, key_labels, query_labels, grads, log_total)
 
 
-def dispatch_kernel(place, n_ref, u_ref, p_ref, m_ref, w_ref, rows_ref, up_ref, pair_ref, g_ref):
-    rows = n_ref[0]
-    pick = p_ref[0]
-    logits = dot_nt(w_ref[...], rows)
+def dispatch_kernel(
+    place, n_ref, u_ref, p_ref, m_ref, w_ref, rows_ref, up_ref, pair_ref, g_ref, pick_ref
+):
+    blocks, tokens, model = n_ref.shape
+    capacity = p_ref.shape[1]
+
+    @pl.when(pl.program_id(0) == 0)
+    def _():
+        pick_ref[...] = jnp.zeros(pick_ref.shape, LOW)
+
+    for block in range(blocks):
+        pick_ref[
+            block * capacity : (block + 1) * capacity, block * tokens : (block + 1) * tokens
+        ] = p_ref[block]
+    pick = pick_ref[...]
+    logits = dot_nt(w_ref[...], n_ref[...].reshape(blocks * tokens, model))
     chosen = m_ref[...] > 0.5
     top = jnp.max(jnp.where(chosen, logits, masked_score), axis=0, keepdims=True)
     power = jnp.where(chosen, jnp.exp(jnp.where(chosen, logits - top, 0.0)), 0.0)
@@ -1553,33 +1593,40 @@
         power, axis=0, keepdims=True
     )
     slot_gate = jnp.sum(pick.astype(jnp.float32) * gate, axis=1, keepdims=True)
-    rows_ref[...] = dot_nn(pick, rows).astype(LOW)
-    ups = dot_nn(pick, u_ref[...])
-    up_ref[...] = ups.astype(LOW)
-    pair_ref[...] = (slot_gate * ups).astype(LOW)
     g_ref[...] = slot_gate
+    tile = tile_of(model)
+    for index in range(model // tile):
+        span = pl.ds(index * tile, tile)
+        rows = n_ref[:, :, span].reshape(blocks * tokens, tile)
+        rows_ref[:, span] = dot_nn(pick, rows).astype(LOW)
+        ups = dot_nn(pick, u_ref[:, span])
+        up_ref[:, span] = ups.astype(LOW)
+        pair_ref[:, span] = (slot_gate * ups).astype(LOW)
 
 
 def dispatch(place, normed, upstream, pick, chosen, w_router):
     blocks, capacity, tokens = pick.shape
     model = upstream.shape[1]
     experts = w_router.shape[0]
-    wide = pl.BlockSpec((capacity, model), lambda b: (b, 0))
+    group = 4
+    wide_spec = pl.BlockSpec((group * capacity, model), lambda b: (b, 0))
     return pl.pallas_call(
         dispatch_kernel,
         name="dispatch",
-        grid=(blocks,),
+        grid=(blocks // group,),
         in_specs=[
             pl.BlockSpec(memory_space=pltpu.SMEM),
-            pl.BlockSpec((1, tokens, model), lambda b: (b, 0, 0)),
-            pl.BlockSpec((tokens, model), lambda b: (b, 0)),
-            pl.BlockSpec((1, capacity, tokens), lambda b: (b, 0, 0)),
-            pl.BlockSpec((experts, tokens), lambda b: (0, b)),
+            pl.BlockSpec((group, tokens, model), lambda b: (b, 0, 0)),
+            pl.BlockSpec((group * tokens, model), lambda b: (b, 0)),
+            pl.BlockSpec((group, capacity, tokens), lambda b: (b, 0, 0)),
+            pl.BlockSpec((experts, group * tokens), lambda b: (0, b)),
             pl.BlockSpec((experts, model), lambda b: (0, 0)),
         ],
-        out_specs=[wide, wide, wide, pl.BlockSpec((capacity, 1), lambda b: (b, 0))],
+        out_specs=[wide_spec] * 3 + [pl.BlockSpec((group * capacity, 1), lambda b: (b, 0))],
         out_shape=[jax.ShapeDtypeStruct((blocks * capacity, model), LOW)] * 3
         + [jax.ShapeDtypeStruct((blocks * capacity, 1), jnp.float32)],
+        scratch_shapes=[pltpu.VMEM((group * capacity, group * tokens), LOW)],
+        compiler_params=pltpu.CompilerParams(vmem_limit_bytes=50 * 1024 * 1024),
     )(place, normed, upstream, pick, chosen, w_router)
 
 
@@ -1649,53 +1696,63 @@
             return pl.ds(0, size)
         return pl.ds(pl.multiple_of(lax.rem(side[0] + which, count) * size, 128), size)
 
+    def offset(which, size, start):
+        if count == 1:
+            return start
+        return pl.multiple_of(lax.rem(side[0] + which, count) * size + start, 128)
+
     for which in range(count):
-        span = place(which, units)
-        pre_gate = pre_up = None
-        for part in range(count):
-            rows = rows_ref[:, place(part, share)]
-            more_gate = dot_nn(rows, w_gate[part][:, span])
-            more_up = dot_nn(rows, w_up[part][:, span])
-            pre_gate = more_gate if pre_gate is None else pre_gate + more_gate
-            pre_up = more_up if pre_up is None else pre_up + more_up
-        d_act = dot_nt(pair_ref[...], w_down[which][...])
-        sigma = 1.0 / (1.0 + jnp.exp(-pre_gate))
-        silu = pre_gate * sigma
-        act_ref[:, span] = (silu * pre_up).astype(LOW)
-        dg_ref[:, span] = (
-            d_act * pre_up * (sigma * (1.0 + pre_gate * (1.0 - sigma)))
-        ).astype(LOW)
-        du_ref[:, span] = (d_act * silu).astype(LOW)
+
+        def hidden_columns(start, size, which=which):
+            span = pl.ds(offset(which, units, start), size)
+            pre_gate = pre_up = None
+            for part in range(count):
+                rows = rows_ref[:, place(part, share)]
+                more_gate = dot_nn(rows, w_gate[part][:, span])
+                more_up = dot_nn(rows, w_up[part][:, span])
+                pre_gate = more_gate if pre_gate is None else pre_gate + more_gate
+                pre_up = more_up if pre_up is None else pre_up + more_up
+            d_act = dot_nt(pair_ref[...], w_down[which][pl.ds(start, size), :])
+            sigma = 0.5 + 0.5 * jnp.tanh(0.5 * pre_gate)
+            silu = pre_gate * sigma
+            act_ref[:, span] = (silu * pre_up).astype(LOW)
+            dg_ref[:, span] = (
+                d_act * pre_up * (sigma * (1.0 + pre_gate * (1.0 - sigma)))
+            ).astype(LOW)
+            du_ref[:, span] = (d_act * silu).astype(LOW)
+
+        over_columns(units, hidden_columns)
 
     def returned(target, values, span):
         for block in range(blocks):
             mine = values[block * capacity : (block + 1) * capacity]
             target[block, :, span] = dot_nn(back_ref[block], mine).astype(LOW)
 
-    d_gate = jnp.zeros(d_gate_ref.shape, jnp.float32)
-    tile = tile_of(model)
-    for index in range(model // tile):
-        span = pl.ds(index * tile, tile)
+    d_gate_ref[...] = jnp.zeros(d_gate_ref.shape, jnp.float32)
+
+    def model_columns(start, size):
+        span = pl.ds(start, size)
         produced = None
         for part in range(count):
             more = dot_nn(act_ref[:, place(part, units)], w_down[part][:, span])
             produced = more if produced is None else produced + more
         produced = produced.astype(LOW).astype(jnp.float32)
-        d_gate += jnp.sum(produced * up_ref[:, span].astype(jnp.float32), axis=1, keepdims=True)
+        d_gate_ref[...] += jnp.sum(
+            produced * up_ref[:, span].astype(jnp.float32), axis=1, keepdims=True
+        )
         returned(out_ref, (gate_ref[...] * produced).astype(LOW), span)
-    d_gate_ref[...] = d_gate
+
+    over_columns(model, model_columns)
     for part in range(count):
-        pieces = 2 if share % 256 == 0 else 1
-        for piece in range(pieces):
-            width = share // pieces
-            rows = pl.ds(piece * width, width)
+
+        def row_columns(start, size, part=part):
+            rows = pl.ds(start, size)
             d_rows = dot_nt(dg_ref[...], w_gate[part][rows, :]) + dot_nt(
                 du_ref[...], w_up[part][rows, :]
             )
-            start = piece * width
-            if count > 1:
-                start = pl.multiple_of(lax.rem(side[0] + part, count) * share + start, 128)
-            returned(term_ref, d_rows.astype(LOW), pl.ds(start, width))
+            returned(term_ref, d_rows.astype(LOW), pl.ds(offset(part, share, start), size))
+
+        over_columns(share, row_columns)
 
 
 def run_expert(side, rows_in, rows_up, d_pair, slot_gate, pick, gates, ups, downs):
@@ -2032,7 +2089,9 @@
             (out_terms, half_model, half_model),
             (blocks(term_o), 0, model),
         ],
-        works=[turned_products(normed_each, [shared_d_gate, shared_d_up], LOW, length)],
+        works=[
+            turned_products(normed_each, [shared_d_gate, shared_d_up], length)
+        ],
     )
     d_pairs = d_pairs.reshape(tokens, KEY_HEADS, 2, HEAD_DIM)
     d_query_low = rotate(
@@ -2065,8 +2124,8 @@
         gathers=[(1, mine_o.astype(LOW))],
         scatters=[(blocks(term_pre), 0, term_pre.shape[1]), (blocks(small_term), 0, 256)],
         works=[
-            turned_products(rows_in, [d_gate_pre, d_up_pre], LOW, rows_in.shape[0]),
-            turned_products(expert_act, [d_pair], LOW, rows_in.shape[0]),
+            turned_products(rows_in, [d_gate_pre, d_up_pre], rows_in.shape[0]),
+            turned_products(expert_act, [d_pair], rows_in.shape[0]),
         ],
     )
     all_o = all_o.reshape(experts, -1, model)[:, : share // experts].reshape(share, model)
@@ -2076,7 +2135,6 @@
     mine_pre, shared_act, term_eg, term_eu, term_ed, grad_sg, grad_su = lax.optimization_barrier(
         (mine_pre, shared_act, term_eg, term_eu, term_ed, grad_sg, grad_su)
     )
-
     own_act = lax.dynamic_slice_in_dim(
         shared_act.reshape(groups, length, -1), place * tokens, tokens, 1
     ).reshape(groups * tokens, -1)
@@ -2093,9 +2151,7 @@
         return total
 
     grad_eg, grad_eu, grad_ed = summed(term_eg), summed(term_eu), summed(term_ed)
-    (grad_sd,) = alone(
-        "down_grads", turned_products(shared_act, [upstream_each], jnp.float32, length)
-    )
+    grad_sd = dot_tn(shared_act, upstream_each)
     grad_sg, grad_su = [
         join_columns(here_side, groups, term, scattered(term, 0)[1:])
         for term in (grad_sg, grad_su)

time: 1200 us -> 1210 us (level)
  matrix products: 66.8 us -> 108 us
  Pallas kernels: 995 us -> 961 us
  waiting for transfers between devices: 6.21 us -> 22.2 us
    pallas_call x2 -> x1, Pallas kernels: 77.6 us -> 16.3 us  [dispatch(): pl.pallas_call(dispatch_kernel, name='dispatch', grid=(blocks // group,),...]
    dot_general x2 -> x3, matrix products: 13.6 us -> 51.1 us  [dot_tn(): lax.dot_general(left, right, (((0,), (0,)), ((), ())), preferred_element_...]
    pallas_call x1, Pallas kernels: 83.6 us -> 103 us  [run_expert(): pl.pallas_call(kernel, name='expert', grid_spec=pltpu.PrefetchScalarGridS...]
    all_gather x1, waiting for transfers between devices: 3.64 us -> 17.7 us  [local(): all_pre = lax.all_gather(mine_pre, 'expert', axis=0, tiled=True)]
  transfers between devices with their start and end apart: 18 -> 18, of which waited for: 3 -> 5; matrix products, arithmetic and copies ran while one was open for 10% -> 13% of each run, Pallas kernels for 55% -> 51%
where the time goes in v2:
time: 1210 us; the launch traced here: 1200 us
  Pallas kernels  961 us (79%)
  matrix products  108 us (9%)
  local copies, waits for them, and re-layouts  49.4 us (4%)
  other arithmetic  44 us (4%)
  waiting for transfers between devices  22.2 us (2%)
  between operations  15.6 us (1%)
    pallas_call x5, Pallas kernels, carry(): pl.pallas_call(kernel, name=name, grid=(steps,), out_shape=out_shapes, in...  775 us
    pallas_call x1, Pallas kernels, run_expert(): pl.pallas_call(kernel, name='expert', grid_spec=pltpu.PrefetchScalarGridS...  103 us
    dot_general x3, matrix products, dot_tn(): lax.dot_general(left, right, (((0,), (0,)), ((), ())), preferred_element_...  51.1 us
    dot_general x10, matrix products, dot_nt(): lax.dot_general(left, right, (((1,), (1,)), ((), ())), preferred_element_...  28.2 us
    pallas_call x1, Pallas kernels, attend_back(): pl.pallas_call(attend_back_kernel, name='attend_back', grid=(KEY_HEADS,),...  27.2 us
    dot_general x9, matrix products, dot_nn(): return jnp.dot(left, right, preferred_element_type=jnp.float32)  26 us
  transfers between devices with their start and end apart: 18, of which 5 were waited for; matrix products, arithmetic and copies ran while one was open for 13% of the time, Pallas kernels for 51%

profile of v2, /device:TPU:0, one launch (start us, length us, event | category | flops | bytes accessed | tf_op | source)
XLA Modules:
  0.0 1203.7 jit_solution(15960099114039554469)
XLA Ops:
  35.0 167.3 %attend.1 = (bf16[1,16,128,1152]{3,2,1,0:T(8,128)(2,1)}, bf16[2,16,128,2560]{3,2,1,0:T(8,128)(2,1)}, bf16[1,1280,1536]{2,1,0:T(8,128)(2,1)}, bf16[1,1280,1536]{2...) custom-call(bf16[128,1152]{1,0:T(8,128)(2,1)} %pad_maximum_fusion.6., ...), custom_call_target="tpu_custom_call" | custom-call | tf_op jit(solution)/shard_map/attend/pallas_call | solution.py:1167
  218.3 114.9 %rows.1 = (bf16[2,16,128,2560]{3,2,1,0:T(8,128)(2,1)}, bf16[4096,1536]{1,0:T(8,128)(2,1)}) custom-call(bf16[128,2560]{1,0:T(8,128)(2,1)} %copy-done.14, bf16[4096,2560]{1,0:T(8,128)(2,1)} %bitcast.116, bf16[1536,2560]{1,0:T(8,128)(2,1)} %refs_2_.3), custom_call_target="tpu_custom_call" | custom-call | tf_op jit(solution)/shard_map/rows/pallas_call | solution.py:1167
  333.3 16.3 %dispatch.1 = (bf16[1024,2560]{1,0:T(8,128)(2,1)}, bf16[1024,2560]{1,0:T(8,128)(2,1)}, bf16[1024,2560]{1,0:T(8,128)(2,1)}, f32[1024,1]{1,0:T(8,128)S(1)}) custom-call(s32[1]{0:T(128)} %bitcast.11.place, bf16[32,128,2560]{2,1,0:T(8,128)(2,1)} %bitcast.113, bf16[4096,2560]{1,0:T(8,128)(2,1)} %bitcast.117, bf16[16,64,128]{2,1,0:T(8,128)(2,1)S(1)} %fusion.41.p_ref, ...), custom_call_target="tpu_custom_call" | custom-call | tf_op jit(solution)/shard_map/dispatch/pallas_call | solution.py:1613
  350.3 103.3 %expert.1 = (bf16[1024,1536]{1,0:T(8,128)(2,1)}, bf16[1024,1536]{1,0:T(8,128)(2,1)}, bf16[1024,1536]{1,0:T(8,128)(2,1)}, f32[1024,1]{1,0:T(8,128)}, bf16[16,128,...) custom-call(s32[1]{0:T(128)} %bitcast.13.refs_0_.side_ref, bf16[1024,2560]{1,0:T(8,128)(2,1)} %get-tuple-element.71.refs_1_.refs_3_, ...), custom_call_target="tpu_custom_call" | custom-call | tf_op jit(solution)/shard_map/expert/pallas_call | solution.py:1774
  455.8 169.0 %row_grads.1 = (f32[128,2560]{1,0:T(8,128)}, f32[128,1280]{1,0:T(8,128)}, f32[16,8,128]{2,1,0:T(8,128)}, bf16[4096,1536]{1,0:T(8,128)(2,1)}, bf16[4096,1536]{1,0...) custom-call(bf16[4,2,2,128,2560]{4,3,2,1,0:T(8,128)(2,1)} %bitcast.141, ...), custom_call_target="tpu_custom_call" | custom-call | tf_op jit(solution)/shard_map/row_grads/pallas_call | solution.py:1167
  632.9 5.0 fusion.79
  638.0 5.1 select_convert_fusion.1
  644.3 27.2 %attend_back.1 = (f32[128,2560]{1,0:T(8,128)S(1)}, bf16[2048,1024]{1,0:T(8,128)(2,1)}) custom-call(s32[1]{0:T(128)} %bitcast.11.place, bf16[128,2560]{1,0:T(8,128)(2,1)S(1)} %copy-done.1, bf16[2048,1152]{1,0:T(8,128)(2,1)} %bitcast.125, bf16[2048,1152]{1,0:T(8,128)(2,1)} %bitcast.126, s32[2048,1]{1,0:T(8,128)S(1)} %copy-done, s32[1,128]{1,0:T(1,128)S(1)} %copy-done.4, ...), custom_call_target="tpu_custom_call" | custom-call | tf_op jit(solution)/shard_map/attend_back/pallas_call | solution.py:1550
  674.5 6.3 fusion.80
  680.8 5.9 convolution_convert_fusion.1
  686.7 173.6 %pair_grads.1 = (f32[128,1024]{1,0:T(8,128)}, f32[128,1280]{1,0:T(8,128)}, f32[80,2560]{1,0:T(8,128)}, bf16[2560,1536]{1,0:T(8,128)(2,1)}, bf16[2560,1536]{1,0:T(8,128)(2,1)}) custom-call(bf16[4,2,2,128,1024]{4,3,2,1,0:T(8,128)(2,1)} %bitcast.151, bf16[4,2,2,128,2560]{4,3,2,1,0:T(8,128)(2,1)} %bitcast.122, bf16[4,2,2,80,2560]{4,3,2,1,0:T(8,128)(2,1)} %bitcast.123, ...), custom_call_target="tpu_custom_call" | custom-call | tf_op jit(solution)/shard_map/pair_grads/pallas_call | solution.py:1167
  871.9 5.2 broadcast_select_fusion.1
  882.8 7.7 convolution_convert_fusion
  890.4 149.8 %sums.1 = (bf16[1,16,80,2560]{3,2,1,0:T(8,128)(2,1)}, f32[80,3584]{1,0:T(8,128)}, f32[80,256]{1,0:T(8,128)}, bf16[2560,1536]{1,0:T(8,128)(2,1)}, bf16[2560,1536]{1,0:T(8,128)(2,1)}, /*index=5*/bf16[1536,2560]{1,0:T(8,128)(2,1)}) custom-call(bf16[80,2560]{1,0:T(8,128)(2,1)} %convert_element_type.157.refs_0_, bf16[4,2,2,80,3584]{4,3,2,1,0:T(8,128)(2,1)} %bitcast.142, ...), custom_call_target="tpu_custom_call" | custom-call | tf_op jit(solution)/shard_map/sums/pallas_call | solution.py:1167
  1047.1 4.5 constant_dynamic-slice_fusion.1
  1060.1 6.2 convolution_convert_fusion.2
  1072.2 37.6 %fusion.83 = f32[1536,2560]{1,0:T(8,128)} fusion(bf16[4096,1536]{1,0:T(8,128)(2,1)} %get-tuple-element.105, bf16[4096,2560]{1,0:T(8,128)(2,1)S(1)} %bitcast.120), kind=kOutput, calls=%fused_computation.177 | convolution fusion | flops 32212254720 | bytes 49283072 | tf_op jit(solution)/shard_map/dot_general | solution.py:31
  1113.9 10.8 join_columns.3
  1124.7 10.5 join_columns.2
  1135.2 7.9 add_bitcast_fusion
  1143.1 7.8 add_bitcast_fusion.1
  1151.0 6.5 add_bitcast_fusion.2
  1157.4 17.7 %all-gather.2.cloned.1.call-done.refs_1_ = bf16[1280,3840]{1,0:T(8,128)(2,1)} async-done(((bf16[80,3840]{1,0:T(8,128)(2,1)}), bf16[1280,3840]{1,0:T(8,128)(2,1)}) %all-gather.2.cloned.1.call-update) | async-done | bytes 9830416 | tf_op jit(solution)/shard_map/all_gather | solution.py:2133
  1175.1 17.9 %widen.1 = (f32[1280,2560]{1,0:T(8,128)}, f32[1280,2560]{1,0:T(8,128)}, f32[1280,512]{1,0:T(8,128)}, f32[1280,512]{1,0:T(8,128)}, f32[1280,256]{1,0:T(8,128)}) custom-call(bf16[1280,2560]{1,0:T(8,128)(2,1)} %bitcast.147, bf16[1280,3840]{1,0:T(8,128)(2,1)} %all-gather.2.cloned.1.call-done.refs_1_), custom_call_target="tpu_custom_call" | custom-call | tf_op jit(solution)/shard_map/widen/pallas_call | solution.py:1674
  (268 shorter events, 104.2 us)
Async XLA Ops:
  7.2 1167.9 %all-gather.2.cloned.1.call-start = ((), (), s32[]{:S(2)}) async-start(), calls=%async_computation | async-start | bytes 10444800 | tf_op jit(solution)/shard_map/all_gather | solution.py:2133
  7.2 22.1 %collective-permute-start.3 = (bf16[1280,2560]{1,0:T(8,128)(2,1)}, bf16[1280,2560]{1,0:T(8,128)(2,1)}, u32[]{:S(2)}, u32[]{:S(2)}) collective-permute-start(bf16[1280,2560]{1,0:T(8,128)(2,1)} %param.20), channel_id=1, source_target_pairs={{1,0},{0,1},{3,2},{2,3},{5,4},{4,5},{7,6},{6,7},{9,8},{8,9},{11,10... | collective-permute-start | bytes 19660808 | tf_op jit(solution)/shard_map/ppermute | solution.py:1836
  10.0 9.1 collective-permute-start
  10.1 14.5 %collective-permute-start.1 = (bf16[1280,512]{1,0:T(8,128)(2,1)}, bf16[1280,512]{1,0:T(8,128)(2,1)}, u32[]{:S(2)}, u32[]{:S(2)}) collective-permute-start(bf16[1280,512]{1,0:T(8,128)(2,1)} %param.21), channel_id=1, source_target_pairs={{1,0},{0,1},{3,2},{2,3},{5,4},{4,5},{7,6},{6,7},{9,8},{8,9},{11,10... | collective-permute-start | bytes 3932168 | tf_op jit(solution)/shard_map/ppermute | solution.py:1836
  10.5 16.3 %collective-permute-start.2 = (bf16[1280,512]{1,0:T(8,128)(2,1)}, bf16[1280,512]{1,0:T(8,128)(2,1)}, u32[]{:S(2)}, u32[]{:S(2)}) collective-permute-start(bf16[1280,512]{1,0:T(8,128)(2,1)} %param.22), channel_id=1, source_target_pairs={{1,0},{0,1},{3,2},{2,3},{5,4},{4,5},{7,6},{6,7},{9,8},{8,9},{11,10... | collective-permute-start | bytes 3932168 | tf_op jit(solution)/shard_map/ppermute | solution.py:1836
  10.6 201.6 %collective-permute-start.4 = (bf16[1280,2560]{1,0:T(8,128)(2,1)}, bf16[1280,2560]{1,0:T(8,128)(2,1)}, u32[]{:S(2)}, u32[]{:S(2)}) collective-permute-start(bf16[1280,2560]{1,0:T(8,128)(2,1)} %param.23), channel_id=1, source_target_pairs={{1,0},{0,1},{3,2},{2,3},{5,4},{4,5},{7,6},{6,7},{9,8},{8,9},{11,10... | collective-permute-start | bytes 19660808 | tf_op jit(solution)/shard_map/ppermute | solution.py:1836
  204.3 476.5 %collective-permute-start.6 = (bf16[128,1280]{1,0:T(8,128)(2,1)}, bf16[128,1280]{1,0:T(8,128)(2,1)}, u32[]{:S(2)}, u32[]{:S(2)}) collective-permute-start(bf16[128,1280]{1,0:T(8,128)(2,1)} %get-tuple-element.185), channel_id=1, source_target_pairs={{1,0},{0,1},{3,2},{2,3},{5,4},{4,5},{7,6},{6,7},{9,8},{8,9},{11,10... | collective-permute-start | bytes 983048 | tf_op jit(solution)/shard_map/ppermute | solution.py:1836
  627.0 2.2 collective-permute-start.5
  632.8 48.0 %collective-permute-start.7 = (bf16[128,2560]{1,0:T(8,128)(2,1)S(1)}, bf16[128,2560]{1,0:T(8,128)(2,1)}, u32[]{:S(2)}, u32[]{:S(2)}) collective-permute-start(bf16[128,2560]{1,0:T(8,128)(2,1)S(1)} %fusion.77), channel_id=1, source_target_pairs={{1,0},{0,1},{3,2},{2,3},{5,4},{4,5},{7,6},{6,7},{9,8},{8,9},{11,10... | collective-permute-start | bytes 1966088 | tf_op jit(solution)/shard_map/ppermute | solution.py:1836
  878.3 2.4 collective-permute-start.10
  879.4 3.4 collective-permute-start.9
  879.9 2.6 collective-permute-start.8
  1047.0 88.2 %collective-permute-start.16 = (bf16[768,2560]{1,0:T(8,128)(2,1)}, bf16[768,2560]{1,0:T(8,128)(2,1)}, u32[]{:S(2)}, u32[]{:S(2)}) collective-permute-start(bf16[768,2560]{1,0:T(8,128)(2,1)} %constant_dynamic-slice_fusion), channel_id=1, source_target_pairs={{1,0},{0,1},{3,2},{2,3},{5,4},{4,5},{7,6},{6,7},{9,8},{8,9},{11,10... | collective-permute-start | bytes 11796488 | tf_op jit(solution)/shard_map/ppermute | solution.py:1836
  1051.6 91.5 %collective-permute-start.15 = (bf16[1280,1536]{1,0:T(8,128)(2,1)}, bf16[1280,1536]{1,0:T(8,128)(2,1)}, u32[]{:S(2)}, u32[]{:S(2)}) collective-permute-start(bf16[1280,1536]{1,0:T(8,128)(2,1)} %constant_dynamic-slice_fusion.1), channel_id=1, source_target_pairs={{1,0},{0,1},{3,2},{2,3},{5,4},{4,5},{7,6},{6,7},{9,8},{8,9},{11,10... | collective-permute-start | bytes 11796488 | tf_op jit(solution)/shard_map/ppermute | solution.py:1836
  1054.3 96.7 %collective-permute-start.14 = (bf16[1280,1536]{1,0:T(8,128)(2,1)}, bf16[1280,1536]{1,0:T(8,128)(2,1)}, u32[]{:S(2)}, u32[]{:S(2)}) collective-permute-start(bf16[1280,1536]{1,0:T(8,128)(2,1)} %constant_dynamic-slice_fusion.2), channel_id=1, source_target_pairs={{1,0},{0,1},{3,2},{2,3},{5,4},{4,5},{7,6},{6,7},{9,8},{8,9},{11,10... | collective-permute-start | bytes 11796488 | tf_op jit(solution)/shard_map/ppermute | solution.py:1836
  1055.6 16.5 %slice-start = ((s8[20971520]{0:T(1024)(128)(4,1)}), s8[4194304]{0:T(1024)(128)(4,1)S(1)}, s32[]{:S(2)}) async-start(s8[20971520]{0:T(1024)(128)(4,1)} %bitcast.118), calls=%async_computation.1 | async-start | bytes 8388608
  1057.9 56.0 %collective-permute-start.13 = (bf16[1280,1536]{1,0:T(8,128)(2,1)}, bf16[1280,1536]{1,0:T(8,128)(2,1)}, u32[]{:S(2)}, u32[]{:S(2)}) collective-permute-start(bf16[1280,1536]{1,0:T(8,128)(2,1)} %constant_dynamic-slice_fusion.3), channel_id=1, source_target_pairs={{1,0},{0,1},{3,2},{2,3},{5,4},{4,5},{7,6},{6,7},{9,8},{8,9},{11,10... | collective-permute-start | bytes 11796488 | tf_op jit(solution)/shard_map/ppermute | solution.py:1836
  1067.3 4.7 collective-permute-start.11
  1069.9 39.8 %copy-start.9 = (bf16[1,128,2560]{2,1,0:T(8,128)(2,1)S(1)}, bf16[1,128,2560]{2,1,0:T(8,128)(2,1)}, u32[]{:S(2)}) copy-start(bf16[1,128,2560]{2,1,0:T(8,128)(2,1)} %param.18) | copy-start | bytes 1966084
  1069.9 39.8 %copy-start.11 = (f32[128,2560]{1,0:T(8,128)S(1)}, f32[128,2560]{1,0:T(8,128)}, u32[]{:S(2)}) copy-start(f32[128,2560]{1,0:T(8,128)} %copy-done.10) | copy-start | bytes 3932164
  1069.9 39.8 %copy-start.19 = (f32[128,1280]{1,0:T(8,128)S(1)}, f32[128,1280]{1,0:T(8,128)}, u32[]{:S(2)}) copy-start(f32[128,1280]{1,0:T(8,128)} %copy-done.18) | copy-start | bytes 1966084
  1069.9 39.8 %copy-start.41 = (f32[128]{0:T(128)S(1)}, f32[128]{0:T(128)}, u32[]{:S(2)}) copy-start(f32[128]{0:T(128)} %copy-done.39) | copy-start | bytes 1540
  1072.0 52.7 %collective-permute-start.12 = (bf16[1280,1536]{1,0:T(8,128)(2,1)}, bf16[1280,1536]{1,0:T(8,128)(2,1)}, u32[]{:S(2)}, u32[]{:S(2)}) collective-permute-start(bf16[1280,1536]{1,0:T(8,128)(2,1)} %constant_dynamic-slice_fusion.4), channel_id=1, source_target_pairs={{1,0},{0,1},{3,2},{2,3},{5,4},{4,5},{7,6},{6,7},{9,8},{8,9},{11,10... | collective-permute-start | bytes 11796488 | tf_op jit(solution)/shard_map/ppermute | solution.py:1836
  1135.2 15.7 %slice-start.11 = ((s8[7864320]{0:T(1024)(128)(4,1)}), s8[4194304]{0:T(1024)(128)(4,1)S(1)}, s32[]{:S(2)}) async-start(s8[7864320]{0:T(1024)(128)(4,1)} %bitcast.145), calls=%async_computation.12 | async-start | bytes 8388608
  (56 other events, 228.0 us)
Sparse Core Ops, SparseCore 0:
  1042.7 132.4 all-gather.1

commit v3 on v1

--- a/solution.py
+++ b/solution.py
@@ -518,17 +518,17 @@
             pltpu.VMEM((4, 2, rows, rest), LOW),
             pltpu.VMEM((4, rows, half), LOW),
             pltpu.VMEM((4, rows, rest), LOW),
-            pltpu.VMEM((4, rows, self.width), LOW),
             pltpu.VMEM((5, rows, self.width), LOW),
-            pltpu.SemaphoreType.DMA((14, 4)),
+            pltpu.SemaphoreType.DMA((18, 4)),
         ]
 
     def stages(
-        self, terms, out, own_a, own_b, got_a, got_b, more_a, more_b, plane_sum, line, sems
+        self, terms, out, own_a, own_b, got_a, got_b, more_a, more_b, line, sems
     ):
         rows, half, width = self.rows, self.half, self.width
         left, right = pl.ds(0, half), pl.ds(half, width - half)
         mine = pl.ds(0, width)
+        mine_left, mine_right = pl.ds(0, half), pl.ds(half, width - half)
         from_left = pl.ds(self.start, half)
         from_right = pl.ds(self.start + half, width - half)
 
@@ -582,18 +582,34 @@
 
         def upward(plane):
             me = lax.axis_index("expert")
-            return send(
-                plane_sum.at[plane], line.at[plane], sems.at[10, plane], sems.at[11, plane],
-                expert=me + 4,
+            return (
+                send(
+                    more_a.at[plane], line.at[plane, :, left],
+                    sems.at[10, plane], sems.at[11, plane], expert=me + 4,
+                ),
+                send(
+                    more_b.at[plane], line.at[plane, :, right],
+                    sems.at[12, plane], sems.at[13, plane], expert=me + 4,
+                ),
             )
 
         def downward(plane, receiver):
             me = lax.axis_index("expert")
             slot = plane + (4 - plane) * (1 - jnp.minimum(jnp.abs(plane - receiver), 1))
-            return send(
-                plane_sum.at[plane], line.at[slot], sems.at[12, plane], sems.at[13, plane],
-                expert=me - 4,
+            return (
+                send(
+                    more_a.at[plane], line.at[slot, :, left],
+                    sems.at[14, plane], sems.at[15, plane], expert=me - 4,
+                ),
+                send(
+                    more_b.at[plane], line.at[slot, :, right],
+                    sems.at[16, plane], sems.at[17, plane], expert=me - 4,
+                ),
             )
+
+        def arrived(copies):
+            for copy in copies:
+                copy.wait_recv()
 
         def begin(copies):
             for copy in copies:
@@ -624,10 +640,10 @@
                 copy.wait_recv()
 
             def add(span):
-                plane_sum[plane, span, left] = (
+                more_a[plane, span, :] = (
                     wide(own_a[slot, x, span, :]) + wide(more_a[plane, span, :])
                 ).astype(LOW)
-                plane_sum[plane, span, right] = (
+                more_b[plane, span, :] = (
                     wide(own_b[slot, y, span, :]) + wide(more_b[plane, span, :])
                 ).astype(LOW)
 
@@ -643,8 +659,11 @@
 
             def join(slot):
                 def add(span):
-                    plane_sum[plane, span, :] = (
-                        wide(plane_sum[plane, span, :]) + wide(line[slot, span, :])
+                    more_a[plane, span, :] = (
+                        wide(more_a[plane, span, :]) + wide(line[slot, span, left])
+                    ).astype(LOW)
+                    more_b[plane, span, :] = (
+                        wide(more_b[plane, span, :]) + wide(line[slot, span, right])
                     ).astype(LOW)
 
                 over_rows(add)
@@ -653,19 +672,19 @@
             def _():
                 @when(depth > 0)
                 def _():
-                    upward(plane).wait_recv()
+                    arrived(upward(plane))
                     join(plane)
 
-                upward(plane).start()
+                begin(upward(plane))
 
             @when(plane < depth)
             def _():
                 @when(depth < 3)
                 def _():
-                    downward(plane, depth).wait_recv()
+                    arrived(downward(plane, depth))
                     join(plane)
 
-                downward(plane, depth - 1).start()
+                begin(downward(plane, depth - 1))
 
         def start():
             for order in range(2):
@@ -675,13 +694,14 @@
             depth = coordinates()[2]
 
             def plain(span):
-                out[span, mine] = wide(plane_sum[depth, span, :])
+                out[span, mine_left] = wide(more_a[depth, span, :])
+                out[span, mine_right] = wide(more_b[depth, span, :])
 
             over_rows(plain)
 
             @when(depth > 0)
             def _():
-                upward(depth).wait_recv()
+                arrived(upward(depth))
 
                 def add(span):
                     out[span, mine] = out[span, mine] + wide(line[depth, span, :])
@@ -690,7 +710,7 @@
 
             @when(depth < 3)
             def _():
-                downward(depth, depth).wait_recv()
+                arrived(downward(depth, depth))
 
                 def add(span):
                     out[span, mine] = out[span, mine] + wide(line[4, span, :])
@@ -702,12 +722,14 @@
                     copy.wait_send()
 
                 @when(plane > depth)
-                def _():
-                    upward(plane).wait_send()
+                def _(plane=plane):
+                    for copy in upward(plane):
+                        copy.wait_send()
 
                 @when(plane < depth)
-                def _():
-                    downward(plane, depth - 1).wait_send()
+                def _(plane=plane):
+                    for copy in downward(plane, depth - 1):
+                        copy.wait_send()
 
         return [
             start,
@@ -1003,7 +1025,7 @@
     exchanges=(),
     works=(),
     lead=0,
-    vmem=60,
+    vmem=62,
 ):
     steps = max(1, sum(work.steps for work in works))
     any_spec = pl.BlockSpec(memory_space=pl.ANY)
@@ -1207,7 +1229,7 @@
     count = len(gates)
     share, hidden = gates[0][1]
     tile = tile_of(hidden)
-    across, height = hidden // tile, 256
+    across, height = hidden // tile, 512
     each, holds = total // groups // height, height // tokens
 
     def body(step, ins, outs, own_gate, own_up):
@@ -1226,7 +1248,7 @@
             pre_gate = more_gate if pre_gate is None else pre_gate + more_gate
             pre_up = more_up if pre_up is None else pre_up + more_up
         grad = ins[1][...].astype(jnp.float32)
-        sigma = 1.0 / (1.0 + jnp.exp(-pre_gate))
+        sigma = 0.5 + 0.5 * jnp.tanh(0.5 * pre_gate)
         silu = pre_gate * sigma
         outs[0][...] = (silu * pre_up).astype(LOW)
         outs[1][...] = (grad * pre_up * (sigma * (1.0 + pre_gate * (1.0 - sigma)))).astype(LOW)
@@ -1306,7 +1328,7 @@
     def right_spot(s):
         return lax.rem(s, deep), lax.rem(s // deep, across)
 
-    work = Work(
+    return Work(
         height // tall * across * deep,
         [(left, (depth, tall), left_spot)]
         + [(right, (depth, tile), right_spot) for right in rights],
@@ -1323,33 +1345,6 @@
         [pltpu.VMEM((tall, total), left.dtype)]
         + [pltpu.VMEM((tall, tile), jnp.float32)] * (len(rights) if deep > 1 else 0),
     )
-    work.flops = 2 * total * height * width * len(rights)
-    work.traffic = 2 * total * (height + len(rights) * width * (height // tall))
-    return work
-
-
-def alone(name, work, vmem=60):
-    count = len(work.inputs)
-
-    def kernel(*refs):
-        outs = refs[count : count + len(work.outputs)]
-        work.body(pl.program_id(0), refs[:count], outs, *refs[count + len(work.outputs) :])
-
-    return pl.pallas_call(
-        kernel,
-        name=name,
-        grid=(work.steps,),
-        in_specs=[
-            pl.BlockSpec(shape, index_of) for _, shape, index_of in work.inputs
-        ],
-        out_specs=[pl.BlockSpec(shape, index_of) for _, _, shape, index_of in work.outputs],
-        out_shape=[jax.ShapeDtypeStruct(shape, dtype) for shape, dtype, _, _ in work.outputs],
-        scratch_shapes=work.scratch,
-        compiler_params=pltpu.CompilerParams(vmem_limit_bytes=vmem * 1024 * 1024),
-        cost_estimate=pl.CostEstimate(
-            flops=work.flops, bytes_accessed=work.traffic, transcendentals=0
-        ),
-    )(*[array for array, _, _ in work.inputs])
 
 
 CHUNK = 256
@@ -1541,10 +1536,22 @@
     )(place, queries, pairs, pairs, key_labels, query_labels, grads, log_total)
 
 
-def dispatch_kernel(place, n_ref, u_ref, p_ref, m_ref, w_ref, rows_ref, up_ref, pair_ref, g_ref):
-    rows = n_ref[0]
-    pick = p_ref[0]
-    logits = dot_nt(w_ref[...], rows)
+def dispatch_kernel(
+    place, n_ref, u_ref, p_ref, m_ref, w_ref, rows_ref, up_ref, pair_ref, g_ref, pick_ref
+):
+    blocks, tokens, model = n_ref.shape
+    capacity = p_ref.shape[1]
+
+    @pl.when(pl.program_id(0) == 0)
+    def _():
+        pick_ref[...] = jnp.zeros(pick_ref.shape, LOW)
+
+    for block in range(blocks):
+        pick_ref[
+            block * capacity : (block + 1) * capacity, block * tokens : (block + 1) * tokens
+        ] = p_ref[block]
+    pick = pick_ref[...]
+    logits = dot_nt(w_ref[...], n_ref[...].reshape(blocks * tokens, model))
     chosen = m_ref[...] > 0.5
     top = jnp.max(jnp.where(chosen, logits, masked_score), axis=0, keepdims=True)
     power = jnp.where(chosen, jnp.exp(jnp.where(chosen, logits - top, 0.0)), 0.0)
@@ -1553,33 +1560,40 @@
         power, axis=0, keepdims=True
     )
     slot_gate = jnp.sum(pick.astype(jnp.float32) * gate, axis=1, keepdims=True)
-    rows_ref[...] = dot_nn(pick, rows).astype(LOW)
-    ups = dot_nn(pick, u_ref[...])
-    up_ref[...] = ups.astype(LOW)
-    pair_ref[...] = (slot_gate * ups).astype(LOW)
     g_ref[...] = slot_gate
+    tile = tile_of(model)
+    for index in range(model // tile):
+        span = pl.ds(index * tile, tile)
+        rows = n_ref[:, :, span].reshape(blocks * tokens, tile)
+        rows_ref[:, span] = dot_nn(pick, rows).astype(LOW)
+        ups = dot_nn(pick, u_ref[:, span])
+        up_ref[:, span] = ups.astype(LOW)
+        pair_ref[:, span] = (slot_gate * ups).astype(LOW)
 
 
 def dispatch(place, normed, upstream, pick, chosen, w_router):
     blocks, capacity, tokens = pick.shape
     model = upstream.shape[1]
     experts = w_router.shape[0]
-    wide = pl.BlockSpec((capacity, model), lambda b: (b, 0))
+    group = 4
+    wide_spec = pl.BlockSpec((group * capacity, model), lambda b: (b, 0))
     return pl.pallas_call(
         dispatch_kernel,
         name="dispatch",
-        grid=(blocks,),
+        grid=(blocks // group,),
         in_specs=[
             pl.BlockSpec(memory_space=pltpu.SMEM),
-            pl.BlockSpec((1, tokens, model), lambda b: (b, 0, 0)),
-            pl.BlockSpec((tokens, model), lambda b: (b, 0)),
-            pl.BlockSpec((1, capacity, tokens), lambda b: (b, 0, 0)),
-            pl.BlockSpec((experts, tokens), lambda b: (0, b)),
+            pl.BlockSpec((group, tokens, model), lambda b: (b, 0, 0)),
+            pl.BlockSpec((group * tokens, model), lambda b: (b, 0)),
+            pl.BlockSpec((group, capacity, tokens), lambda b: (b, 0, 0)),
+            pl.BlockSpec((experts, group * tokens), lambda b: (0, b)),
             pl.BlockSpec((experts, model), lambda b: (0, 0)),
         ],
-        out_specs=[wide, wide, wide, pl.BlockSpec((capacity, 1), lambda b: (b, 0))],
+        out_specs=[wide_spec] * 3 + [pl.BlockSpec((group * capacity, 1), lambda b: (b, 0))],
         out_shape=[jax.ShapeDtypeStruct((blocks * capacity, model), LOW)] * 3
         + [jax.ShapeDtypeStruct((blocks * capacity, 1), jnp.float32)],
+        scratch_shapes=[pltpu.VMEM((group * capacity, group * tokens), LOW)],
+        compiler_params=pltpu.CompilerParams(vmem_limit_bytes=50 * 1024 * 1024),
     )(place, normed, upstream, pick, chosen, w_router)
 
 
@@ -1659,7 +1673,7 @@
             pre_gate = more_gate if pre_gate is None else pre_gate + more_gate
             pre_up = more_up if pre_up is None else pre_up + more_up
         d_act = dot_nt(pair_ref[...], w_down[which][...])
-        sigma = 1.0 / (1.0 + jnp.exp(-pre_gate))
+        sigma = 0.5 + 0.5 * jnp.tanh(0.5 * pre_gate)
         silu = pre_gate * sigma
         act_ref[:, span] = (silu * pre_up).astype(LOW)
         dg_ref[:, span] = (
@@ -2032,7 +2046,9 @@
             (out_terms, half_model, half_model),
             (blocks(term_o), 0, model),
         ],
-        works=[turned_products(normed_each, [shared_d_gate, shared_d_up], LOW, length)],
+        works=[
+            turned_products(normed_each, [shared_d_gate, shared_d_up], LOW, length)
+        ],
     )
     d_pairs = d_pairs.reshape(tokens, KEY_HEADS, 2, HEAD_DIM)
     d_query_low = rotate(
@@ -2076,7 +2092,6 @@
     mine_pre, shared_act, term_eg, term_eu, term_ed, grad_sg, grad_su = lax.optimization_barrier(
         (mine_pre, shared_act, term_eg, term_eu, term_ed, grad_sg, grad_su)
     )
-
     own_act = lax.dynamic_slice_in_dim(
         shared_act.reshape(groups, length, -1), place * tokens, tokens, 1
     ).reshape(groups * tokens, -1)
@@ -2093,15 +2108,14 @@
         return total
 
     grad_eg, grad_eu, grad_ed = summed(term_eg), summed(term_eu), summed(term_ed)
-    (grad_sd,) = alone(
-        "down_grads", turned_products(shared_act, [upstream_each], jnp.float32, length)
-    )
+    grad_sd = dot_tn(shared_act, upstream_each)
     grad_sg, grad_su = [
         join_columns(here_side, groups, term, scattered(term, 0)[1:])
         for term in (grad_sg, grad_su)
     ]
-    grad_o, grad_q, grad_k, grad_v, small_grads = widen(
-        [all_o, all_pre], [[], [model, model + wide, model + 2 * wide]]
+    (grad_o,) = widen([all_o], [[]])
+    grad_q, grad_k, grad_v, small_grads = widen(
+        [all_pre], [[model, model + wide, model + 2 * wide]]
     )
     small_grads = small_grads[:, : 2 + experts].T
     return (

time: 1200 us -> 1160 us (0.967); the launches traced: 1190 us -> 1160 us
  Pallas kernels: 995 us -> 925 us
  matrix products: 66.8 us -> 108 us
    pallas_call x2 -> x1, Pallas kernels: 77.6 us -> 16.3 us  [dispatch(): pl.pallas_call(dispatch_kernel, name='dispatch', grid=(blocks // group,),...]
    dot_general x2 -> x3, matrix products: 13.6 us -> 51 us  [dot_tn(): lax.dot_general(left, right, (((0,), (0,)), ((), ())), preferred_element_...]
    pallas_call x5, Pallas kernels: 767 us -> 755 us  [carry(): pl.pallas_call(kernel, name=name, grid=(steps,), out_shape=out_shapes, in...]
  transfers between devices with their start and end apart: 18 -> 18, of which waited for: 3 -> 5; matrix products, arithmetic and copies ran while one was open for 10% -> 14% of each run, Pallas kernels for 55% -> 52%
where the time goes in v3:
time: 1160 us
  Pallas kernels  925 us (80%)
  matrix products  108 us (9%)
  local copies, waits for them, and re-layouts  48.3 us (4%)
  other arithmetic  44.4 us (4%)
  between operations  15.3 us (1%)
  waiting for transfers between devices  12.2 us (1%)
    pallas_call x5, Pallas kernels, carry(): pl.pallas_call(kernel, name=name, grid=(steps,), out_shape=out_shapes, in...  755 us
    pallas_call x1, Pallas kernels, run_expert(): pl.pallas_call(kernel, name='expert', grid_spec=pltpu.PrefetchScalarGridS...  83.5 us
    dot_general x3, matrix products, dot_tn(): lax.dot_general(left, right, (((0,), (0,)), ((), ())), preferred_element_...  51 us
    dot_general x10, matrix products, dot_nt(): lax.dot_general(left, right, (((1,), (1,)), ((), ())), preferred_element_...  28.2 us
    pallas_call x1, Pallas kernels, attend_back(): pl.pallas_call(attend_back_kernel, name='attend_back', grid=(KEY_HEADS,),...  27.2 us
    dot_general x9, matrix products, dot_nn(): return jnp.dot(left, right, preferred_element_type=jnp.float32)  26 us
  transfers between devices with their start and end apart: 18, of which 5 were waited for; matrix products, arithmetic and copies ran while one was open for 14% of the time, Pallas kernels for 52%

profile of v3, /device:TPU:0, one launch (start us, length us, event | category | flops | bytes accessed | tf_op | source)
XLA Modules:
  0.0 1157.6 jit_solution(3575273051850056401)
XLA Ops:
  35.0 167.7 %attend.1 = (bf16[1,16,128,1152]{3,2,1,0:T(8,128)(2,1)}, bf16[2,16,128,2560]{3,2,1,0:T(8,128)(2,1)}, bf16[1,1280,1536]{2,1,0:T(8,128)(2,1)}, bf16[1,1280,1536]{2...) custom-call(bf16[128,1152]{1,0:T(8,128)(2,1)} %pad_maximum_fusion.6., ...), custom_call_target="tpu_custom_call" | custom-call | tf_op jit(solution)/shard_map/attend/pallas_call | solution.py:1167
  218.7 113.7 %rows.1 = (bf16[2,16,128,2560]{3,2,1,0:T(8,128)(2,1)}, bf16[4096,1536]{1,0:T(8,128)(2,1)}) custom-call(bf16[128,2560]{1,0:T(8,128)(2,1)} %copy-done.14, bf16[4096,2560]{1,0:T(8,128)(2,1)} %bitcast.116, bf16[1536,2560]{1,0:T(8,128)(2,1)} %refs_2_.3), custom_call_target="tpu_custom_call" | custom-call | tf_op jit(solution)/shard_map/rows/pallas_call | solution.py:1167
  332.4 16.3 %dispatch.1 = (bf16[1024,2560]{1,0:T(8,128)(2,1)}, bf16[1024,2560]{1,0:T(8,128)(2,1)}, bf16[1024,2560]{1,0:T(8,128)(2,1)}, f32[1024,1]{1,0:T(8,128)S(1)}) custom-call(s32[1]{0:T(128)} %bitcast.11.place, bf16[32,128,2560]{2,1,0:T(8,128)(2,1)} %bitcast.113, bf16[4096,2560]{1,0:T(8,128)(2,1)} %bitcast.117, bf16[16,64,128]{2,1,0:T(8,128)(2,1)S(1)} %fusion.41.p_ref, ...), custom_call_target="tpu_custom_call" | custom-call | tf_op jit(solution)/shard_map/dispatch/pallas_call | solution.py:1580
  349.4 83.5 %expert.1 = (bf16[1024,1536]{1,0:T(8,128)(2,1)}, bf16[1024,1536]{1,0:T(8,128)(2,1)}, bf16[1024,1536]{1,0:T(8,128)(2,1)}, f32[1024,1]{1,0:T(8,128)}, bf16[16,128,...) custom-call(s32[1]{0:T(128)} %bitcast.13.refs_0_.side_ref, bf16[1024,2560]{1,0:T(8,128)(2,1)} %get-tuple-element.70.refs_1_.refs_3_, ...), custom_call_target="tpu_custom_call" | custom-call | tf_op jit(solution)/shard_map/expert/pallas_call | solution.py:1731
  435.1 166.7 %row_grads.1 = (f32[128,2560]{1,0:T(8,128)}, f32[128,1280]{1,0:T(8,128)}, f32[16,8,128]{2,1,0:T(8,128)}, bf16[4096,1536]{1,0:T(8,128)(2,1)}, bf16[4096,1536]{1,0...) custom-call(bf16[4,2,2,128,2560]{4,3,2,1,0:T(8,128)(2,1)} %bitcast.141, ...), custom_call_target="tpu_custom_call" | custom-call | tf_op jit(solution)/shard_map/row_grads/pallas_call | solution.py:1167
  610.0 5.0 fusion.79
  615.0 5.1 select_convert_fusion.1
  621.3 27.2 %attend_back.1 = (f32[128,2560]{1,0:T(8,128)S(1)}, bf16[2048,1024]{1,0:T(8,128)(2,1)}) custom-call(s32[1]{0:T(128)} %bitcast.11.place, bf16[128,2560]{1,0:T(8,128)(2,1)S(1)} %copy-done.1, bf16[2048,1152]{1,0:T(8,128)(2,1)} %bitcast.125, bf16[2048,1152]{1,0:T(8,128)(2,1)} %bitcast.126, s32[2048,1]{1,0:T(8,128)S(1)} %copy-done, s32[1,128]{1,0:T(1,128)S(1)} %copy-done.4, ...), custom_call_target="tpu_custom_call" | custom-call | tf_op jit(solution)/shard_map/attend_back/pallas_call | solution.py:1517
  651.5 6.3 fusion.80
  657.8 5.9 convolution_convert_fusion.1
  663.7 169.4 %pair_grads.1 = (f32[128,1024]{1,0:T(8,128)}, f32[128,1280]{1,0:T(8,128)}, f32[80,2560]{1,0:T(8,128)}, bf16[2560,1536]{1,0:T(8,128)(2,1)}, bf16[2560,1536]{1,0:T(8,128)(2,1)}) custom-call(bf16[4,2,2,128,1024]{4,3,2,1,0:T(8,128)(2,1)} %bitcast.151, bf16[4,2,2,128,2560]{4,3,2,1,0:T(8,128)(2,1)} %bitcast.122, bf16[4,2,2,80,2560]{4,3,2,1,0:T(8,128)(2,1)} %bitcast.123, ...), custom_call_target="tpu_custom_call" | custom-call | tf_op jit(solution)/shard_map/pair_grads/pallas_call | solution.py:1167
  844.7 5.2 broadcast_select_fusion.1
  855.6 7.7 convolution_convert_fusion
  863.2 137.7 %sums.1 = (bf16[1,16,80,2560]{3,2,1,0:T(8,128)(2,1)}, f32[80,3584]{1,0:T(8,128)}, f32[80,256]{1,0:T(8,128)}, bf16[2560,1536]{1,0:T(8,128)(2,1)}, bf16[2560,1536]{1,0:T(8,128)(2,1)}, /*index=5*/bf16[1536,2560]{1,0:T(8,128)(2,1)}) custom-call(bf16[80,2560]{1,0:T(8,128)(2,1)} %convert_element_type.157.refs_0_, bf16[4,2,2,80,3584]{4,3,2,1,0:T(8,128)(2,1)} %bitcast.142, ...), custom_call_target="tpu_custom_call" | custom-call | tf_op jit(solution)/shard_map/sums/pallas_call | solution.py:1167
  1020.7 6.2 convolution_convert_fusion.2
  1032.5 37.5 %fusion.83 = f32[1536,2560]{1,0:T(8,128)} fusion(bf16[4096,1536]{1,0:T(8,128)(2,1)} %get-tuple-element.104, bf16[4096,2560]{1,0:T(8,128)(2,1)S(1)} %bitcast.120), kind=kOutput, calls=%fused_computation.177 | convolution fusion | flops 32212254720 | bytes 49283072 | tf_op jit(solution)/shard_map/dot_general | solution.py:31
  1070.0 10.2 widen.3
  1084.5 10.5 join_columns.3
  1095.1 10.7 join_columns.2
  1105.8 7.8 add_bitcast_fusion
  1113.6 8.1 add_bitcast_fusion.1
  1121.7 6.5 add_bitcast_fusion.2
  1128.2 7.1 all-gather.2.cloned.1.call-done.refs_0_
  1135.3 11.9 %widen.2 = (f32[1280,2560]{1,0:T(8,128)}, f32[1280,512]{1,0:T(8,128)}, f32[1280,512]{1,0:T(8,128)}, f32[1280,256]{1,0:T(8,128)}) custom-call(bf16[1280,3840]{1,0:T(8,128)(2,1)} %all-gather.2.cloned.1.call-done.refs_0_), custom_call_target="tpu_custom_call" | custom-call | tf_op jit(solution)/shard_map/widen/pallas_call | solution.py:1641
  (269 shorter events, 108.6 us)
Async XLA Ops:
  7.2 11.8 %copy-start.37 = (bf16[1280,16]{0,1:T(8,128)(2,1)S(1)}, bf16[1280,16]{0,1:T(8,128)(2,1)}, u32[]{:S(2)}) copy-start(bf16[1280,16]{0,1:T(8,128)(2,1)} %param.25) | copy-start | bytes 122884
  7.2 1128.1 %all-gather.2.cloned.1.call-start = ((), (), s32[]{:S(2)}) async-start(), calls=%async_computation | async-start | bytes 10444800 | tf_op jit(solution)/shard_map/all_gather | solution.py:2090
  7.2 22.1 %collective-permute-start.3 = (bf16[1280,2560]{1,0:T(8,128)(2,1)}, bf16[1280,2560]{1,0:T(8,128)(2,1)}, u32[]{:S(2)}, u32[]{:S(2)}) collective-permute-start(bf16[1280,2560]{1,0:T(8,128)(2,1)} %param.20), channel_id=1, source_target_pairs={{1,0},{0,1},{3,2},{2,3},{5,4},{4,5},{7,6},{6,7},{9,8},{8,9},{11,10... | collective-permute-start | bytes 19660808 | tf_op jit(solution)/shard_map/ppermute | solution.py:1793
  10.0 9.1 collective-permute-start
  10.1 14.5 %collective-permute-start.1 = (bf16[1280,512]{1,0:T(8,128)(2,1)}, bf16[1280,512]{1,0:T(8,128)(2,1)}, u32[]{:S(2)}, u32[]{:S(2)}) collective-permute-start(bf16[1280,512]{1,0:T(8,128)(2,1)} %param.21), channel_id=1, source_target_pairs={{1,0},{0,1},{3,2},{2,3},{5,4},{4,5},{7,6},{6,7},{9,8},{8,9},{11,10... | collective-permute-start | bytes 3932168 | tf_op jit(solution)/shard_map/ppermute | solution.py:1793
  10.5 16.3 %collective-permute-start.2 = (bf16[1280,512]{1,0:T(8,128)(2,1)}, bf16[1280,512]{1,0:T(8,128)(2,1)}, u32[]{:S(2)}, u32[]{:S(2)}) collective-permute-start(bf16[1280,512]{1,0:T(8,128)(2,1)} %param.22), channel_id=1, source_target_pairs={{1,0},{0,1},{3,2},{2,3},{5,4},{4,5},{7,6},{6,7},{9,8},{8,9},{11,10... | collective-permute-start | bytes 3932168 | tf_op jit(solution)/shard_map/ppermute | solution.py:1793
  10.6 202.0 %collective-permute-start.4 = (bf16[1280,2560]{1,0:T(8,128)(2,1)}, bf16[1280,2560]{1,0:T(8,128)(2,1)}, u32[]{:S(2)}, u32[]{:S(2)}) collective-permute-start(bf16[1280,2560]{1,0:T(8,128)(2,1)} %param.23), channel_id=1, source_target_pairs={{1,0},{0,1},{3,2},{2,3},{5,4},{4,5},{7,6},{6,7},{9,8},{8,9},{11,10... | collective-permute-start | bytes 19660808 | tf_op jit(solution)/shard_map/ppermute | solution.py:1793
  204.7 453.1 %collective-permute-start.6 = (bf16[128,1280]{1,0:T(8,128)(2,1)}, bf16[128,1280]{1,0:T(8,128)(2,1)}, u32[]{:S(2)}, u32[]{:S(2)}) collective-permute-start(bf16[128,1280]{1,0:T(8,128)(2,1)} %get-tuple-element.183), channel_id=1, source_target_pairs={{1,0},{0,1},{3,2},{2,3},{5,4},{4,5},{7,6},{6,7},{9,8},{8,9},{11,10... | collective-permute-start | bytes 983048 | tf_op jit(solution)/shard_map/ppermute | solution.py:1793
  604.0 2.2 collective-permute-start.5
  609.8 48.0 %collective-permute-start.7 = (bf16[128,2560]{1,0:T(8,128)(2,1)S(1)}, bf16[128,2560]{1,0:T(8,128)(2,1)}, u32[]{:S(2)}, u32[]{:S(2)}) collective-permute-start(bf16[128,2560]{1,0:T(8,128)(2,1)S(1)} %fusion.77), channel_id=1, source_target_pairs={{1,0},{0,1},{3,2},{2,3},{5,4},{4,5},{7,6},{6,7},{9,8},{8,9},{11,10... | collective-permute-start | bytes 1966088 | tf_op jit(solution)/shard_map/ppermute | solution.py:1793
  851.1 2.4 collective-permute-start.10
  852.1 3.4 collective-permute-start.9
  852.6 2.6 collective-permute-start.8
  1007.7 98.0 %collective-permute-start.16 = (bf16[768,2560]{1,0:T(8,128)(2,1)}, bf16[768,2560]{1,0:T(8,128)(2,1)}, u32[]{:S(2)}, u32[]{:S(2)}) collective-permute-start(bf16[768,2560]{1,0:T(8,128)(2,1)} %constant_dynamic-slice_fusion), channel_id=1, source_target_pairs={{1,0},{0,1},{3,2},{2,3},{5,4},{4,5},{7,6},{6,7},{9,8},{8,9},{11,10... | collective-permute-start | bytes 11796488 | tf_op jit(solution)/shard_map/ppermute | solution.py:1793
  1012.2 101.4 %collective-permute-start.15 = (bf16[1280,1536]{1,0:T(8,128)(2,1)}, bf16[1280,1536]{1,0:T(8,128)(2,1)}, u32[]{:S(2)}, u32[]{:S(2)}) collective-permute-start(bf16[1280,1536]{1,0:T(8,128)(2,1)} %constant_dynamic-slice_fusion.1), channel_id=1, source_target_pairs={{1,0},{0,1},{3,2},{2,3},{5,4},{4,5},{7,6},{6,7},{9,8},{8,9},{11,10... | collective-permute-start | bytes 11796488 | tf_op jit(solution)/shard_map/ppermute | solution.py:1793
  1014.9 106.8 %collective-permute-start.14 = (bf16[1280,1536]{1,0:T(8,128)(2,1)}, bf16[1280,1536]{1,0:T(8,128)(2,1)}, u32[]{:S(2)}, u32[]{:S(2)}) collective-permute-start(bf16[1280,1536]{1,0:T(8,128)(2,1)} %constant_dynamic-slice_fusion.2), channel_id=1, source_target_pairs={{1,0},{0,1},{3,2},{2,3},{5,4},{4,5},{7,6},{6,7},{9,8},{8,9},{11,10... | collective-permute-start | bytes 11796488 | tf_op jit(solution)/shard_map/ppermute | solution.py:1793
  1016.3 16.2 %slice-start = ((s8[20971520]{0:T(1024)(128)(4,1)}), s8[4194304]{0:T(1024)(128)(4,1)S(1)}, s32[]{:S(2)}) async-start(s8[20971520]{0:T(1024)(128)(4,1)} %bitcast.118), calls=%async_computation.1 | async-start | bytes 8388608
  1018.6 66.0 %collective-permute-start.13 = (bf16[1280,1536]{1,0:T(8,128)(2,1)}, bf16[1280,1536]{1,0:T(8,128)(2,1)}, u32[]{:S(2)}, u32[]{:S(2)}) collective-permute-start(bf16[1280,1536]{1,0:T(8,128)(2,1)} %constant_dynamic-slice_fusion.3), channel_id=1, source_target_pairs={{1,0},{0,1},{3,2},{2,3},{5,4},{4,5},{7,6},{6,7},{9,8},{8,9},{11,10... | collective-permute-start | bytes 11796488 | tf_op jit(solution)/shard_map/ppermute | solution.py:1793
  1018.6 13.9 %slice-start.1 = ((s8[20971520]{0:T(1024)(128)(4,1)}), s8[4194304]{0:T(1024)(128)(4,1)S(1)}, s32[]{:S(2)}) async-start(s8[20971520]{0:T(1024)(128)(4,1)} %bitcast.118), calls=%async_computation.2 | async-start | bytes 8388608
  1020.7 11.8 %slice-start.2 = ((s8[20971520]{0:T(1024)(128)(4,1)}), s8[4194304]{0:T(1024)(128)(4,1)S(1)}, s32[]{:S(2)}) async-start(s8[20971520]{0:T(1024)(128)(4,1)} %bitcast.118), calls=%async_computation.3 | async-start | bytes 8388608
  1027.0 5.3 collective-permute-start.11
  1032.3 37.7 %copy-start.33 = (bf16[128,2560]{1,0:T(8,128)(2,1)}, bf16[128,2560]{1,0:T(8,128)(2,1)S(1)}, u32[]{:S(2)}) copy-start(bf16[128,2560]{1,0:T(8,128)(2,1)S(1)} %collective-permute-done.11) | copy-start | bytes 1966084
  1032.3 62.8 %collective-permute-start.12 = (bf16[1280,1536]{1,0:T(8,128)(2,1)}, bf16[1280,1536]{1,0:T(8,128)(2,1)}, u32[]{:S(2)}, u32[]{:S(2)}) collective-permute-start(bf16[1280,1536]{1,0:T(8,128)(2,1)} %constant_dynamic-slice_fusion.4), channel_id=1, source_target_pairs={{1,0},{0,1},{3,2},{2,3},{5,4},{4,5},{7,6},{6,7},{9,8},{8,9},{11,10... | collective-permute-start | bytes 11796488 | tf_op jit(solution)/shard_map/ppermute | solution.py:1793
  1105.8 16.0 %slice-start.11 = ((s8[7864320]{0:T(1024)(128)(4,1)}), s8[4194304]{0:T(1024)(128)(4,1)S(1)}, s32[]{:S(2)}) async-start(s8[7864320]{0:T(1024)(128)(4,1)} %bitcast.145), calls=%async_computation.12 | async-start | bytes 8388608
  (56 other events, 219.9 us)
Sparse Core Ops, SparseCore 0:
  1003.4 131.8 all-gather.1
